TPU v7x, 32 devices: a whole 2x2x4 slice. The times are simulated.
32 devices in a mesh: seq: 4 (over x, core), blk: 8 (over z, y).
Axes of the slice: x: 2, y: 2, z: 4, core: 2. Of those that a mesh axis runs over, the one named last changes fastest.
Arguments:
- residual_in: bfloat16 [8, 512, 2048], P('blk', 'seq'), may hold values from -6 to 6
- segment_ids: int32 [8, 512], P('blk'), may hold values from 0 to 2, never falling along the last dimension, each value on 1 to 256 neighbouring positions
- attn_gain: bfloat16 [2048], replicated, may hold values from 0.5 to 1.5
- w_qkv: bfloat16 [2048, 16, 384], P(None, 'seq')
- w_out: bfloat16 [16, 128, 2048], P('seq'), may hold values from -0.125 to 0.125
- ffn_gain: bfloat16 [2048], replicated, may hold values from 0.5 to 1.5
- w_router: bfloat16 [2048, 8], replicated, may hold values from -0.125 to 0.125
- routes: int32 [8, 512, 2], P('blk', 'seq'), may hold values from 0 to 7, all different within a row; in each aligned block of 128 rows (0 to 127, 128 to 255, ..., all dimensions but the last counted through in order) at most 48 rows name the same one
- w_gate_up: bfloat16 [8, 2048, 2048], P('blk'), may hold values from -0.125 to 0.125
- w_down: bfloat16 [8, 1024, 2048], P('blk'), may hold values from -0.1875 to 0.1875
- page_owner: int32 [8, 8], P('blk'), may hold values from 0 to 7, each once within a row
Outputs:
- residual_out: bfloat16 [8, 512, 2048], P('blk', 'seq')
- kv_cache: bfloat16 [8, 8, 64, 4096], P('blk', None, None, 'seq')
Inputs may be any that keep to these rules, and one draw needn't show every extreme that they name: `segment_ids`: within a pack the numbers never fall; 1 to 3 prompts a pack, the longest exactly 256 tokens. `routes`: each token names 2 different experts; among the 128 tokens of one device no expert is named more than 48 times, a bound that some block reaches. `page_owner`: each row is a permutation.
All inputs are finite; a program needn't handle non-finite values.
Results may differ from a plain program's by a relative error of at most 0.025.
Values may be sent and summed in bfloat16 or wider, within the bound.
No kernel may reach another device: no remote copies, remote signals or barrier semaphores. Data moves between devices by JAX's collectives and lax.ppermute only.
A program may use at most 128 MiB of HBM per device.

v0:
```python
import math

import jax
import jax.numpy as jnp
from jax import lax
from jax.sharding import PartitionSpec as P

EPS = 1e-06


def rms_norm(value, gain):
    wide = value.astype(jnp.float32)
    scale = lax.rsqrt(jnp.mean(wide * wide, axis=-1, keepdims=True) + EPS)
    return (wide * scale * gain.astype(jnp.float32)).astype(jnp.bfloat16)


def on_device(
    residual_in,
    segment_ids,
    attn_gain,
    w_qkv,
    w_out,
    ffn_gain,
    w_router,
    routes,
    w_gate_up,
    w_down,
    page_owner,
):
    local_rows = residual_in[0]
    tok_dev = local_rows.shape[0]
    heads_here = w_qkv.shape[1]
    head_dim = w_out.shape[1]
    blk_count = lax.axis_size("blk")
    normed = rms_norm(local_rows, attn_gain)
    w_flat = w_qkv.reshape(w_qkv.shape[0], heads_here * 3 * head_dim)
    qkv = jnp.dot(
        lax.all_gather(normed, "seq", axis=0, tiled=True),
        w_flat,
        preferred_element_type=jnp.float32,
    ).astype(jnp.bfloat16)
    group_len = qkv.shape[0]
    qkv = qkv.reshape(group_len, heads_here, 3 * head_dim)
    query = qkv[:, :, :head_dim]
    key_rows = qkv[:, :, head_dim : 2 * head_dim]
    value_rows = qkv[:, :, 2 * head_dim :]
    scores = jnp.einsum(
        "qhd,khd->hqk", query, key_rows, preferred_element_type=jnp.float32
    ) / math.sqrt(head_dim)
    segment_row = segment_ids[0]
    same = segment_row[:, None] == segment_row[None, :]
    scores = jnp.where(same[None], scores, jnp.float32(-1e30))
    top = jnp.max(scores, axis=-1, keepdims=True)
    weights = jnp.exp(scores - top)
    probs = (weights / jnp.sum(weights, axis=-1, keepdims=True)).astype(jnp.bfloat16)
    context = jnp.einsum(
        "hqk,khd->qhd", probs, value_rows, preferred_element_type=jnp.float32
    ).astype(jnp.bfloat16)
    context_flat = context.reshape(group_len, heads_here * head_dim)
    w_out_flat = w_out.reshape(heads_here * head_dim, w_out.shape[2])
    mixed = lax.psum_scatter(
        jnp.dot(context_flat, w_out_flat, preferred_element_type=jnp.float32).astype(jnp.bfloat16),
        "seq",
        scatter_dimension=0,
        tiled=True,
    ).astype(jnp.float32)
    resid = (local_rows.astype(jnp.float32) + mixed).astype(jnp.bfloat16)
    kv_rows = qkv[:, :, head_dim:].reshape(group_len, heads_here * 2 * head_dim)
    page_len = group_len // blk_count
    pages = kv_rows.reshape(blk_count, page_len, kv_rows.shape[1])
    owners = page_owner[0]
    places = jnp.arange(blk_count, dtype=jnp.int32)
    match = owners[None, :] == places[:, None]
    source_page = jnp.sum(jnp.where(match, places[None, :], 0), axis=1)
    outgoing = jnp.take(pages, source_page, axis=0)
    arrived = lax.all_to_all(outgoing, "blk", split_axis=0, concat_axis=0, tiled=True)
    kv_cache = arrived[None]
    ffn_in = rms_norm(resid, ffn_gain)
    logits = jnp.dot(ffn_in, w_router, preferred_element_type=jnp.float32)
    gates = jax.nn.sigmoid(logits).astype(jnp.bfloat16)
    expert_count = w_router.shape[1]
    route_rows = routes[0]
    expert_ids = jnp.arange(expert_count, dtype=jnp.int32)
    chosen = jnp.any(route_rows[:, :, None] == expert_ids[None, None, :], axis=1)
    dense_gate = jnp.where(chosen, gates, jnp.zeros_like(gates))
    capacity = tok_dev * 3 // 8
    slots = jnp.arange(capacity, dtype=jnp.int32)
    row_ids = jnp.arange(tok_dev, dtype=jnp.int32)
    gate_up = w_gate_up[0]
    down = w_down[0]
    ff_width = down.shape[0]
    all_rows, all_gates = (
        lax.all_gather(ffn_in, "blk", axis=0, tiled=True),
        lax.all_gather(dense_gate, "blk", axis=0, tiled=True),
    )
    own_expert = lax.axis_index("blk") * w_gate_up.shape[0]
    gate_col = lax.dynamic_slice_in_dim(all_gates, own_expert, 1, 1)[:, 0]
    blocks = tok_dev * lax.axis_size("blk") // tok_dev
    active = (gate_col > 0).reshape(blocks, tok_dev)
    rank = jnp.cumsum(active.astype(jnp.int32), axis=1) - 1
    hit = active[:, None, :] & (rank[:, None, :] == slots[None, :, None])
    slot_row = jnp.sum(jnp.where(hit, row_ids[None, None, :], 0), axis=2)
    block_ids = jnp.arange(blocks, dtype=jnp.int32)
    picked_index = (block_ids[:, None] * tok_dev + slot_row).reshape(-1)
    expert_rows = jnp.take(all_rows, picked_index, axis=0)
    both = jnp.dot(expert_rows, gate_up, preferred_element_type=jnp.float32)
    hidden = (jax.nn.silu(both[:, :ff_width]) * both[:, ff_width:]).astype(jnp.bfloat16)
    output = jnp.dot(hidden, down, preferred_element_type=jnp.float32)
    weighted = (jnp.take(gate_col, picked_index).astype(jnp.float32)[:, None] * output).astype(
        jnp.bfloat16
    )
    back_index = (block_ids[:, None] * capacity + jnp.clip(rank, 0, capacity - 1)).reshape(-1)
    per_row = jnp.take(weighted, back_index, axis=0)
    combined = lax.psum_scatter(
        jnp.where(
            active.reshape(-1)[:, None], per_row.astype(jnp.float32), jnp.float32(0.0)
        ).astype(jnp.bfloat16),
        "blk",
        scatter_dimension=0,
        tiled=True,
    ).astype(jnp.float32)
    residual_out = (resid.astype(jnp.float32) + combined).astype(jnp.bfloat16)[None]
    return (residual_out, kv_cache)


def solution(mesh):
    in_specs = (
        P("blk", "seq", None),
        P("blk", None),
        P(),
        P(None, "seq", None),
        P("seq", None, None),
        P(),
        P(),
        P("blk", "seq", None),
        P("blk", None, None),
        P("blk", None, None),
        P("blk", None),
    )
    out_specs = (P("blk", "seq", None), P("blk", None, None, "seq"))
    return jax.shard_map(
        on_device, mesh=mesh, in_specs=in_specs, out_specs=out_specs, check_vma=False
    )
```

profile of v0, /device:TPU:0, one launch (start us, length us, event | category | flops | bytes accessed | tf_op | source)
XLA Modules:
  0.0 314.8 jit_solution(3379441126681018942)
XLA Ops:
  9.3 2.0 fusion.28
  11.4 6.6 %copy.29 = bf16[256,8,4,384]{3,1,2,0:T(8,128)(2,1)} copy(bf16[256,8,4,384]{3,2,1,0:T(4,128)(2,1)} %bitcast.50) | data formatting | bytes 12582912
  18.2 18.5 %all-gather.3.cloned.1.call-done = bf16[512,2048]{1,0:T(8,128)(2,1)} async-done(((bf16[128,2048]{1,0:T(8,128)(2,1)}), bf16[512,2048]{1,0:T(8,128)(2,1)}) %all-gather.3.cloned.1.call-update) | async-done | bytes 2097168 | tf_op jit(solution)/shard_map/all_gather | solution.py:38
  36.8 8.1 %convolution_convert_fusion = bf16[512,1536]{1,0:T(8,128)(2,1)} fusion(bf16[512,2048]{1,0:T(8,128)(2,1)} %all-gather.3.cloned.1.call-done, bf16[2048,1536]{1,0:T(8,128)(2,1)} %bitcast.51), kind=kOutput, calls=%fused_computation.16 | convolution fusion | flops 3222011904 | bytes 9961472 | tf_op jit(solution)/shard_map/dot_general | solution.py:37
  44.9 3.9 %reshape.213 = bf16[512,4,384]{2,1,0:T(4,128)(2,1)} reshape(bf16[512,1536]{1,0:T(8,128)(2,1)} %convolution_convert_fusion) | data formatting | bytes 3145728 | tf_op jit(solution)/shard_map/reshape | solution.py:43
  48.8 1.9 fusion.47
  51.4 3.9 %fusion.48 = (f32[4,512]{1,0:T(4,128)S(1)}, f32[4,512,512]{1,2,0:T(8,128)}) fusion(f32[4,512,512]{1,2,0:T(8,128)S(1)} %fusion.34, pred[512,512]{0,1:T(8,128)(4,1)S(1)} %broadcast_compare_fusion), kind=kOutput, calls=%fused_computation.93 | output fusion | flops 6291967 | bytes 8658944 | tf_op jit(solution)/shard_map/sub | solution.py:54
  55.3 5.3 %bitcast_convert_fusion = bf16[512,2048]{1,0:T(8,128)(2,1)} fusion(bf16[4,128,2048]{2,1,0:T(8,128)(2,1)S(1)} %copy-done, f32[4,512,512]{1,2,0:T(8,128)} %get-tuple-element.10, f32[4,512]{1,0:T(4,128)S(1)} %get-tuple-element.9, bf16[512,4,128]{2,1,0:T(4,128)(2,1)S(1)} %get-tuple-element.6), kind=kOutput, calls=%fused_computation.10 | convolution fusion | flops 1345585152 | bytes 8921088 | tf_op jit(solution)/shard_map/dot_general | solution.py:62
  60.7 31.5 %reduce-scatter.3.cloned.1.call-done = bf16[128,2048]{1,0:T(8,128)(2,1)} async-done(((bf16[512,2048]{1,0:T(8,128)(2,1)}), bf16[128,2048]{1,0:T(8,128)(2,1)}) %reduce-scatter.3.cloned.1.call-update) | async-done | bytes 524304 | tf_op jit(solution)/shard_map/reduce_scatter | solution.py:61
  93.5 2.0 fusion.24
  97.0 26.6 %all_gather.10 = bf16[1024,8]{0,1:T(8,128)(2,1)S(1)} all-gather(bf16[128,8]{0,1:T(8,128)(2,1)S(1)} %fusion.21), channel_id=1, replica_groups=mesh['seq'=4,'blk'=8] {'blk'}, dimensions={0}, use_global_device_ids=true | all-gather | bytes 18432 | tf_op jit(solution)/shard_map/all_gather | solution.py:94
  124.4 2.8 gather_fusion
  127.4 42.0 %all-gather.5.cloned.1.call-done = bf16[1024,2048]{1,0:T(8,128)(2,1)} async-done(((bf16[128,2048]{1,0:T(8,128)(2,1)}), bf16[1024,2048]{1,0:T(8,128)(2,1)}) %all-gather.5.cloned.1.call-update) | async-done | bytes 4194320 | tf_op jit(solution)/shard_map/all_gather | solution.py:93
  169.4 7.1 %gather_fusion.1 = bf16[384,2048]{1,0:T(8,128)(2,1)S(1)} fusion(bf16[1024,2048]{1,0:T(8,128)(2,1)} %all-gather.5.cloned.1.call-done, s32[1024]{0:T(1024)S(1)} %pad_clamp_fusion.1), kind=kCustom, calls=%fused_computation.1 | custom fusion | bytes 3147264 | tf_op jit(solution)/shard_map/jit(_take)/gather | solution.py:105
  176.5 6.1 %fusion.1 = f32[384,2048]{1,0:T(8,128)S(1)} fusion(bf16[1,2048,2048]{2,1,0:T(8,128)(2,1)} %param.19, bf16[384,2048]{1,0:T(8,128)(2,1)S(1)} %gather_fusion.1, pred[384]{0:T(512)(128)(4,1)S(1)} %get-tuple-element.5), kind=kOutput, calls=%fused_computation.5 | convolution fusion | flops 3222011904 | bytes 13107584 | tf_op jit(solution)/shard_map/dot_general | solution.py:106
  182.6 1.8 multiply_convert_fusion
  184.4 6.0 %gather_fusion.2 = bf16[1024,2048]{1,0:T(8,128)(2,1)} fusion(bf16[384,2048]{1,0:T(8,128)(2,1)S(1)} %multiply_convert_fusion, s32[1024]{0:T(1024)S(1)} %broadcast_clamp_fusion), kind=kCustom, calls=%fused_computation.2 | custom fusion | bytes 8392704 | tf_op jit(solution)/shard_map/jit(_take)/gather | solution.py:113
  190.5 4.4 %select_convert_fusion = bf16[1024,2048]{1,0:T(8,128)(2,1)} fusion(bf16[1024,2048]{1,0:T(8,128)(2,1)} %gather_fusion.2, pred[1024]{0:T(1024)(128)(4,1)S(1)} %get-tuple-element.2, pred[1024]{0:T(1024)(128)(4,1)S(1)} %compare_reduce_fusion), kind=kLoop, calls=%fused_computation.7 | loop fusion | flops 8388608 | bytes 8390656 | tf_op jit(solution)/shard_map/convert_element_type | solution.py:117
  196.1 1.5 reshape_reshape.3
  197.6 3.0 gather_fusion.3
  202.0 53.9 %all_to_all.5 = bf16[8,64,1024]{2,1,0:T(8,128)(2,1)} all-to-all(bf16[8,64,1024]{2,1,0:T(8,128)(2,1)S(1)} %broadcast_select_fusion), channel_id=1, replica_groups=mesh['seq'=4,'blk'=8] {'blk'}, dimensions={0} | all-to-all | bytes 2097152 | tf_op jit(solution)/shard_map/all_to_all | solution.py:76
  255.9 48.0 %reduce-scatter.5.cloned.1.call-done = bf16[128,2048]{1,0:T(8,128)(2,1)} async-done(((bf16[1024,2048]{1,0:T(8,128)(2,1)}), bf16[128,2048]{1,0:T(8,128)(2,1)}) %reduce-scatter.5.cloned.1.call-update) | async-done | bytes 524304 | tf_op jit(solution)/shard_map/reduce_scatter | solution.py:114
  303.9 2.1 fusion.33
  306.0 2.3 copy.38
  (62 shorter events, 9.4 us)
Async XLA Ops:
  7.2 48.2 %copy-start = (bf16[4,128,2048]{2,1,0:T(8,128)(2,1)S(1)}, bf16[4,128,2048]{2,1,0:T(8,128)(2,1)}, u32[]{:S(2)}) copy-start(bf16[4,128,2048]{2,1,0:T(8,128)(2,1)} %param.15) | copy-start | bytes 6291460
  7.2 29.6 %all-gather.3.cloned.1.call-start = ((), (), s32[]{:S(2)}) async-start(), calls=%async_computation.3 | async-start | bytes 2621440 | tf_op jit(solution)/shard_map/all_gather | solution.py:38
  11.3 80.9 %reduce-scatter.3.cloned.1.call-start = ((), (), s32[]{:S(2)}) async-start(), calls=%async_computation.4 | async-start | bytes 2621440 | tf_op jit(solution)/shard_map/reduce_scatter | solution.py:61
  11.4 6.6 %copy-start.5 = (s32[1,512]{1,0:T(1,128)S(1)}, s32[1,512]{1,0:T(1,128)}, u32[]{:S(2)}) copy-start(s32[1,512]{1,0:T(1,128)} %param.12) | copy-start | bytes 6148
  55.3 5.3 %copy-start.6 = (bf16[2048]{0:T(1024)(128)(2,1)S(1)}, bf16[2048]{0:T(1024)(128)(2,1)}, u32[]{:S(2)}) copy-start(bf16[2048]{0:T(1024)(128)(2,1)} %param.16) | copy-start | bytes 12292
  55.3 36.9 %copy-start.2 = (bf16[1,128,2048]{2,1,0:T(8,128)(2,1)S(1)}, bf16[1,128,2048]{2,1,0:T(8,128)(2,1)}, u32[]{:S(2)}) copy-start(bf16[1,128,2048]{2,1,0:T(8,128)(2,1)} %param.11) | copy-start | bytes 1572868
  60.6 35.1 %copy-start.7 = (s32[1,128,2]{1,2,0:T(2,128)S(1)}, s32[1,128,2]{1,2,0:T(2,128)}, u32[]{:S(2)}) copy-start(s32[1,128,2]{1,2,0:T(2,128)} %param.18) | copy-start | bytes 3076
  60.6 35.1 %copy-start.4 = (bf16[2048,8]{0,1:T(8,128)(2,1)S(1)}, bf16[2048,8]{0,1:T(8,128)(2,1)}, u32[]{:S(2)}) copy-start(bf16[2048,8]{0,1:T(8,128)(2,1)} %param.17) | copy-start | bytes 98308
  60.6 108.7 %all-gather.5.cloned.1.call-start = ((), (), s32[]{:S(2)}) async-start(), calls=%async_computation.5 | async-start | bytes 4718592 | tf_op jit(solution)/shard_map/all_gather | solution.py:93
  95.6 208.3 %reduce-scatter.5.cloned.1.call-start = ((), (), s32[]{:S(2)}) async-start(), calls=%async_computation.6 | async-start | bytes 4718592 | tf_op jit(solution)/shard_map/reduce_scatter | solution.py:114
  176.5 6.1 %copy-start.8 = (bf16[1,1024,2048]{2,1,0:T(8,128)(2,1)S(1)}, bf16[1,1024,2048]{2,1,0:T(8,128)(2,1)}, u32[]{:S(2)}) copy-start(bf16[1,1024,2048]{2,1,0:T(8,128)(2,1)} %param.20) | copy-start | bytes 12582916
  194.9 0.7 copy-start.9
  194.9 1.2 slice-start
  196.1 107.8 %copy-start.3 = (bf16[128,2048]{1,0:T(8,128)(2,1)S(1)}, bf16[128,2048]{1,0:T(8,128)(2,1)}, u32[]{:S(2)}) copy-start(bf16[128,2048]{1,0:T(8,128)(2,1)} %reduce-scatter.3.cloned.1.call-done) | copy-start | bytes 1572868
  197.6 110.6 %copy-start.1 = (bf16[4,128,2048]{2,1,0:T(8,128)(2,1)S(1)}, bf16[4,128,2048]{2,1,0:T(8,128)(2,1)}, u32[]{:S(2)}) copy-start(bf16[4,128,2048]{2,1,0:T(8,128)(2,1)} %param.15) | copy-start | bytes 6291460
Sparse Core Ops, SparseCore 0:
  11.5 25.2 all-gather.2
  60.7 31.4 reduce-scatter.2
  95.7 73.5 all-gather.4
  195.0 108.8 reduce-scatter.4
where the time goes:
time: 315 us
  waiting for transfers between devices  140 us (44%)
  blocking collectives  80.4 us (26%)
  local copies, waits for them, and re-layouts  36.5 us (12%)
  matrix products  23.2 us (7%)
  other arithmetic  20.4 us (6%)
  between operations  14 us (4%)
    all_to_all x1, blocking collectives, on_device(): lax.all_to_all(outgoing, 'blk', split_axis=0, concat_axis=0, tiled=True)  53.9 us
    reduce_scatter x1, waiting for transfers between devices, on_device(): lax.psum_scatter(jnp.where(active.reshape(-1)[:, None], per_row.astype(jn...  48 us
    all_gather x1, waiting for transfers between devices, on_device(): lax.all_gather(ffn_in, 'blk', axis=0, tiled=True)  42 us
    reduce_scatter x1, waiting for transfers between devices, on_device(): lax.psum_scatter(jnp.dot(context_flat, w_out_flat, preferred_element_type...  31.5 us
    all_gather x1, blocking collectives, on_device(): lax.all_gather(dense_gate, 'blk', axis=0, tiled=True)  26.6 us
    all_gather x1, waiting for transfers between devices, on_device(): lax.all_gather(normed, 'seq', axis=0, tiled=True)  18.5 us
    unnamed x22, local copies, waits for them, and re-layouts  9.55 us
    dot_general x1, matrix products, on_device(): jnp.dot(lax.all_gather(normed, 'seq', axis=0, tiled=True), w_flat, prefer...  8.07 us
  transfers between devices with their start and end apart: 4, of which 4 were waited for; matrix products, arithmetic and copies ran while one was open for 6% of the time, Pallas kernels for 0%

commit v1 on v0

v1 whole, which is shorter than its diff:
```python
import math

import jax
import jax.numpy as jnp
from jax import lax
from jax.sharding import PartitionSpec as P

EPS = 1e-06


def rms_norm(value, gain):
    wide = value.astype(jnp.float32)
    scale = lax.rsqrt(jnp.mean(wide * wide, axis=-1, keepdims=True) + EPS)
    return (wide * scale * gain.astype(jnp.float32)).astype(jnp.bfloat16)


def swap(value, axis, step):
    size = lax.axis_size(axis)
    return lax.ppermute(value, axis, [(i, i ^ step) for i in range(size)])


def on_device(
    residual_in,
    segment_ids,
    attn_gain,
    w_qkv,
    w_out,
    ffn_gain,
    w_router,
    routes,
    w_gate_up,
    w_down,
    page_owner,
):
    own = residual_in[0]
    tok_dev, width = own.shape
    heads_here = w_qkv.shape[1]
    head_dim = w_out.shape[1]
    seq_count = lax.axis_size("seq")
    blk_count = lax.axis_size("blk")
    seq_me = lax.axis_index("seq")
    blk_me = lax.axis_index("blk")
    seq_steps = jnp.arange(seq_count, dtype=jnp.int32)
    blk_steps = jnp.arange(blk_count, dtype=jnp.int32)

    core = swap(own, "seq", 1)
    far = swap(own, "seq", 2)
    far_core = swap(far, "seq", 1)

    capacity = tok_dev * 3 // 8
    route_rows = routes[0]
    experts = blk_me ^ blk_steps
    chosen = jnp.any(route_rows[:, :, None] == experts[None, None, :], axis=1)
    rank = jnp.cumsum(chosen.astype(jnp.int32), axis=0) - 1
    slot = jnp.where(chosen, rank, -1)
    slots = jnp.arange(capacity, dtype=jnp.int32)
    hit = slot.T[:, None, :] == slots[None, :, None]
    pick = hit.astype(jnp.bfloat16).reshape(blk_count * capacity, tok_dev)

    w_flat = w_qkv.reshape(width, heads_here * 3 * head_dim)

    def project(rows):
        return jnp.dot(
            rms_norm(rows, attn_gain), w_flat, preferred_element_type=jnp.float32
        ).astype(jnp.bfloat16)

    qkv = jnp.concatenate(
        [
            project(jnp.concatenate([own, core], axis=0)),
            project(jnp.concatenate([far, far_core], axis=0)),
        ],
        axis=0,
    )
    group_len = qkv.shape[0]
    segment_row = jnp.take(
        segment_ids[0].reshape(seq_count, tok_dev), seq_me ^ seq_steps, axis=0
    ).reshape(group_len)

    page_len = group_len // blk_count
    per_dev = tok_dev // page_len
    qkv_heads = qkv.reshape(group_len, heads_here, 3 * head_dim)
    kv_rows = qkv_heads[:, :, head_dim:].reshape(blk_count, page_len, heads_here * 2 * head_dim)
    owners = page_owner[0]
    page_of = jnp.sum(
        jnp.where(owners[None, :] == experts[:, None], blk_steps[None, :], 0), axis=1
    )
    place = ((page_of // per_dev) ^ seq_me) * per_dev + page_of % per_dev
    outgoing = jnp.take(kv_rows, place, axis=0)
    arrived = jnp.stack(
        [outgoing[0]] + [swap(outgoing[s], "blk", s) for s in range(1, blk_count)]
    )
    kv_cache = jnp.take(arrived, experts, axis=0)[None]

    query = qkv_heads[:, :, :head_dim]
    key_rows = qkv_heads[:, :, head_dim : 2 * head_dim]
    value_rows = qkv_heads[:, :, 2 * head_dim :]
    scores = jnp.einsum(
        "qhd,khd->hqk", query, key_rows, preferred_element_type=jnp.float32
    ) / math.sqrt(head_dim)
    same = segment_row[:, None] == segment_row[None, :]
    scores = jnp.where(same[None], scores, jnp.float32(-1e30))
    top = jnp.max(scores, axis=-1, keepdims=True)
    weights = jnp.exp(scores - top)
    probs = (weights / jnp.sum(weights, axis=-1, keepdims=True)).astype(jnp.bfloat16)
    context = jnp.einsum(
        "hqk,khd->qhd", probs, value_rows, preferred_element_type=jnp.float32
    ).astype(jnp.bfloat16)
    context_flat = context.reshape(group_len, heads_here * head_dim)
    w_out_flat = w_out.reshape(heads_here * head_dim, width)
    mixed = jnp.dot(context_flat, w_out_flat, preferred_element_type=jnp.float32)
    parts = mixed.astype(jnp.bfloat16).reshape(seq_count, tok_dev, width)

    here = parts[3]
    far_sum = (parts[2].astype(jnp.float32) + swap(here, "seq", 1).astype(jnp.float32)).astype(
        jnp.bfloat16
    )
    from_core = swap(parts[1], "seq", 1)
    from_far = swap(far_sum, "seq", 2)
    resid = (
        own.astype(jnp.float32)
        + (mixed[:tok_dev] + from_core.astype(jnp.float32))
        + from_far.astype(jnp.float32)
    ).astype(jnp.bfloat16)

    ffn_in = rms_norm(resid, ffn_gain)
    sent = jnp.dot(pick, ffn_in, preferred_element_type=jnp.float32).astype(jnp.bfloat16)
    sent = sent.reshape(blk_count, capacity, width)
    rows = jnp.concatenate(
        [sent[0]] + [swap(sent[s], "blk", s) for s in range(1, blk_count)], axis=0
    )

    gates = jax.nn.sigmoid(jnp.dot(ffn_in, w_router, preferred_element_type=jnp.float32)).astype(
        jnp.bfloat16
    )
    expert_ids = jnp.arange(w_router.shape[1], dtype=jnp.int32)
    gate_of = jnp.sum(
        jnp.where(experts[:, None, None] == expert_ids[None, None, :], gates[None], 0), axis=2
    ).astype(jnp.bfloat16)
    weigh = jnp.where(hit, gate_of[:, None, :], 0).reshape(blk_count * capacity, tok_dev)

    gate_up = w_gate_up[0]
    down = w_down[0]
    ff_width = down.shape[0]
    both = jnp.dot(rows, gate_up, preferred_element_type=jnp.float32)
    hidden = (jax.nn.silu(both[:, :ff_width]) * both[:, ff_width:]).astype(jnp.bfloat16)
    output = jnp.dot(hidden, down, preferred_element_type=jnp.float32).astype(jnp.bfloat16)
    output = output.reshape(blk_count, capacity, width)
    back = jnp.concatenate(
        [output[0]] + [swap(output[s], "blk", s) for s in range(1, blk_count)], axis=0
    )
    total = lax.dot_general(
        weigh, back, (((0,), (0,)), ((), ())), preferred_element_type=jnp.float32
    )
    residual_out = (resid.astype(jnp.float32) + total).astype(jnp.bfloat16)[None]
    return (residual_out, kv_cache)


def solution(mesh):
    in_specs = (
        P("blk", "seq", None),
        P("blk", None),
        P(),
        P(None, "seq", None),
        P("seq", None, None),
        P(),
        P(),
        P("blk", "seq", None),
        P("blk", None, None),
        P("blk", None, None),
        P("blk", None),
    )
    out_specs = (P("blk", "seq", None), P("blk", None, None, "seq"))
    return jax.shard_map(
        on_device, mesh=mesh, in_specs=in_specs, out_specs=out_specs, check_vma=False
    )
```

time: 315 us -> 174 us (0.55)
  the two profiles are of different devices: /device:TPU:0 before, /device:TPU:8 now
where the time goes in v1:
time: 174 us; the launch traced here: 173 us
  waiting for transfers between devices  65.8 us (38%)
  starting transfers between devices  35.6 us (20%)
  local copies, waits for them, and re-layouts  32 us (18%)
  matrix products  24.7 us (14%)
  other arithmetic  14 us (8%)
    ppermute x27, waiting for transfers between devices, swap(): return lax.ppermute(value, axis, [(i, i ^ step) for i in range(size)])  65.8 us
    ppermute x27, starting transfers between devices, swap(): return lax.ppermute(value, axis, [(i, i ^ step) for i in range(size)])  35.6 us
    unnamed x47, local copies, waits for them, and re-layouts  16.8 us
    dot_general x1, matrix products, on_device(): jnp.dot(context_flat, w_out_flat, preferred_element_type=jnp.float32)  6.86 us
    dot_general x2, matrix products, project(): jnp.dot(rms_norm(rows, attn_gain), w_flat, preferred_element_type=jnp.flo...  6.82 us
    dot_general x1, matrix products, on_device(): both = jnp.dot(rows, gate_up, preferred_element_type=jnp.float32)  6.23 us
    sub x1, other arithmetic, on_device(): weights = jnp.exp(scores - top)  4.04 us
    reshape x1, local copies, waits for them, and re-layouts, on_device(): qkv_heads = qkv.reshape(group_len, heads_here, 3 * head_dim)  3.94 us
  transfers between devices with their start and end apart: 27, of which 14 were waited for; matrix products, arithmetic and copies ran while one was open for 25% of the time, Pallas kernels for 0%

profile of v1, /device:TPU:8, one launch (start us, length us, event | category | flops | bytes accessed | tf_op | source)
XLA Modules:
  0.0 173.2 jit_solution(13560556298756741555)
XLA Ops:
  5.7 6.7 %copy.29 = bf16[256,8,4,384]{3,1,2,0:T(8,128)(2,1)} copy(bf16[256,8,4,384]{3,2,1,0:T(4,128)(2,1)} %bitcast.77) | data formatting | bytes 12582912
  14.9 4.9 %convolution_convert_fusion.2 = bf16[256,1536]{1,0:T(8,128)(2,1)S(1)} fusion(bf16[2048,1536]{1,0:T(8,128)(2,1)} %bitcast.78, f32[2048]{0:T(1024)S(1)} %convert_element_type.92, f32[256]{0:T(256)S(1)} %add_rsqrt_fusion.1, bf16[128,2048]{1,0:T(8,128)(2,1)} %collective-permute-done, bf16[128,2048]{1,0:T(8,128)(2,1)S(1)} %bitcast.85), kind=kOutput, calls=%fused_computation.20 | convolution fusion | flops 1614675968 | bytes 8135680 | tf_op jit(solution)/shard_map/dot_general | solution.py:63
  23.3 3.9 %reshape.207 = bf16[512,4,384]{2,1,0:T(4,128)(2,1)} reshape(bf16[512,1536]{1,0:T(8,128)(2,1)} %pad_maximum_fusion) | data formatting | bytes 3145728 | tf_op jit(solution)/shard_map/reshape | solution.py:81
  38.1 2.6 %collective-permute-start.23 = (bf16[64,1024]{1,0:T(8,128)(2,1)S(1)}, bf16[64,1024]{1,0:T(8,128)(2,1)}, u32[]{:S(2)}, u32[]{:S(2)}) collective-permute-start(bf16[64,1024]{1,0:T(8,128)(2,1)S(1)} %get-tuple-element.31), channel_id=1, source_target_pairs={{0,4},{1,5},{2,6},{3,7},{4,0},{5,1},{6,2},{7,3},{8,12},{9,13},{10,... | collective-permute-start | bytes 393224 | tf_op jit(solution)/shard_map/ppermute | solution.py:19
  42.7 4.0 %fusion.61 = (f32[4,512]{1,0:T(4,128)S(1)}, f32[4,512,512]{1,2,0:T(8,128)}) fusion(f32[4,512,512]{1,2,0:T(8,128)S(1)} %fusion.42, pred[512,512]{0,1:T(8,128)(4,1)S(1)} %broadcast_compare_fusion), kind=kOutput, calls=%fused_computation.138 | output fusion | flops 6291967 | bytes 8658944 | tf_op jit(solution)/shard_map/sub | solution.py:103
  46.7 6.9 %fusion.62 = (bf16[512,2048]{1,0:T(8,128)(2,1)}, f32[512,2048]{1,0:T(8,128)}) fusion(bf16[4,128,2048]{2,1,0:T(8,128)(2,1)S(1)} %copy-done, f32[4,512,512]{1,2,0:T(8,128)} %get-tuple-element.37, f32[4,512]{1,0:T(4,128)S(1)} %get-tuple-element.36, bf16[512,4,128]{2,1,0:T(4,128)(2,1)S(1)} %copy-done.7), kind=kOutput, calls=%fused_computation.139 | convolution fusion | flops 1345585152 | bytes 13115392 | tf_op jit(solution)/shard_map/dot_general | solution.py:110
  70.7 8.2 %collective-permute-done.5 = bf16[128,2048]{1,0:T(8,128)(2,1)S(1)} collective-permute-done((bf16[128,2048]{1,0:T(8,128)(2,1)S(1)}, bf16[128,2048]{1,0:T(8,128)(2,1)S(1)}, u32[]{:S(2)}, u32[]{:S(2)}) %collective-permute-start.5) | collective-permute-done | bytes 524320 | tf_op jit(solution)/shard_map/ppermute | solution.py:19
  84.2 2.3 %collective-permute-start.7 = (bf16[48,2048]{1,0:T(8,128)(2,1)S(1)}, bf16[48,2048]{1,0:T(8,128)(2,1)S(1)}, u32[]{:S(2)}, u32[]{:S(2)}) collective-permute-start(bf16[48,2048]{1,0:T(8,128)(2,1)S(1)} %get-tuple-element.22), channel_id=1, source_target_pairs={{0,2},{1,3},{2,0},{3,1},{4,6},{5,7},{6,4},{7,5},{8,10},{9,11},{10,... | collective-permute-start | bytes 589832 | tf_op jit(solution)/shard_map/ppermute | solution.py:19
  86.5 4.1 %collective-permute-start.9 = (bf16[48,2048]{1,0:T(8,128)(2,1)S(1)}, bf16[48,2048]{1,0:T(8,128)(2,1)S(1)}, u32[]{:S(2)}, u32[]{:S(2)}) collective-permute-start(bf16[48,2048]{1,0:T(8,128)(2,1)S(1)} %get-tuple-element.20), channel_id=1, source_target_pairs={{0,4},{1,5},{2,6},{3,7},{4,0},{5,1},{6,2},{7,3},{8,12},{9,13},{10,... | collective-permute-start | bytes 589832 | tf_op jit(solution)/shard_map/ppermute | solution.py:19
  93.0 6.3 %collective-permute-done.7 = bf16[48,2048]{1,0:T(8,128)(2,1)S(1)} collective-permute-done((bf16[48,2048]{1,0:T(8,128)(2,1)S(1)}, bf16[48,2048]{1,0:T(8,128)(2,1)S(1)}, u32[]{:S(2)}, u32[]{:S(2)}) %collective-permute-start.7) | collective-permute-done | bytes 196640 | tf_op jit(solution)/shard_map/ppermute | solution.py:19
  99.3 2.3 %collective-permute-done.8 = bf16[48,2048]{1,0:T(8,128)(2,1)S(1)} collective-permute-done((bf16[48,2048]{1,0:T(8,128)(2,1)S(1)}, bf16[48,2048]{1,0:T(8,128)(2,1)S(1)}, u32[]{:S(2)}, u32[]{:S(2)}) %collective-permute-start.8) | collective-permute-done | bytes 196640 | tf_op jit(solution)/shard_map/ppermute | solution.py:19
  101.6 11.2 %collective-permute-done.9 = bf16[48,2048]{1,0:T(8,128)(2,1)S(1)} collective-permute-done((bf16[48,2048]{1,0:T(8,128)(2,1)S(1)}, bf16[48,2048]{1,0:T(8,128)(2,1)S(1)}, u32[]{:S(2)}, u32[]{:S(2)}) %collective-permute-start.9) | collective-permute-done | bytes 196640 | tf_op jit(solution)/shard_map/ppermute | solution.py:19
  112.8 4.2 %collective-permute-done.10 = bf16[48,2048]{1,0:T(8,128)(2,1)S(1)} collective-permute-done((bf16[48,2048]{1,0:T(8,128)(2,1)S(1)}, bf16[48,2048]{1,0:T(8,128)(2,1)S(1)}, u32[]{:S(2)}, u32[]{:S(2)}) %collective-permute-start.10) | collective-permute-done | bytes 196640 | tf_op jit(solution)/shard_map/ppermute | solution.py:19
  117.0 3.9 %collective-permute-done.11 = bf16[48,2048]{1,0:T(8,128)(2,1)S(1)} collective-permute-done((bf16[48,2048]{1,0:T(8,128)(2,1)S(1)}, bf16[48,2048]{1,0:T(8,128)(2,1)S(1)}, u32[]{:S(2)}, u32[]{:S(2)}) %collective-permute-start.11) | collective-permute-done | bytes 196640 | tf_op jit(solution)/shard_map/ppermute | solution.py:19
  121.0 2.8 %collective-permute-done.12 = bf16[48,2048]{1,0:T(8,128)(2,1)S(1)} collective-permute-done((bf16[48,2048]{1,0:T(8,128)(2,1)S(1)}, bf16[48,2048]{1,0:T(8,128)(2,1)S(1)}, u32[]{:S(2)}, u32[]{:S(2)}) %collective-permute-start.12) | collective-permute-done | bytes 196640 | tf_op jit(solution)/shard_map/ppermute | solution.py:19
  123.8 6.2 %fusion.1 = f32[384,2048]{1,0:T(8,128)S(1)} fusion(bf16[384,2048]{1,0:T(8,128)(2,1)S(1)} %constant_dynamic-update-slice_fusion, bf16[1,2048,2048]{2,1,0:T(8,128)(2,1)} %param.21), kind=kOutput, calls=%fused_computation.4 | convolution fusion | flops 3221225472 | bytes 13107200 | tf_op jit(solution)/shard_map/dot_general | solution.py:144
  133.6 2.7 %collective-permute-start.15 = (bf16[48,2048]{1,0:T(8,128)(2,1)S(1)}, bf16[48,2048]{1,0:T(8,128)(2,1)S(1)}, u32[]{:S(2)}, u32[]{:S(2)}) collective-permute-start(bf16[48,2048]{1,0:T(8,128)(2,1)S(1)} %get-tuple-element.13), channel_id=1, source_target_pairs={{0,3},{1,2},{2,1},{3,0},{4,7},{5,6},{6,5},{7,4},{8,11},{9,10},{10,... | collective-permute-start | bytes 589832 | tf_op jit(solution)/shard_map/ppermute | solution.py:19
  136.3 2.2 %collective-permute-start.16 = (bf16[48,2048]{1,0:T(8,128)(2,1)S(1)}, bf16[48,2048]{1,0:T(8,128)(2,1)S(1)}, u32[]{:S(2)}, u32[]{:S(2)}) collective-permute-start(bf16[48,2048]{1,0:T(8,128)(2,1)S(1)} %get-tuple-element.12), channel_id=1, source_target_pairs={{0,4},{1,5},{2,6},{3,7},{4,0},{5,1},{6,2},{7,3},{8,12},{9,13},{10,... | collective-permute-start | bytes 589832 | tf_op jit(solution)/shard_map/ppermute | solution.py:19
  139.7 2.9 %collective-permute-start.18 = (bf16[48,2048]{1,0:T(8,128)(2,1)S(1)}, bf16[48,2048]{1,0:T(8,128)(2,1)S(1)}, u32[]{:S(2)}, u32[]{:S(2)}) collective-permute-start(bf16[48,2048]{1,0:T(8,128)(2,1)S(1)} %get-tuple-element.10), channel_id=1, source_target_pairs={{0,6},{1,7},{2,4},{3,5},{4,2},{5,3},{6,0},{7,1},{8,14},{9,15},{10,... | collective-permute-start | bytes 589832 | tf_op jit(solution)/shard_map/ppermute | solution.py:19
  144.3 2.8 %collective-permute-start.19 = (bf16[48,2048]{1,0:T(8,128)(2,1)S(1)}, bf16[48,2048]{1,0:T(8,128)(2,1)S(1)}, u32[]{:S(2)}, u32[]{:S(2)}) collective-permute-start(bf16[48,2048]{1,0:T(8,128)(2,1)S(1)} %get-tuple-element.9), channel_id=1, source_target_pairs={{0,7},{1,6},{2,5},{3,4},{4,3},{5,2},{6,1},{7,0},{8,15},{9,14},{10,... | collective-permute-start | bytes 589832 | tf_op jit(solution)/shard_map/ppermute | solution.py:19
  147.1 13.4 %collective-permute-done.16 = bf16[48,2048]{1,0:T(8,128)(2,1)S(1)} collective-permute-done((bf16[48,2048]{1,0:T(8,128)(2,1)S(1)}, bf16[48,2048]{1,0:T(8,128)(2,1)S(1)}, u32[]{:S(2)}, u32[]{:S(2)}) %collective-permute-start.16) | collective-permute-done | bytes 196640 | tf_op jit(solution)/shard_map/ppermute | solution.py:19
  160.5 4.2 %collective-permute-done.17 = bf16[48,2048]{1,0:T(8,128)(2,1)S(1)} collective-permute-done((bf16[48,2048]{1,0:T(8,128)(2,1)S(1)}, bf16[48,2048]{1,0:T(8,128)(2,1)S(1)}, u32[]{:S(2)}, u32[]{:S(2)}) %collective-permute-start.17) | collective-permute-done | bytes 196640 | tf_op jit(solution)/shard_map/ppermute | solution.py:19
  164.7 4.4 %collective-permute-done.18 = bf16[48,2048]{1,0:T(8,128)(2,1)S(1)} collective-permute-done((bf16[48,2048]{1,0:T(8,128)(2,1)S(1)}, bf16[48,2048]{1,0:T(8,128)(2,1)S(1)}, u32[]{:S(2)}, u32[]{:S(2)}) %collective-permute-start.18) | collective-permute-done | bytes 196640 | tf_op jit(solution)/shard_map/ppermute | solution.py:19
  169.1 2.8 %collective-permute-done.19 = bf16[48,2048]{1,0:T(8,128)(2,1)S(1)} collective-permute-done((bf16[48,2048]{1,0:T(8,128)(2,1)S(1)}, bf16[48,2048]{1,0:T(8,128)(2,1)S(1)}, u32[]{:S(2)}, u32[]{:S(2)}) %collective-permute-start.19) | collective-permute-done | bytes 196640 | tf_op jit(solution)/shard_map/ppermute | solution.py:19
  (139 shorter events, 56.3 us)
Async XLA Ops:
  0.6 13.9 %collective-permute-start.1 = (bf16[128,2048]{1,0:T(8,128)(2,1)}, bf16[128,2048]{1,0:T(8,128)(2,1)S(1)}, u32[]{:S(2)}, u32[]{:S(2)}) collective-permute-start(bf16[128,2048]{1,0:T(8,128)(2,1)} %bitcast.82), channel_id=1, source_target_pairs={{0,16},{8,24},{16,0},{24,8},{1,17},{9,25},{17,1},{25,9},{2,18},{10... | collective-permute-start | bytes 1572872 | tf_op jit(solution)/shard_map/ppermute | solution.py:19
  2.2 10.6 %collective-permute-start = (bf16[128,2048]{1,0:T(8,128)(2,1)}, bf16[128,2048]{1,0:T(8,128)(2,1)}, u32[]{:S(2)}, u32[]{:S(2)}) collective-permute-start(bf16[128,2048]{1,0:T(8,128)(2,1)} %bitcast.83), channel_id=1, source_target_pairs={{0,8},{8,0},{16,24},{24,16},{1,9},{9,1},{17,25},{25,17},{2,10},{10... | collective-permute-start | bytes 1572872 | tf_op jit(solution)/shard_map/ppermute | solution.py:19
  34.6 20.3 %collective-permute-start.20 = (bf16[64,1024]{1,0:T(8,128)(2,1)}, bf16[64,1024]{1,0:T(8,128)(2,1)}, u32[]{:S(2)}, u32[]{:S(2)}) collective-permute-start(bf16[64,1024]{1,0:T(8,128)(2,1)} %get-tuple-element.34), channel_id=1, source_target_pairs={{0,1},{1,0},{2,3},{3,2},{4,5},{5,4},{6,7},{7,6},{8,9},{9,8},{10,11... | collective-permute-start | bytes 393224 | tf_op jit(solution)/shard_map/ppermute | solution.py:19
  36.1 22.0 %collective-permute-start.21 = (bf16[64,1024]{1,0:T(8,128)(2,1)}, bf16[64,1024]{1,0:T(8,128)(2,1)}, u32[]{:S(2)}, u32[]{:S(2)}) collective-permute-start(bf16[64,1024]{1,0:T(8,128)(2,1)} %get-tuple-element.33), channel_id=1, source_target_pairs={{0,2},{1,3},{2,0},{3,1},{4,6},{5,7},{6,4},{7,5},{8,10},{9,11},{10,... | collective-permute-start | bytes 393224 | tf_op jit(solution)/shard_map/ppermute | solution.py:19
  36.5 23.1 %collective-permute-start.22 = (bf16[64,1024]{1,0:T(8,128)(2,1)}, bf16[64,1024]{1,0:T(8,128)(2,1)}, u32[]{:S(2)}, u32[]{:S(2)}) collective-permute-start(bf16[64,1024]{1,0:T(8,128)(2,1)} %get-tuple-element.32), channel_id=1, source_target_pairs={{0,3},{1,2},{2,1},{3,0},{4,7},{5,6},{6,5},{7,4},{8,11},{9,10},{10,... | collective-permute-start | bytes 393224 | tf_op jit(solution)/shard_map/ppermute | solution.py:19
  38.1 23.6 %collective-permute-start.23 = (bf16[64,1024]{1,0:T(8,128)(2,1)S(1)}, bf16[64,1024]{1,0:T(8,128)(2,1)}, u32[]{:S(2)}, u32[]{:S(2)}) collective-permute-start(bf16[64,1024]{1,0:T(8,128)(2,1)S(1)} %get-tuple-element.31), channel_id=1, source_target_pairs={{0,4},{1,5},{2,6},{3,7},{4,0},{5,1},{6,2},{7,3},{8,12},{9,13},{10,... | collective-permute-start | bytes 393224 | tf_op jit(solution)/shard_map/ppermute | solution.py:19
  40.7 25.3 %collective-permute-start.24 = (bf16[64,1024]{1,0:T(8,128)(2,1)S(1)}, bf16[64,1024]{1,0:T(8,128)(2,1)}, u32[]{:S(2)}, u32[]{:S(2)}) collective-permute-start(bf16[64,1024]{1,0:T(8,128)(2,1)S(1)} %get-tuple-element.30), channel_id=1, source_target_pairs={{0,5},{1,4},{2,7},{3,6},{4,1},{5,0},{6,3},{7,2},{8,13},{9,12},{10,... | collective-permute-start | bytes 393224 | tf_op jit(solution)/shard_map/ppermute | solution.py:19
  54.9 12.6 %collective-permute-start.25 = (bf16[64,1024]{1,0:T(8,128)(2,1)S(1)}, bf16[64,1024]{1,0:T(8,128)(2,1)S(1)}, u32[]{:S(2)}, u32[]{:S(2)}) collective-permute-start(bf16[64,1024]{1,0:T(8,128)(2,1)S(1)} %get-tuple-element.29), channel_id=1, source_target_pairs={{0,6},{1,7},{2,4},{3,5},{4,2},{5,3},{6,0},{7,1},{8,14},{9,15},{10,... | collective-permute-start | bytes 393224 | tf_op jit(solution)/shard_map/ppermute | solution.py:19
  59.7 8.5 %collective-permute-start.26 = (bf16[64,1024]{1,0:T(8,128)(2,1)S(1)}, bf16[64,1024]{1,0:T(8,128)(2,1)S(1)}, u32[]{:S(2)}, u32[]{:S(2)}) collective-permute-start(bf16[64,1024]{1,0:T(8,128)(2,1)S(1)} %get-tuple-element.28), channel_id=1, source_target_pairs={{0,7},{1,6},{2,5},{3,4},{4,3},{5,2},{6,1},{7,0},{8,15},{9,14},{10,... | collective-permute-start | bytes 393224 | tf_op jit(solution)/shard_map/ppermute | solution.py:19
  61.7 9.0 %collective-permute-start.3 = (bf16[128,2048]{1,0:T(8,128)(2,1)S(1)}, bf16[128,2048]{1,0:T(8,128)(2,1)}, u32[]{:S(2)}, u32[]{:S(2)}) collective-permute-start(bf16[128,2048]{1,0:T(8,128)(2,1)S(1)} %get-tuple-element.7), channel_id=1, source_target_pairs={{0,8},{8,0},{16,24},{24,16},{1,9},{9,1},{17,25},{25,17},{2,10},{10... | collective-permute-start | bytes 1572872 | tf_op jit(solution)/shard_map/ppermute | solution.py:19
  64.7 14.2 %collective-permute-start.5 = (bf16[128,2048]{1,0:T(8,128)(2,1)S(1)}, bf16[128,2048]{1,0:T(8,128)(2,1)S(1)}, u32[]{:S(2)}, u32[]{:S(2)}) collective-permute-start(bf16[128,2048]{1,0:T(8,128)(2,1)S(1)} %add_convert_fusion), channel_id=1, source_target_pairs={{0,16},{8,24},{16,0},{24,8},{1,17},{9,25},{17,1},{25,9},{2,18},{10... | collective-permute-start | bytes 1572872 | tf_op jit(solution)/shard_map/ppermute | solution.py:19
  81.5 10.0 %collective-permute-start.6 = (bf16[48,2048]{1,0:T(8,128)(2,1)S(1)}, bf16[48,2048]{1,0:T(8,128)(2,1)S(1)}, u32[]{:S(2)}, u32[]{:S(2)}) collective-permute-start(bf16[48,2048]{1,0:T(8,128)(2,1)S(1)} %get-tuple-element.23), channel_id=1, source_target_pairs={{0,1},{1,0},{2,3},{3,2},{4,5},{5,4},{6,7},{7,6},{8,9},{9,8},{10,11... | collective-permute-start | bytes 589832 | tf_op jit(solution)/shard_map/ppermute | solution.py:19
  84.2 15.0 %collective-permute-start.7 = (bf16[48,2048]{1,0:T(8,128)(2,1)S(1)}, bf16[48,2048]{1,0:T(8,128)(2,1)S(1)}, u32[]{:S(2)}, u32[]{:S(2)}) collective-permute-start(bf16[48,2048]{1,0:T(8,128)(2,1)S(1)} %get-tuple-element.22), channel_id=1, source_target_pairs={{0,2},{1,3},{2,0},{3,1},{4,6},{5,7},{6,4},{7,5},{8,10},{9,11},{10,... | collective-permute-start | bytes 589832 | tf_op jit(solution)/shard_map/ppermute | solution.py:19
  86.5 15.2 %collective-permute-start.8 = (bf16[48,2048]{1,0:T(8,128)(2,1)S(1)}, bf16[48,2048]{1,0:T(8,128)(2,1)S(1)}, u32[]{:S(2)}, u32[]{:S(2)}) collective-permute-start(bf16[48,2048]{1,0:T(8,128)(2,1)S(1)} %get-tuple-element.21), channel_id=1, source_target_pairs={{0,3},{1,2},{2,1},{3,0},{4,7},{5,6},{6,5},{7,4},{8,11},{9,10},{10,... | collective-permute-start | bytes 589832 | tf_op jit(solution)/shard_map/ppermute | solution.py:19
  86.5 26.3 %collective-permute-start.9 = (bf16[48,2048]{1,0:T(8,128)(2,1)S(1)}, bf16[48,2048]{1,0:T(8,128)(2,1)S(1)}, u32[]{:S(2)}, u32[]{:S(2)}) collective-permute-start(bf16[48,2048]{1,0:T(8,128)(2,1)S(1)} %get-tuple-element.20), channel_id=1, source_target_pairs={{0,4},{1,5},{2,6},{3,7},{4,0},{5,1},{6,2},{7,3},{8,12},{9,13},{10,... | collective-permute-start | bytes 589832 | tf_op jit(solution)/shard_map/ppermute | solution.py:19
  90.6 26.4 %collective-permute-start.10 = (bf16[48,2048]{1,0:T(8,128)(2,1)S(1)}, bf16[48,2048]{1,0:T(8,128)(2,1)S(1)}, u32[]{:S(2)}, u32[]{:S(2)}) collective-permute-start(bf16[48,2048]{1,0:T(8,128)(2,1)S(1)} %get-tuple-element.19), channel_id=1, source_target_pairs={{0,5},{1,4},{2,7},{3,6},{4,1},{5,0},{6,3},{7,2},{8,13},{9,12},{10,... | collective-permute-start | bytes 589832 | tf_op jit(solution)/shard_map/ppermute | solution.py:19
  91.5 29.4 %collective-permute-start.11 = (bf16[48,2048]{1,0:T(8,128)(2,1)S(1)}, bf16[48,2048]{1,0:T(8,128)(2,1)S(1)}, u32[]{:S(2)}, u32[]{:S(2)}) collective-permute-start(bf16[48,2048]{1,0:T(8,128)(2,1)S(1)} %get-tuple-element.18), channel_id=1, source_target_pairs={{0,6},{1,7},{2,4},{3,5},{4,2},{5,3},{6,0},{7,1},{8,14},{9,15},{10,... | collective-permute-start | bytes 589832 | tf_op jit(solution)/shard_map/ppermute | solution.py:19
  99.2 24.5 %collective-permute-start.12 = (bf16[48,2048]{1,0:T(8,128)(2,1)S(1)}, bf16[48,2048]{1,0:T(8,128)(2,1)S(1)}, u32[]{:S(2)}, u32[]{:S(2)}) collective-permute-start(bf16[48,2048]{1,0:T(8,128)(2,1)S(1)} %get-tuple-element.17), channel_id=1, source_target_pairs={{0,7},{1,6},{2,5},{3,4},{4,3},{5,2},{6,1},{7,0},{8,15},{9,14},{10,... | collective-permute-start | bytes 589832 | tf_op jit(solution)/shard_map/ppermute | solution.py:19
  133.5 10.8 %collective-permute-start.14 = (bf16[48,2048]{1,0:T(8,128)(2,1)S(1)}, bf16[48,2048]{1,0:T(8,128)(2,1)S(1)}, u32[]{:S(2)}, u32[]{:S(2)}) collective-permute-start(bf16[48,2048]{1,0:T(8,128)(2,1)S(1)} %get-tuple-element.14), channel_id=1, source_target_pairs={{0,2},{1,3},{2,0},{3,1},{4,6},{5,7},{6,4},{7,5},{8,10},{9,11},{10,... | collective-permute-start | bytes 589832 | tf_op jit(solution)/shard_map/ppermute | solution.py:19
  133.6 13.5 %collective-permute-start.15 = (bf16[48,2048]{1,0:T(8,128)(2,1)S(1)}, bf16[48,2048]{1,0:T(8,128)(2,1)S(1)}, u32[]{:S(2)}, u32[]{:S(2)}) collective-permute-start(bf16[48,2048]{1,0:T(8,128)(2,1)S(1)} %get-tuple-element.13), channel_id=1, source_target_pairs={{0,3},{1,2},{2,1},{3,0},{4,7},{5,6},{6,5},{7,4},{8,11},{9,10},{10,... | collective-permute-start | bytes 589832 | tf_op jit(solution)/shard_map/ppermute | solution.py:19
  136.3 24.2 %collective-permute-start.16 = (bf16[48,2048]{1,0:T(8,128)(2,1)S(1)}, bf16[48,2048]{1,0:T(8,128)(2,1)S(1)}, u32[]{:S(2)}, u32[]{:S(2)}) collective-permute-start(bf16[48,2048]{1,0:T(8,128)(2,1)S(1)} %get-tuple-element.12), channel_id=1, source_target_pairs={{0,4},{1,5},{2,6},{3,7},{4,0},{5,1},{6,2},{7,3},{8,12},{9,13},{10,... | collective-permute-start | bytes 589832 | tf_op jit(solution)/shard_map/ppermute | solution.py:19
  138.5 26.3 %collective-permute-start.17 = (bf16[48,2048]{1,0:T(8,128)(2,1)S(1)}, bf16[48,2048]{1,0:T(8,128)(2,1)S(1)}, u32[]{:S(2)}, u32[]{:S(2)}) collective-permute-start(bf16[48,2048]{1,0:T(8,128)(2,1)S(1)} %get-tuple-element.11), channel_id=1, source_target_pairs={{0,5},{1,4},{2,7},{3,6},{4,1},{5,0},{6,3},{7,2},{8,13},{9,12},{10,... | collective-permute-start | bytes 589832 | tf_op jit(solution)/shard_map/ppermute | solution.py:19
  139.7 29.4 %collective-permute-start.18 = (bf16[48,2048]{1,0:T(8,128)(2,1)S(1)}, bf16[48,2048]{1,0:T(8,128)(2,1)S(1)}, u32[]{:S(2)}, u32[]{:S(2)}) collective-permute-start(bf16[48,2048]{1,0:T(8,128)(2,1)S(1)} %get-tuple-element.10), channel_id=1, source_target_pairs={{0,6},{1,7},{2,4},{3,5},{4,2},{5,3},{6,0},{7,1},{8,14},{9,15},{10,... | collective-permute-start | bytes 589832 | tf_op jit(solution)/shard_map/ppermute | solution.py:19
  144.3 27.6 %collective-permute-start.19 = (bf16[48,2048]{1,0:T(8,128)(2,1)S(1)}, bf16[48,2048]{1,0:T(8,128)(2,1)S(1)}, u32[]{:S(2)}, u32[]{:S(2)}) collective-permute-start(bf16[48,2048]{1,0:T(8,128)(2,1)S(1)} %get-tuple-element.9), channel_id=1, source_target_pairs={{0,7},{1,6},{2,5},{3,4},{4,3},{5,2},{6,1},{7,0},{8,15},{9,14},{10,... | collective-permute-start | bytes 589832 | tf_op jit(solution)/shard_map/ppermute | solution.py:19
  (18 other events, 169.9 us)

commit v2 on v1

v2 whole, which is shorter than its diff:
```python
import functools
import math

import jax
import jax.numpy as jnp
from jax import lax
from jax.experimental import pallas as pl
from jax.experimental.pallas import tpu as pltpu
from jax.sharding import PartitionSpec as P

EPS = 1e-06
F32 = jnp.float32
BF16 = jnp.bfloat16
MIB = 1 << 20


def rms_norm(value, gain):
    wide = value.astype(F32)
    scale = lax.rsqrt(jnp.mean(wide * wide, axis=-1, keepdims=True) + EPS)
    return (wide * scale * gain.astype(F32)).astype(BF16)


def swap(value, axis, step):
    size = lax.axis_size(axis)
    return lax.ppermute(value, axis, [(i, i ^ step) for i in range(size)])


def whole(shape):
    return pl.BlockSpec(shape, lambda *_: (0,) * len(shape))


def params(mib):
    return pltpu.CompilerParams(vmem_limit_bytes=mib * MIB)


def cost(flops, bytes_accessed):
    return pl.CostEstimate(flops=flops, bytes_accessed=bytes_accessed, transcendentals=0)


def project_kernel(a_ref, b_ref, gain_ref, w_ref, q_ref, kv_ref, normed):
    rows = a_ref.shape[0]
    head_dim = q_ref.shape[1]

    @pl.when(pl.program_id(0) == 0)
    def _():
        normed[:rows] = rms_norm(a_ref[...], gain_ref[...])
        normed[rows:] = rms_norm(b_ref[...], gain_ref[...])

    out = jnp.dot(normed[...], w_ref[...], preferred_element_type=F32).astype(BF16)
    q_ref[...] = out[:, :head_dim]
    kv_ref[...] = out[:, head_dim:]


def project(a, b, gain, w_flat, heads, head_dim):
    rows, width = a.shape
    return pl.pallas_call(
        project_kernel,
        grid=(heads,),
        out_shape=(
            jax.ShapeDtypeStruct((2 * rows, heads * head_dim), BF16),
            jax.ShapeDtypeStruct((2 * rows, heads * 2 * head_dim), BF16),
        ),
        in_specs=[
            whole((rows, width)),
            whole((rows, width)),
            whole((1, width)),
            pl.BlockSpec((width, 3 * head_dim), lambda h: (0, h)),
        ],
        out_specs=(
            pl.BlockSpec((2 * rows, head_dim), lambda h: (0, h)),
            pl.BlockSpec((2 * rows, 2 * head_dim), lambda h: (0, h)),
        ),
        scratch_shapes=[pltpu.VMEM((2 * rows, width), BF16)],
        compiler_params=params(24),
        cost_estimate=cost(2 * 2 * rows * width * 3 * heads * head_dim, w_flat.size * 2),
        name="project",
    )(a, b, gain, w_flat)


def pages_out_kernel(place_ref, near_ref, far_ref, *refs):
    outs, sems = refs[:-1], refs[-1]
    page_len = outs[0].shape[0]
    pages_near = near_ref.shape[0] // page_len
    for s, out in enumerate(outs):
        place = place_ref[s]

        @pl.when(place < pages_near)
        def _(place=place, out=out, s=s):
            start = pl.multiple_of(place * page_len, page_len)
            pltpu.make_async_copy(near_ref.at[pl.ds(start, page_len)], out, sems.at[s]).start()

        @pl.when(place >= pages_near)
        def _(place=place, out=out, s=s):
            start = pl.multiple_of((place - pages_near) * page_len, page_len)
            pltpu.make_async_copy(far_ref.at[pl.ds(start, page_len)], out, sems.at[s]).start()

    for s, out in enumerate(outs):
        pltpu.make_async_copy(near_ref.at[pl.ds(0, page_len)], out, sems.at[s]).wait()


def pages_out(place, near, far, count):
    page_len = 2 * near.shape[0] // count
    shape = jax.ShapeDtypeStruct((page_len, near.shape[1]), BF16)
    any_spec = pl.BlockSpec(memory_space=pl.ANY)
    return pl.pallas_call(
        pages_out_kernel,
        out_shape=(shape,) * count,
        in_specs=[pl.BlockSpec(memory_space=pltpu.SMEM), any_spec, any_spec],
        out_specs=(any_spec,) * count,
        scratch_shapes=[pltpu.SemaphoreType.DMA((count,))],
        cost_estimate=cost(0, 4 * near.size * 2),
        name="pages_out",
    )(place, near, far)


def pages_in_kernel(slot_ref, *refs):
    pages, out, sems = refs[:-2], refs[-2], refs[-1]
    copies = [
        pltpu.make_async_copy(page, out.at[0, slot_ref[s]], sems.at[s])
        for s, page in enumerate(pages)
    ]
    for copy in copies:
        copy.start()
    for copy in copies:
        copy.wait()


def pages_in(slot, pages):
    count = len(pages)
    any_spec = pl.BlockSpec(memory_space=pl.ANY)
    return pl.pallas_call(
        pages_in_kernel,
        out_shape=jax.ShapeDtypeStruct((1, count) + pages[0].shape, BF16),
        in_specs=[pl.BlockSpec(memory_space=pltpu.SMEM)] + [any_spec] * count,
        out_specs=any_spec,
        scratch_shapes=[pltpu.SemaphoreType.DMA((count,))],
        cost_estimate=cost(0, 4 * count * pages[0].size),
        name="pages_in",
    )(slot, *pages)


def attend_kernel(
    col_ref, row_ref, q_near, q_far, kv_near, kv_far, keep_ref, send_ref, bias, *, head_dim
):
    half = q_near.shape[0]
    block = half // 2
    factor = math.log2(math.e) / math.sqrt(head_dim)
    bias[...] = jnp.where(col_ref[...] == row_ref[...], F32(0), F32(-1e30))
    for h in range(q_near.shape[1] // head_dim):
        q_cols = slice(h * head_dim, (h + 1) * head_dim)
        k_cols = slice(2 * h * head_dim, (2 * h + 1) * head_dim)
        v_cols = slice((2 * h + 1) * head_dim, (2 * h + 2) * head_dim)
        key = jnp.concatenate([kv_near[:, k_cols], kv_far[:, k_cols]], axis=0)
        value = jnp.concatenate([kv_near[:, v_cols], kv_far[:, v_cols]], axis=0)
        for part, q_ref in enumerate((q_near, q_far)):
            scores = lax.dot_general(
                q_ref[:, q_cols], key, (((1,), (1,)), ((), ())), preferred_element_type=F32
            )
            scores = scores + bias[part * half : (part + 1) * half]
            top = jnp.max(scores, axis=-1, keepdims=True)
            weights = jnp.exp2((scores - top) * factor)
            total = jnp.sum(weights, axis=-1, keepdims=True)
            context = jnp.dot(weights.astype(BF16), value, preferred_element_type=F32)
            context = (context / total).astype(BF16)
            rows = slice(part * block, (part + 1) * block)
            keep_ref[rows, q_cols] = context[:block]
            send_ref[rows, q_cols] = context[block:]


def attend(segment_row, q_near, q_far, kv_near, kv_far, head_dim):
    group_len = segment_row.shape[0]
    half = q_near.shape[0]
    cols = q_near.shape[1]
    shape = jax.ShapeDtypeStruct((half, cols), BF16)
    return pl.pallas_call(
        functools.partial(attend_kernel, head_dim=head_dim),
        out_shape=(shape, shape),
        scratch_shapes=[pltpu.VMEM((group_len, group_len), F32)],
        compiler_params=params(32),
        cost_estimate=cost(4 * group_len * group_len * cols, 6 * q_near.size * 2),
        name="attend",
    )(segment_row[:, None], segment_row[None, :], q_near, q_far, kv_near, kv_far)


def out_project_kernel(mine_ref, theirs_ref, w_mine, w_theirs, out_ref):
    out = jnp.dot(mine_ref[...], w_mine[...], preferred_element_type=F32)
    out = out + jnp.dot(theirs_ref[...], w_theirs[...], preferred_element_type=F32)
    out_ref[...] = out.astype(out_ref.dtype)


def out_project(which, mine, theirs, w_mine, w_theirs, dtype):
    rows, depth = mine.shape[0] // 2, mine.shape[1]
    width = w_mine.shape[1]
    tile = width // 4
    ctx = pl.BlockSpec((rows, depth), lambda n: (which, 0))
    weight = pl.BlockSpec((depth, tile), lambda n: (0, n))
    return pl.pallas_call(
        out_project_kernel,
        grid=(width // tile,),
        out_shape=jax.ShapeDtypeStruct((rows, width), dtype),
        in_specs=[ctx, ctx, weight, weight],
        out_specs=pl.BlockSpec((rows, tile), lambda n: (0, n)),
        compiler_params=params(16),
        cost_estimate=cost(4 * rows * depth * width, 4 * w_mine.size),
        name="out_project",
    )(mine, theirs, w_mine, w_theirs)


def dispatch_kernel(own_ref, mixed_ref, far_ref, gain_ref, pick_ref, resid_ref, ffn_ref, *outs):
    resid = own_ref[...].astype(F32) + mixed_ref[...] + far_ref[...].astype(F32)
    resid = resid.astype(BF16)
    resid_ref[...] = resid
    ffn_in = rms_norm(resid, gain_ref[...])
    ffn_ref[...] = ffn_in
    rows = outs[0].shape[0]
    picked = jnp.dot(pick_ref[...], ffn_in, preferred_element_type=F32).astype(BF16)
    for s, out in enumerate(outs):
        out[...] = picked[s * rows : (s + 1) * rows]


def dispatch(own, mixed, far, gain, pick, count):
    rows, width = own.shape
    capacity = pick.shape[0] // count
    block = jax.ShapeDtypeStruct((rows, width), BF16)
    sent = jax.ShapeDtypeStruct((capacity, width), BF16)
    return pl.pallas_call(
        dispatch_kernel,
        out_shape=(block, block) + (sent,) * count,
        compiler_params=params(40),
        cost_estimate=cost(2 * pick.size * width, 4 * own.size + 2 * pick.shape[0] * width),
        name="dispatch",
    )(own, mixed, far, gain, pick)


def expert_kernel(*refs, count):
    ins, (gate_ref, up_ref, down_ref) = refs[:count], refs[count : count + 3]
    outs, (rows, total) = refs[count + 3 : 2 * count + 3], refs[2 * count + 3 :]
    size = ins[0].shape[0]
    step = pl.program_id(0)

    @pl.when(step == 0)
    def _():
        for s, ref in enumerate(ins):
            rows[s * size : (s + 1) * size] = ref[...]

    gate = jnp.dot(rows[...], gate_ref[0], preferred_element_type=F32)
    up = jnp.dot(rows[...], up_ref[0], preferred_element_type=F32)
    hidden = (jax.nn.silu(gate) * up).astype(BF16)
    part = jnp.dot(hidden, down_ref[0], preferred_element_type=F32)

    @pl.when(step == 0)
    def _():
        total[...] = part

    @pl.when(step > 0)
    def _():
        total[...] += part

    @pl.when(step == pl.num_programs(0) - 1)
    def _():
        for s, out in enumerate(outs):
            out[...] = total[s * size : (s + 1) * size].astype(BF16)


def expert(blocks, w_gate_up, w_down):
    count = len(blocks)
    size, width = blocks[0].shape
    ff = w_down.shape[1]
    tile = 256
    steps = ff // tile
    return pl.pallas_call(
        functools.partial(expert_kernel, count=count),
        grid=(steps,),
        out_shape=(jax.ShapeDtypeStruct((size, width), BF16),) * count,
        in_specs=[whole((size, width))] * count
        + [
            pl.BlockSpec((1, width, tile), lambda n: (0, 0, n)),
            pl.BlockSpec((1, width, tile), lambda n: (0, 0, n + steps)),
            pl.BlockSpec((1, tile, width), lambda n: (0, n, 0)),
        ],
        out_specs=(whole((size, width)),) * count,
        scratch_shapes=[
            pltpu.VMEM((count * size, width), BF16),
            pltpu.VMEM((count * size, width), F32),
        ],
        compiler_params=params(48),
        cost_estimate=cost(6 * count * size * width * ff, 6 * width * ff),
        name="expert",
    )(*blocks, w_gate_up, w_gate_up, w_down)


def combine_kernel(base_ref, weigh_ref, *refs):
    ins, out_ref, rows = refs[:-2], refs[-2], refs[-1]
    size = ins[0].shape[0]
    for s, ref in enumerate(ins):
        rows[s * size : (s + 1) * size] = ref[...]
    total = jnp.dot(weigh_ref[...], rows[...], preferred_element_type=F32)
    out_ref[...] = (base_ref[...].astype(F32) + total).astype(out_ref.dtype)


def combine(base, weigh, blocks, dtype):
    size, width = blocks[0].shape
    return pl.pallas_call(
        combine_kernel,
        out_shape=jax.ShapeDtypeStruct(base.shape, dtype),
        scratch_shapes=[pltpu.VMEM((len(blocks) * size, width), BF16)],
        compiler_params=params(32),
        cost_estimate=cost(2 * weigh.size * width, 2 * len(blocks) * size * width),
        name="combine",
    )(base, weigh, *blocks)


def on_device(
    residual_in,
    segment_ids,
    attn_gain,
    w_qkv,
    w_out,
    ffn_gain,
    w_router,
    routes,
    w_gate_up,
    w_down,
    page_owner,
):
    own = residual_in[0]
    tok_dev, width = own.shape
    heads_here = w_qkv.shape[1]
    head_dim = w_out.shape[1]
    seq_count = lax.axis_size("seq")
    blk_count = lax.axis_size("blk")
    group_len = seq_count * tok_dev
    seq_me = lax.axis_index("seq")
    blk_me = lax.axis_index("blk")
    seq_steps = jnp.arange(seq_count, dtype=jnp.int32)
    blk_steps = jnp.arange(blk_count, dtype=jnp.int32)

    far = swap(own, "seq", 2)
    core = swap(own, "seq", 1)
    far_core = swap(far, "seq", 1)
    w_mine = w_out.reshape(heads_here * head_dim, width)
    w_theirs = swap(w_mine, "seq", 1)

    capacity = tok_dev * 3 // 8
    route_rows = routes[0]
    experts = blk_me ^ blk_steps
    chosen = jnp.any(route_rows[:, :, None] == experts[None, None, :], axis=1)
    rank = jnp.cumsum(chosen.astype(jnp.int32), axis=0) - 1
    slot = jnp.where(chosen, rank, -1)
    slots = jnp.arange(capacity, dtype=jnp.int32)
    hit = slot.T[:, None, :] == slots[None, :, None]
    pick = hit.astype(BF16).reshape(blk_count * capacity, tok_dev)

    segment_blocks = segment_ids[0].reshape(seq_count, tok_dev)
    at = (seq_me ^ seq_steps)[:, None] == seq_steps[None, :]
    segment_row = jnp.sum(
        jnp.where(at[:, :, None], segment_blocks[None], 0), axis=1
    ).reshape(group_len)

    w_flat = w_qkv.reshape(width, heads_here * 3 * head_dim)
    gain = attn_gain[None]
    q_near, kv_near = project(own, core, gain, w_flat, heads_here, head_dim)
    q_far, kv_far = project(far, far_core, gain, w_flat, heads_here, head_dim)

    page_len = group_len // blk_count
    per_dev = tok_dev // page_len
    owners = page_owner[0]
    page_of = jnp.sum(
        jnp.where(owners[None, :] == experts[:, None], blk_steps[None, :], 0), axis=1
    )
    place = ((page_of // per_dev) ^ seq_me) * per_dev + page_of % per_dev
    outgoing = pages_out(place, kv_near, kv_far, blk_count)
    arrived = [outgoing[0]] + [swap(outgoing[s], "blk", s) for s in range(1, blk_count)]
    kv_cache = pages_in(experts, arrived)

    keep, send = attend(segment_row, q_near, q_far, kv_near, kv_far, head_dim)
    theirs = swap(send, "seq", 1)
    far_sum = out_project(1, keep, theirs, w_mine, w_theirs, BF16)
    from_far = swap(far_sum, "seq", 2)
    mixed = out_project(0, keep, theirs, w_mine, w_theirs, F32)

    resid, ffn_in, *sent = dispatch(own, mixed, from_far, ffn_gain[None], pick, blk_count)

    gates = jax.nn.sigmoid(jnp.dot(ffn_in, w_router, preferred_element_type=F32)).astype(BF16)
    expert_ids = jnp.arange(w_router.shape[1], dtype=jnp.int32)
    gate_of = jnp.sum(
        jnp.where(experts[:, None, None] == expert_ids[None, None, :], gates[None], 0), axis=2
    ).astype(BF16)
    weigh = jnp.where(hit, gate_of[:, None, :], 0).astype(BF16)
    weigh = weigh.reshape(blk_count * capacity, tok_dev).T

    half, quarter = blk_count // 2, blk_count // 4
    groups = [range(half), range(half, half + quarter), range(half + quarter, blk_count)]
    base = resid
    for number, group in enumerate(groups):
        blocks = [sent[s] if s == 0 else swap(sent[s], "blk", s) for s in group]
        outs = expert(blocks, w_gate_up, w_down)
        back = [out if s == 0 else swap(out, "blk", s) for s, out in zip(group, outs)]
        columns = weigh[:, group[0] * capacity : (group[-1] + 1) * capacity]
        base = combine(base, columns, back, BF16 if number == len(groups) - 1 else F32)
    return (base[None], kv_cache)


def solution(mesh):
    in_specs = (
        P("blk", "seq", None),
        P("blk", None),
        P(),
        P(None, "seq", None),
        P("seq", None, None),
        P(),
        P(),
        P("blk", "seq", None),
        P("blk", None, None),
        P("blk", None, None),
        P("blk", None),
    )
    out_specs = (P("blk", "seq", None), P("blk", None, None, "seq"))
    return jax.shard_map(
        on_device, mesh=mesh, in_specs=in_specs, out_specs=out_specs, check_vma=False
    )
```

time: 174 us -> 225 us (1.29)
  the two profiles are of different devices: /device:TPU:8 before, /device:TPU:0 now
where the time goes in v2:
time: 225 us; the launch traced here: 224 us
  Pallas kernels  110 us (49%)
  waiting for transfers between devices  49.3 us (22%)
  starting transfers between devices  46.6 us (21%)
  local copies, waits for them, and re-layouts  14 us (6%)
  other arithmetic  3.57 us (2%)
    ppermute x27, waiting for transfers between devices, swap(): return lax.ppermute(value, axis, [(i, i ^ step) for i in range(size)])  49.3 us
    ppermute x27, starting transfers between devices, swap(): return lax.ppermute(value, axis, [(i, i ^ step) for i in range(size)])  46.6 us
    pallas_call x1, Pallas kernels, pages_in(): pl.pallas_call(pages_in_kernel, out_shape=jax.ShapeDtypeStruct((1, count)...  33.6 us
    pallas_call x1, Pallas kernels, pages_out(): pl.pallas_call(pages_out_kernel, out_shape=(shape,) * count, in_specs=[pl...  33.6 us
    pallas_call x3, Pallas kernels, expert(): pl.pallas_call(functools.partial(expert_kernel, count=count), grid=(steps...  18.3 us
    unnamed x29, local copies, waits for them, and re-layouts  11.7 us
    pallas_call x2, Pallas kernels, project(): pl.pallas_call(project_kernel, grid=(heads,), out_shape=(jax.ShapeDtypeSt...  9.29 us
    pallas_call x2, Pallas kernels, out_project(): pl.pallas_call(out_project_kernel, grid=(width // tile,), out_shape=jax.S...  7.37 us
  transfers between devices with their start and end apart: 27, of which 10 were waited for; matrix products, arithmetic and copies ran while one was open for 6% of the time, Pallas kernels for 45%

profile of v2, /device:TPU:0, one launch (start us, length us, event | category | flops | bytes accessed | tf_op | source)
XLA Modules:
  0.0 224.4 jit_solution(11780897069711000421)
XLA Ops:
  4.7 11.7 %collective-permute-done.1.a_ref = bf16[128,2048]{1,0:T(8,128)(2,1)S(1)} collective-permute-done((bf16[128,2048]{1,0:T(8,128)(2,1)}, bf16[128,2048]{1,0:T(8,128)(2,1)S(1)}, u32[]{:S(2)}, u32[]{:S(2)}) %collective-permute-start.1) | collective-permute-done | bytes 524320 | tf_op jit(solution)/shard_map/ppermute | solution.py:25
  16.5 6.6 %copy.33 = bf16[256,8,4,384]{3,1,2,0:T(8,128)(2,1)} copy(bf16[256,8,4,384]{3,2,1,0:T(4,128)(2,1)} %bitcast.30) | data formatting | bytes 12582912
  23.7 2.8 %copy-done.1 = bf16[256,8,4,384]{3,1,2,0:T(8,128)(2,1)S(1)} copy-done((bf16[256,8,4,384]{3,1,2,0:T(8,128)(2,1)S(1)}, bf16[256,8,4,384]{3,1,2,0:T(8,128)(2,1)}, u32[]{:S(2)}) %copy-start.1) | copy-done | bytes 6291480
  26.5 4.0 %project.2 = (bf16[256,512]{1,0:T(8,128)(2,1)S(1)}, bf16[256,1024]{1,0:T(8,128)(2,1)S(1)}) custom-call(bf16[128,2048]{1,0:T(8,128)(2,1)S(1)} %bitcast.26, bf16[128,2048]{1,0:T(8,128)(2,1)S(1)} %collective-permute-done.b_ref, bf16[1,2048]{1,0:T(2,128)(2,1)S(1)} %broadcast_in_dim.95.gain_ref, bf16[2048,1536]{1,0:T(8,128)(2,1)S(1)} %bitcast.19), custom_call_target="tpu_custom_call" | custom-call | flops 1610612736 | bytes 6291456 | tf_op jit(solution)/shard_map/project/pallas_call | solution.py:56
  30.6 5.2 %project.3 = (bf16[256,512]{1,0:T(8,128)(2,1)S(1)}, bf16[256,1024]{1,0:T(8,128)(2,1)S(1)}) custom-call(bf16[128,2048]{1,0:T(8,128)(2,1)S(1)} %collective-permute-done.1.a_ref, bf16[128,2048]{1,0:T(8,128)(2,1)} %collective-permute-done.2.b_ref, bf16[1,2048]{1,0:T(2,128)(2,1)S(1)} %broadcast_in_dim.95.gain_ref, bf16[2048,1536]{1,0:T(8,128)(2,1)S(1)} %bitcast.20), custom_call_target="tpu_custom_call" | custom-call | flops 1610612736 | bytes 6291456 | tf_op jit(solution)/shard_map/project/pallas_call | solution.py:56
  35.9 3.4 %attend.1 = (bf16[256,512]{1,0:T(8,128)(2,1)S(1)}, bf16[256,512]{1,0:T(8,128)(2,1)}) custom-call(s32[512,1]{1,0:T(8,128)S(1)} %copy.23.col_ref, s32[1,512]{1,0:T(1,128)S(1)} %bitcast.29, bf16[256,512]{1,0:T(8,128)(2,1)S(1)} %get-tuple-element.34.q_near, bf16[256,512]{1,0:T(8,128)(2,1)S(1)} %get-tuple-element.35.q_far, ...), custom_call_target="tpu_custom_call" | custom-call | flops 536870912 | bytes 1572864 | tf_op jit(solution)/shard_map/attend/pallas_call | solution.py:175
  41.2 4.1 %out_project.3 = bf16[128,2048]{1,0:T(8,128)(2,1)} custom-call(bf16[256,512]{1,0:T(8,128)(2,1)S(1)} %get-tuple-element.38.mine_ref, bf16[256,512]{1,0:T(8,128)(2,1)S(1)} %collective-permute-done.3.theirs_ref, bf16[512,2048]{1,0:T(8,128)(2,1)S(1)} %bitcast.22, bf16[512,2048]{1,0:T(8,128)(2,1)} %collective-permute-done.4.w_theirs), custom_call_target="tpu_custom_call" | custom-call | flops 536870912 | bytes 4194304 | tf_op jit(solution)/shard_map/out_project/pallas_call | solution.py:197
  48.5 33.6 %pages_out.1 = (bf16[64,1024]{1,0:T(8,128)(2,1)}, bf16[64,1024]{1,0:T(8,128)(2,1)}, bf16[64,1024]{1,0:T(8,128)(2,1)}, bf16[64,1024]{1,0:T(8,128)(2,1)}, bf16[64,...) custom-call(s32[8]{0:T(128)} %fusion.4.place_ref, ...), custom_call_target="tpu_custom_call" | custom-call | bytes 2097152 | tf_op jit(solution)/shard_map/pages_out/pallas_call | solution.py:105
  91.4 3.5 %collective-permute-start.25 = (bf16[64,1024]{1,0:T(8,128)(2,1)}, bf16[64,1024]{1,0:T(8,128)(2,1)}, u32[]{:S(2)}, u32[]{:S(2)}) collective-permute-start(bf16[64,1024]{1,0:T(8,128)(2,1)} %get-tuple-element.64), channel_id=1, source_target_pairs={{0,6},{1,7},{2,4},{3,5},{4,2},{5,3},{6,0},{7,1},{8,14},{9,15},{10,... | collective-permute-start | bytes 393224 | tf_op jit(solution)/shard_map/ppermute | solution.py:25
  95.0 3.0 %collective-permute-start.26 = (bf16[64,1024]{1,0:T(8,128)(2,1)}, bf16[64,1024]{1,0:T(8,128)(2,1)}, u32[]{:S(2)}, u32[]{:S(2)}) collective-permute-start(bf16[64,1024]{1,0:T(8,128)(2,1)} %get-tuple-element.65), channel_id=1, source_target_pairs={{0,7},{1,6},{2,5},{3,4},{4,3},{5,2},{6,1},{7,0},{8,15},{9,14},{10,... | collective-permute-start | bytes 393224 | tf_op jit(solution)/shard_map/ppermute | solution.py:25
  98.6 11.1 %collective-permute-done.24.refs_5_ = bf16[64,1024]{1,0:T(8,128)(2,1)} collective-permute-done((bf16[64,1024]{1,0:T(8,128)(2,1)}, bf16[64,1024]{1,0:T(8,128)(2,1)}, u32[]{:S(2)}, u32[]{:S(2)}) %collective-permute-start.24) | collective-permute-done | bytes 131104 | tf_op jit(solution)/shard_map/ppermute | solution.py:25
  109.7 33.6 %pages_in.1 = bf16[1,8,64,1024]{3,2,1,0:T(8,128)(2,1)} custom-call(s32[8]{0:T(128)} %copy-done.11, bf16[64,1024]{1,0:T(8,128)(2,1)} %get-tuple-element.58.refs_0_, bf16[64,1024]{1,0:T(8,128)(2,1)} %copy-done.9, bf16[64,1024]{1,0:T(8,128)(2,1)} %collective-permute-done.21.refs_2_, bf16[64,1024]{1,0:T(8,128)(2,1)} %collective-permute-done.22.refs_3_, ...), custom_call_target="tpu_custom_call" | custom-call | bytes 2097152 | tf_op jit(solution)/shard_map/pages_in/pallas_call | solution.py:131
  143.3 3.2 %out_project.2.mixed_ref = f32[128,2048]{1,0:T(8,128)S(1)} custom-call(bf16[256,512]{1,0:T(8,128)(2,1)S(1)} %get-tuple-element.38.mine_ref, bf16[256,512]{1,0:T(8,128)(2,1)S(1)} %collective-permute-done.3.theirs_ref, bf16[512,2048]{1,0:T(8,128)(2,1)S(1)} %bitcast.23, bf16[512,2048]{1,0:T(8,128)(2,1)} %collective-permute-done.4.w_theirs), custom_call_target="tpu_custom_call" | custom-call | flops 536870912 | bytes 4194304 | tf_op jit(solution)/shard_map/out_project/pallas_call | solution.py:197
  149.2 2.7 %collective-permute-start.16 = (bf16[48,2048]{1,0:T(8,128)(2,1)S(1)}, bf16[48,2048]{1,0:T(8,128)(2,1)S(1)}, u32[]{:S(2)}, u32[]{:S(2)}) collective-permute-start(bf16[48,2048]{1,0:T(8,128)(2,1)S(1)} %get-tuple-element.54), channel_id=1, source_target_pairs={{0,6},{1,7},{2,4},{3,5},{4,2},{5,3},{6,0},{7,1},{8,14},{9,15},{10,... | collective-permute-start | bytes 589832 | tf_op jit(solution)/shard_map/ppermute | solution.py:25
  154.5 3.6 %collective-permute-start.7 = (bf16[48,2048]{1,0:T(8,128)(2,1)}, bf16[48,2048]{1,0:T(8,128)(2,1)S(1)}, u32[]{:S(2)}, u32[]{:S(2)}) collective-permute-start(bf16[48,2048]{1,0:T(8,128)(2,1)} %get-tuple-element.44), channel_id=1, source_target_pairs={{0,2},{1,3},{2,0},{3,1},{4,6},{5,7},{6,4},{7,5},{8,10},{9,11},{10,... | collective-permute-start | bytes 589832 | tf_op jit(solution)/shard_map/ppermute | solution.py:25
  158.7 3.8 %collective-permute-done.6.refs_1_ = bf16[48,2048]{1,0:T(8,128)(2,1)S(1)} collective-permute-done((bf16[48,2048]{1,0:T(8,128)(2,1)}, bf16[48,2048]{1,0:T(8,128)(2,1)S(1)}, u32[]{:S(2)}, u32[]{:S(2)}) %collective-permute-start.6) | collective-permute-done | bytes 196640 | tf_op jit(solution)/shard_map/ppermute | solution.py:25
  172.3 6.6 %expert.3 = (bf16[48,2048]{1,0:T(8,128)(2,1)S(1)}, bf16[48,2048]{1,0:T(8,128)(2,1)S(1)}, bf16[48,2048]{1,0:T(8,128)(2,1)S(1)}, bf16[48,2048]{1,0:T(8,128)(2,1)S(1)}) custom-call(bf16[48,2048]{1,0:T(8,128)(2,1)S(1)} %get-tuple-element.42.refs_0_, bf16[48,2048]{1,0:T(8,128)(2,1)S(1)} %collective-permute-done.6.refs_1_, ...), custom_call_target="tpu_custom_call" | custom-call | flops 2415919104 | bytes 12582912 | tf_op jit(solution)/shard_map/expert/pallas_call | solution.py:271
  179.0 3.2 %collective-permute-start.10 = (bf16[48,2048]{1,0:T(8,128)(2,1)S(1)}, bf16[48,2048]{1,0:T(8,128)(2,1)S(1)}, u32[]{:S(2)}, u32[]{:S(2)}) collective-permute-start(bf16[48,2048]{1,0:T(8,128)(2,1)S(1)} %get-tuple-element.48), channel_id=1, source_target_pairs={{0,2},{1,3},{2,0},{3,1},{4,6},{5,7},{6,4},{7,5},{8,10},{9,11},{10,... | collective-permute-start | bytes 589832 | tf_op jit(solution)/shard_map/ppermute | solution.py:25
  183.3 5.8 %expert.5 = (bf16[48,2048]{1,0:T(8,128)(2,1)S(1)}, bf16[48,2048]{1,0:T(8,128)(2,1)S(1)}) custom-call(bf16[48,2048]{1,0:T(8,128)(2,1)S(1)} %collective-permute-done.16.refs_0_, bf16[48,2048]{1,0:T(8,128)(2,1)S(1)} %collective-permute-done.17.refs_1_, bf16[1,2048,2048]{2,1,0:T(8,128)(2,1)} %refs_3_.3, bf16[1,2048,2048]{2,1,0:T(8,128)(2,1)} %refs_3_.3, ...), custom_call_target="tpu_custom_call" | custom-call | flops 1207959552 | bytes 12582912 | tf_op jit(solution)/shard_map/expert/pallas_call | solution.py:271
  190.1 2.8 %collective-permute-start.19 = (bf16[48,2048]{1,0:T(8,128)(2,1)S(1)}, bf16[48,2048]{1,0:T(8,128)(2,1)S(1)}, u32[]{:S(2)}, u32[]{:S(2)}) collective-permute-start(bf16[48,2048]{1,0:T(8,128)(2,1)S(1)} %get-tuple-element.57), channel_id=1, source_target_pairs={{0,7},{1,6},{2,5},{3,4},{4,3},{5,2},{6,1},{7,0},{8,15},{9,14},{10,... | collective-permute-start | bytes 589832 | tf_op jit(solution)/shard_map/ppermute | solution.py:25
  192.9 5.8 %expert.4 = (bf16[48,2048]{1,0:T(8,128)(2,1)S(1)}, bf16[48,2048]{1,0:T(8,128)(2,1)S(1)}) custom-call(bf16[48,2048]{1,0:T(8,128)(2,1)S(1)} %collective-permute-done.12.refs_0_, bf16[48,2048]{1,0:T(8,128)(2,1)S(1)} %collective-permute-done.13.refs_1_, bf16[1,2048,2048]{2,1,0:T(8,128)(2,1)} %refs_3_.3, bf16[1,2048,2048]{2,1,0:T(8,128)(2,1)} %refs_3_.3, ...), custom_call_target="tpu_custom_call" | custom-call | flops 1207959552 | bytes 12582912 | tf_op jit(solution)/shard_map/expert/pallas_call | solution.py:271
  198.9 3.9 %collective-permute-start.15 = (bf16[48,2048]{1,0:T(8,128)(2,1)S(1)}, bf16[48,2048]{1,0:T(8,128)(2,1)S(1)}, u32[]{:S(2)}, u32[]{:S(2)}) collective-permute-start(bf16[48,2048]{1,0:T(8,128)(2,1)S(1)} %get-tuple-element.53), channel_id=1, source_target_pairs={{0,5},{1,4},{2,7},{3,6},{4,1},{5,0},{6,3},{7,2},{8,13},{9,12},{10,... | collective-permute-start | bytes 589832 | tf_op jit(solution)/shard_map/ppermute | solution.py:25
  205.0 5.0 %collective-permute-done.9.refs_1_ = bf16[48,2048]{1,0:T(8,128)(2,1)S(1)} collective-permute-done((bf16[48,2048]{1,0:T(8,128)(2,1)S(1)}, bf16[48,2048]{1,0:T(8,128)(2,1)S(1)}, u32[]{:S(2)}, u32[]{:S(2)}) %collective-permute-start.9) | collective-permute-done | bytes 196640 | tf_op jit(solution)/shard_map/ppermute | solution.py:25
  210.2 10.4 %collective-permute-done.14.refs_0_ = bf16[48,2048]{1,0:T(8,128)(2,1)S(1)} collective-permute-done((bf16[48,2048]{1,0:T(8,128)(2,1)S(1)}, bf16[48,2048]{1,0:T(8,128)(2,1)S(1)}, u32[]{:S(2)}, u32[]{:S(2)}) %collective-permute-start.14) | collective-permute-done | bytes 196640 | tf_op jit(solution)/shard_map/ppermute | solution.py:25
  (103 shorter events, 43.7 us)
Async XLA Ops:
  0.6 40.5 %collective-permute-start.4 = (bf16[512,2048]{1,0:T(8,128)(2,1)}, bf16[512,2048]{1,0:T(8,128)(2,1)}, u32[]{:S(2)}, u32[]{:S(2)}) collective-permute-start(bf16[512,2048]{1,0:T(8,128)(2,1)} %bitcast.21), channel_id=1, source_target_pairs={{0,8},{8,0},{16,24},{24,16},{1,9},{9,1},{17,25},{25,17},{2,10},{10... | collective-permute-start | bytes 6291464 | tf_op jit(solution)/shard_map/ppermute | solution.py:25
  1.2 15.3 %collective-permute-start.1 = (bf16[128,2048]{1,0:T(8,128)(2,1)}, bf16[128,2048]{1,0:T(8,128)(2,1)S(1)}, u32[]{:S(2)}, u32[]{:S(2)}) collective-permute-start(bf16[128,2048]{1,0:T(8,128)(2,1)} %bitcast.24), channel_id=1, source_target_pairs={{0,16},{8,24},{16,0},{24,8},{1,17},{9,25},{17,1},{25,9},{2,18},{10... | collective-permute-start | bytes 1572872 | tf_op jit(solution)/shard_map/ppermute | solution.py:25
  3.7 20.0 %collective-permute-start = (bf16[128,2048]{1,0:T(8,128)(2,1)}, bf16[128,2048]{1,0:T(8,128)(2,1)S(1)}, u32[]{:S(2)}, u32[]{:S(2)}) collective-permute-start(bf16[128,2048]{1,0:T(8,128)(2,1)} %bitcast.25), channel_id=1, source_target_pairs={{0,8},{8,0},{16,24},{24,16},{1,9},{9,1},{17,25},{25,17},{2,10},{10... | collective-permute-start | bytes 1572872 | tf_op jit(solution)/shard_map/ppermute | solution.py:25
  16.5 14.1 %collective-permute-start.2 = (bf16[128,2048]{1,0:T(8,128)(2,1)S(1)}, bf16[128,2048]{1,0:T(8,128)(2,1)}, u32[]{:S(2)}, u32[]{:S(2)}) collective-permute-start(bf16[128,2048]{1,0:T(8,128)(2,1)S(1)} %collective-permute-done.1.a_ref), channel_id=1, source_target_pairs={{0,8},{8,0},{16,24},{24,16},{1,9},{9,1},{17,25},{25,17},{2,10},{10... | collective-permute-start | bytes 1572872 | tf_op jit(solution)/shard_map/ppermute | solution.py:25
  45.3 101.3 %collective-permute-start.5 = (bf16[128,2048]{1,0:T(8,128)(2,1)}, bf16[128,2048]{1,0:T(8,128)(2,1)}, u32[]{:S(2)}, u32[]{:S(2)}) collective-permute-start(bf16[128,2048]{1,0:T(8,128)(2,1)} %out_project.3), channel_id=1, source_target_pairs={{0,16},{8,24},{16,0},{24,8},{1,17},{9,25},{17,1},{25,9},{2,18},{10... | collective-permute-start | bytes 1572872 | tf_op jit(solution)/shard_map/ppermute | solution.py:25
  82.1 7.9 %collective-permute-start.20 = (bf16[64,1024]{1,0:T(8,128)(2,1)}, bf16[64,1024]{1,0:T(8,128)(2,1)S(1)}, u32[]{:S(2)}, u32[]{:S(2)}) collective-permute-start(bf16[64,1024]{1,0:T(8,128)(2,1)} %get-tuple-element.59), channel_id=1, source_target_pairs={{0,1},{1,0},{2,3},{3,2},{4,5},{5,4},{6,7},{7,6},{8,9},{9,8},{10,11... | collective-permute-start | bytes 393224 | tf_op jit(solution)/shard_map/ppermute | solution.py:25
  85.3 9.7 %collective-permute-start.22 = (bf16[64,1024]{1,0:T(8,128)(2,1)}, bf16[64,1024]{1,0:T(8,128)(2,1)}, u32[]{:S(2)}, u32[]{:S(2)}) collective-permute-start(bf16[64,1024]{1,0:T(8,128)(2,1)} %get-tuple-element.61), channel_id=1, source_target_pairs={{0,3},{1,2},{2,1},{3,0},{4,7},{5,6},{6,5},{7,4},{8,11},{9,10},{10,... | collective-permute-start | bytes 393224 | tf_op jit(solution)/shard_map/ppermute | solution.py:25
  87.5 11.2 %collective-permute-start.23 = (bf16[64,1024]{1,0:T(8,128)(2,1)}, bf16[64,1024]{1,0:T(8,128)(2,1)}, u32[]{:S(2)}, u32[]{:S(2)}) collective-permute-start(bf16[64,1024]{1,0:T(8,128)(2,1)} %get-tuple-element.62), channel_id=1, source_target_pairs={{0,4},{1,5},{2,6},{3,7},{4,0},{5,1},{6,2},{7,3},{8,12},{9,13},{10,... | collective-permute-start | bytes 393224 | tf_op jit(solution)/shard_map/ppermute | solution.py:25
  90.1 19.7 %collective-permute-start.24 = (bf16[64,1024]{1,0:T(8,128)(2,1)}, bf16[64,1024]{1,0:T(8,128)(2,1)}, u32[]{:S(2)}, u32[]{:S(2)}) collective-permute-start(bf16[64,1024]{1,0:T(8,128)(2,1)} %get-tuple-element.63), channel_id=1, source_target_pairs={{0,5},{1,4},{2,7},{3,6},{4,1},{5,0},{6,3},{7,2},{8,13},{9,12},{10,... | collective-permute-start | bytes 393224 | tf_op jit(solution)/shard_map/ppermute | solution.py:25
  91.4 18.3 %collective-permute-start.25 = (bf16[64,1024]{1,0:T(8,128)(2,1)}, bf16[64,1024]{1,0:T(8,128)(2,1)}, u32[]{:S(2)}, u32[]{:S(2)}) collective-permute-start(bf16[64,1024]{1,0:T(8,128)(2,1)} %get-tuple-element.64), channel_id=1, source_target_pairs={{0,6},{1,7},{2,4},{3,5},{4,2},{5,3},{6,0},{7,1},{8,14},{9,15},{10,... | collective-permute-start | bytes 393224 | tf_op jit(solution)/shard_map/ppermute | solution.py:25
  95.0 14.8 %collective-permute-start.26 = (bf16[64,1024]{1,0:T(8,128)(2,1)}, bf16[64,1024]{1,0:T(8,128)(2,1)}, u32[]{:S(2)}, u32[]{:S(2)}) collective-permute-start(bf16[64,1024]{1,0:T(8,128)(2,1)} %get-tuple-element.65), channel_id=1, source_target_pairs={{0,7},{1,6},{2,5},{3,4},{4,3},{5,2},{6,1},{7,0},{8,15},{9,14},{10,... | collective-permute-start | bytes 393224 | tf_op jit(solution)/shard_map/ppermute | solution.py:25
  149.2 32.9 %collective-permute-start.16 = (bf16[48,2048]{1,0:T(8,128)(2,1)S(1)}, bf16[48,2048]{1,0:T(8,128)(2,1)S(1)}, u32[]{:S(2)}, u32[]{:S(2)}) collective-permute-start(bf16[48,2048]{1,0:T(8,128)(2,1)S(1)} %get-tuple-element.54), channel_id=1, source_target_pairs={{0,6},{1,7},{2,4},{3,5},{4,2},{5,3},{6,0},{7,1},{8,14},{9,15},{10,... | collective-permute-start | bytes 589832 | tf_op jit(solution)/shard_map/ppermute | solution.py:25
  151.8 31.4 %collective-permute-start.17 = (bf16[48,2048]{1,0:T(8,128)(2,1)S(1)}, bf16[48,2048]{1,0:T(8,128)(2,1)S(1)}, u32[]{:S(2)}, u32[]{:S(2)}) collective-permute-start(bf16[48,2048]{1,0:T(8,128)(2,1)S(1)} %get-tuple-element.55), channel_id=1, source_target_pairs={{0,7},{1,6},{2,5},{3,4},{4,3},{5,2},{6,1},{7,0},{8,15},{9,14},{10,... | collective-permute-start | bytes 589832 | tf_op jit(solution)/shard_map/ppermute | solution.py:25
  152.5 10.0 %collective-permute-start.6 = (bf16[48,2048]{1,0:T(8,128)(2,1)}, bf16[48,2048]{1,0:T(8,128)(2,1)S(1)}, u32[]{:S(2)}, u32[]{:S(2)}) collective-permute-start(bf16[48,2048]{1,0:T(8,128)(2,1)} %get-tuple-element.43), channel_id=1, source_target_pairs={{0,1},{1,0},{2,3},{3,2},{4,5},{5,4},{6,7},{7,6},{8,9},{9,8},{10,11... | collective-permute-start | bytes 589832 | tf_op jit(solution)/shard_map/ppermute | solution.py:25
  154.5 11.3 %collective-permute-start.7 = (bf16[48,2048]{1,0:T(8,128)(2,1)}, bf16[48,2048]{1,0:T(8,128)(2,1)S(1)}, u32[]{:S(2)}, u32[]{:S(2)}) collective-permute-start(bf16[48,2048]{1,0:T(8,128)(2,1)} %get-tuple-element.44), channel_id=1, source_target_pairs={{0,2},{1,3},{2,0},{3,1},{4,6},{5,7},{6,4},{7,5},{8,10},{9,11},{10,... | collective-permute-start | bytes 589832 | tf_op jit(solution)/shard_map/ppermute | solution.py:25
  158.1 12.0 %collective-permute-start.8 = (bf16[48,2048]{1,0:T(8,128)(2,1)S(1)}, bf16[48,2048]{1,0:T(8,128)(2,1)S(1)}, u32[]{:S(2)}, u32[]{:S(2)}) collective-permute-start(bf16[48,2048]{1,0:T(8,128)(2,1)S(1)} %get-tuple-element.45), channel_id=1, source_target_pairs={{0,3},{1,2},{2,1},{3,0},{4,7},{5,6},{6,5},{7,4},{8,11},{9,10},{10,... | collective-permute-start | bytes 589832 | tf_op jit(solution)/shard_map/ppermute | solution.py:25
  162.5 27.6 %collective-permute-start.12 = (bf16[48,2048]{1,0:T(8,128)(2,1)S(1)}, bf16[48,2048]{1,0:T(8,128)(2,1)S(1)}, u32[]{:S(2)}, u32[]{:S(2)}) collective-permute-start(bf16[48,2048]{1,0:T(8,128)(2,1)S(1)} %get-tuple-element.50), channel_id=1, source_target_pairs={{0,4},{1,5},{2,6},{3,7},{4,0},{5,1},{6,2},{7,3},{8,12},{9,13},{10,... | collective-permute-start | bytes 589832 | tf_op jit(solution)/shard_map/ppermute | solution.py:25
  165.8 27.2 %collective-permute-start.13 = (bf16[48,2048]{1,0:T(8,128)(2,1)S(1)}, bf16[48,2048]{1,0:T(8,128)(2,1)S(1)}, u32[]{:S(2)}, u32[]{:S(2)}) collective-permute-start(bf16[48,2048]{1,0:T(8,128)(2,1)S(1)} %get-tuple-element.51), channel_id=1, source_target_pairs={{0,5},{1,4},{2,7},{3,6},{4,1},{5,0},{6,3},{7,2},{8,13},{9,12},{10,... | collective-permute-start | bytes 589832 | tf_op jit(solution)/shard_map/ppermute | solution.py:25
  179.0 19.9 %collective-permute-start.10 = (bf16[48,2048]{1,0:T(8,128)(2,1)S(1)}, bf16[48,2048]{1,0:T(8,128)(2,1)S(1)}, u32[]{:S(2)}, u32[]{:S(2)}) collective-permute-start(bf16[48,2048]{1,0:T(8,128)(2,1)S(1)} %get-tuple-element.48), channel_id=1, source_target_pairs={{0,2},{1,3},{2,0},{3,1},{4,6},{5,7},{6,4},{7,5},{8,10},{9,11},{10,... | collective-permute-start | bytes 589832 | tf_op jit(solution)/shard_map/ppermute | solution.py:25
  182.1 21.0 %collective-permute-start.11 = (bf16[48,2048]{1,0:T(8,128)(2,1)S(1)}, bf16[48,2048]{1,0:T(8,128)(2,1)S(1)}, u32[]{:S(2)}, u32[]{:S(2)}) collective-permute-start(bf16[48,2048]{1,0:T(8,128)(2,1)S(1)} %get-tuple-element.49), channel_id=1, source_target_pairs={{0,3},{1,2},{2,1},{3,0},{4,7},{5,6},{6,5},{7,4},{8,11},{9,10},{10,... | collective-permute-start | bytes 589832 | tf_op jit(solution)/shard_map/ppermute | solution.py:25
  189.1 34.2 %collective-permute-start.18 = (bf16[48,2048]{1,0:T(8,128)(2,1)S(1)}, bf16[48,2048]{1,0:T(8,128)(2,1)S(1)}, u32[]{:S(2)}, u32[]{:S(2)}) collective-permute-start(bf16[48,2048]{1,0:T(8,128)(2,1)S(1)} %get-tuple-element.56), channel_id=1, source_target_pairs={{0,6},{1,7},{2,4},{3,5},{4,2},{5,3},{6,0},{7,1},{8,14},{9,15},{10,... | collective-permute-start | bytes 589832 | tf_op jit(solution)/shard_map/ppermute | solution.py:25
  190.1 33.2 %collective-permute-start.19 = (bf16[48,2048]{1,0:T(8,128)(2,1)S(1)}, bf16[48,2048]{1,0:T(8,128)(2,1)S(1)}, u32[]{:S(2)}, u32[]{:S(2)}) collective-permute-start(bf16[48,2048]{1,0:T(8,128)(2,1)S(1)} %get-tuple-element.57), channel_id=1, source_target_pairs={{0,7},{1,6},{2,5},{3,4},{4,3},{5,2},{6,1},{7,0},{8,15},{9,14},{10,... | collective-permute-start | bytes 589832 | tf_op jit(solution)/shard_map/ppermute | solution.py:25
  198.8 21.9 %collective-permute-start.14 = (bf16[48,2048]{1,0:T(8,128)(2,1)S(1)}, bf16[48,2048]{1,0:T(8,128)(2,1)S(1)}, u32[]{:S(2)}, u32[]{:S(2)}) collective-permute-start(bf16[48,2048]{1,0:T(8,128)(2,1)S(1)} %get-tuple-element.52), channel_id=1, source_target_pairs={{0,4},{1,5},{2,6},{3,7},{4,0},{5,1},{6,2},{7,3},{8,12},{9,13},{10,... | collective-permute-start | bytes 589832 | tf_op jit(solution)/shard_map/ppermute | solution.py:25
  198.9 24.1 %collective-permute-start.15 = (bf16[48,2048]{1,0:T(8,128)(2,1)S(1)}, bf16[48,2048]{1,0:T(8,128)(2,1)S(1)}, u32[]{:S(2)}, u32[]{:S(2)}) collective-permute-start(bf16[48,2048]{1,0:T(8,128)(2,1)S(1)} %get-tuple-element.53), channel_id=1, source_target_pairs={{0,5},{1,4},{2,7},{3,6},{4,1},{5,0},{6,3},{7,2},{8,13},{9,12},{10,... | collective-permute-start | bytes 589832 | tf_op jit(solution)/shard_map/ppermute | solution.py:25
  (17 other events, 289.7 us)

commit v3 on v0

v3 whole, which is shorter than its diff:
```python
import functools
import math

import jax
import jax.numpy as jnp
from jax import lax
from jax.experimental import pallas as pl
from jax.experimental.pallas import tpu as pltpu
from jax.sharding import PartitionSpec as P

EPS = 1e-06
F32 = jnp.float32
BF16 = jnp.bfloat16
VMEM_SPEC = pl.BlockSpec(memory_space=pltpu.VMEM)
SMEM_SPEC = pl.BlockSpec(memory_space=pltpu.SMEM)


def rms_norm(value, gain):
    wide = value.astype(F32)
    scale = lax.rsqrt(jnp.mean(wide * wide, axis=-1, keepdims=True) + EPS)
    return (wide * scale * gain.astype(F32)).astype(BF16)


def swap(value, axis, step):
    size = lax.axis_size(axis)
    return lax.ppermute(value, axis, [(i, i ^ step) for i in range(size)])


def held(value):
    return pltpu.with_memory_space_constraint(value, pltpu.VMEM)


def array(shape, dtype=BF16):
    return jax.ShapeDtypeStruct(shape, dtype)


def call(kernel, name, out_shape, args, mib, flops, scratch=(), scalars=0):
    outs = out_shape if isinstance(out_shape, tuple) else (out_shape,)
    moved = sum(a.size * a.dtype.itemsize for a in (*args, *outs))
    return pl.pallas_call(
        kernel,
        out_shape=out_shape,
        in_specs=[SMEM_SPEC] * scalars + [VMEM_SPEC] * (len(args) - scalars),
        scratch_shapes=scratch,
        compiler_params=pltpu.CompilerParams(vmem_limit_bytes=mib << 20),
        cost_estimate=pl.CostEstimate(flops=flops, bytes_accessed=moved, transcendentals=0),
        name=name,
    )(*args)


def plan_kernel(routes_ref, pick_ref, *, count):
    top, rows = routes_ref.shape
    capacity = pick_ref.shape[0] // count
    expert = lax.axis_index("blk") ^ lax.broadcasted_iota(jnp.int32, (count, rows), 0)
    chosen = jnp.zeros((count, rows), F32)
    for t in range(top):
        chosen = jnp.maximum(chosen, jnp.where(routes_ref[t : t + 1] == expert, F32(1), F32(0)))
    before = lax.broadcasted_iota(jnp.int32, (rows, rows), 0)
    after = lax.broadcasted_iota(jnp.int32, (rows, rows), 1)
    upto = jnp.where(before <= after, F32(1), F32(0)).astype(BF16)
    rank = jnp.dot(chosen.astype(BF16), upto, preferred_element_type=F32) - 1
    slot = jnp.where(chosen > 0, rank, F32(-1))
    place = lax.broadcasted_iota(jnp.int32, (capacity, rows), 0).astype(F32)
    for s in range(count):
        hit = jnp.where(slot[s : s + 1] == place, F32(1), F32(0))
        pick_ref[s * capacity : (s + 1) * capacity] = hit.astype(BF16)


def plan(routes, count):
    top, rows = routes.shape
    capacity = rows * 3 // 8
    return call(
        functools.partial(plan_kernel, count=count),
        "plan",
        array((count * capacity, rows)),
        (routes,),
        4,
        2 * count * rows * rows,
    )


def project_rows(a_ref, b_ref, gain_ref, w_ref, q_ref, kv_ref, normed, head_dim):
    rows = a_ref.shape[0]
    normed[:rows] = rms_norm(a_ref[...], gain_ref[0:1])
    normed[rows:] = rms_norm(b_ref[...], gain_ref[0:1])
    for h in range(q_ref.shape[1] // head_dim):
        columns = slice(3 * h * head_dim, 3 * (h + 1) * head_dim)
        out = jnp.dot(normed[...], w_ref[:, columns], preferred_element_type=F32).astype(BF16)
        q_ref[:, h * head_dim : (h + 1) * head_dim] = out[:, :head_dim]
        kv_ref[:, 2 * h * head_dim : 2 * (h + 1) * head_dim] = out[:, head_dim:]


def project_kernel(a_ref, b_ref, gain_ref, w_ref, q_ref, kv_ref, normed, *, head_dim):
    project_rows(a_ref, b_ref, gain_ref, w_ref, q_ref, kv_ref, normed, head_dim)


def project(a, b, gains, w_flat, heads, head_dim):
    rows, width = a.shape
    return call(
        functools.partial(project_kernel, head_dim=head_dim),
        "project",
        (array((2 * rows, heads * head_dim)), array((2 * rows, heads * 2 * head_dim))),
        (a, b, gains, w_flat),
        12,
        4 * rows * w_flat.size,
        [pltpu.VMEM((2 * rows, width), BF16)],
    )


def attend_kernel(
    seg_ref,
    q_near,
    kv_near,
    a_ref,
    b_ref,
    gain_ref,
    w_ref,
    keep_ref,
    send_ref,
    q_far,
    kv_far,
    normed,
    bias,
    *,
    head_dim,
):
    project_rows(a_ref, b_ref, gain_ref, w_ref, q_far, kv_far, normed, head_dim)
    block = a_ref.shape[0]
    half = 2 * block
    me = lax.axis_index("seq")
    row = jnp.concatenate(
        [
            seg_ref[:, pl.ds(pl.multiple_of((me ^ k) * block, block), block)]
            for k in range(seg_ref.shape[1] // block)
        ],
        axis=1,
    ).astype(F32)
    column = jnp.broadcast_to(row, (8, row.shape[1])).T[:, 0:1]
    bias[...] = jnp.where(column == row, F32(0), F32(-1e30))
    factor = math.log2(math.e) / math.sqrt(head_dim)
    for h in range(q_near.shape[1] // head_dim):
        q_cols = slice(h * head_dim, (h + 1) * head_dim)
        k_cols = slice(2 * h * head_dim, (2 * h + 1) * head_dim)
        v_cols = slice((2 * h + 1) * head_dim, (2 * h + 2) * head_dim)
        key = jnp.concatenate([kv_near[:, k_cols], kv_far[:, k_cols]], axis=0)
        value = jnp.concatenate([kv_near[:, v_cols], kv_far[:, v_cols]], axis=0)
        for part, q_ref in enumerate((q_near, q_far)):
            scores = lax.dot_general(
                q_ref[:, q_cols], key, (((1,), (1,)), ((), ())), preferred_element_type=F32
            )
            scores = scores + bias[part * half : (part + 1) * half]
            top = jnp.max(scores, axis=-1, keepdims=True)
            weights = jnp.exp2((scores - top) * factor)
            total = jnp.sum(weights, axis=-1, keepdims=True)
            context = jnp.dot(weights.astype(BF16), value, preferred_element_type=F32)
            context = (context / total).astype(BF16)
            rows = slice(part * block, (part + 1) * block)
            keep_ref[rows, q_cols] = context[:block]
            send_ref[rows, q_cols] = context[block:]


def attend(segments, q_near, kv_near, a, b, gains, w_flat, head_dim):
    group_len = segments.shape[1]
    half, cols = q_near.shape
    return call(
        functools.partial(attend_kernel, head_dim=head_dim),
        "attend",
        (array((half, cols)), array((half, cols))),
        (segments, q_near, kv_near, a, b, gains, w_flat),
        16,
        2 * half * w_flat.size + 4 * group_len * group_len * cols,
        [
            pltpu.VMEM((half, cols), BF16),
            pltpu.VMEM((half, 2 * cols), BF16),
            pltpu.VMEM((half, a.shape[1]), BF16),
            pltpu.VMEM((group_len, group_len), F32),
        ],
    )


def out_project_kernel(mine_ref, theirs_ref, w_mine, w_theirs, out_ref, *, which):
    rows = slice(which * out_ref.shape[0], (which + 1) * out_ref.shape[0])
    out = jnp.dot(mine_ref[rows], w_mine[...], preferred_element_type=F32)
    out = out + jnp.dot(theirs_ref[rows], w_theirs[...], preferred_element_type=F32)
    out_ref[...] = out.astype(out_ref.dtype)


def out_project(which, mine, theirs, w_mine, w_theirs, dtype):
    rows, depth = mine.shape[0] // 2, mine.shape[1]
    width = w_mine.shape[1]
    return call(
        functools.partial(out_project_kernel, which=which),
        "out_project",
        array((rows, width), dtype),
        (mine, theirs, w_mine, w_theirs),
        8,
        4 * rows * depth * width,
    )


def pages_out_kernel(owner_ref, *refs, count):
    blocks, outs, (rows, pages) = refs[:-count - 2], refs[-count - 2 : -2], refs[-2:]
    size = blocks[0].shape[0]
    page_len, share = outs[0].shape
    seq_me, blk_me = lax.axis_index("seq"), lax.axis_index("blk")
    columns = pl.ds(pl.multiple_of(seq_me * share, share), share)
    for k, block in enumerate(blocks):
        start = pl.multiple_of((seq_me ^ k) * size, size)
        rows[pl.ds(start, size)] = block[:, columns]
    for j in range(count):
        pages[owner_ref[0, j] ^ blk_me] = rows[j * page_len : (j + 1) * page_len]
    for s, out in enumerate(outs):
        out[...] = pages[s]


def pages_out(owners, blocks):
    count = owners.shape[1]
    group_len = len(blocks) * blocks[0].shape[0]
    page_len, share = group_len // count, blocks[0].shape[1] // len(blocks)
    return call(
        functools.partial(pages_out_kernel, count=count),
        "pages_out",
        (array((page_len, share)),) * count,
        (owners, *blocks),
        8,
        0,
        [pltpu.VMEM((group_len, share), BF16), pltpu.VMEM((count, page_len, share), BF16)],
        scalars=1,
    )


def pages_in_kernel(*refs):
    pages, out = refs[:-1], refs[-1]
    page_len = pages[0].shape[0]
    blk_me = lax.axis_index("blk")
    for s, page in enumerate(pages):
        out[pl.ds(pl.multiple_of((blk_me ^ s) * page_len, page_len), page_len)] = page[...]


def pages_in(pages):
    page_len, share = pages[0].shape
    return call(
        pages_in_kernel, "pages_in", array((len(pages) * page_len, share)), tuple(pages), 4, 0
    )


def cache_kernel(*refs, head_dim):
    *shares, gain_ref, w_ref, out_ref, rows = refs
    share = shares[0].shape[1]
    me = lax.axis_index("seq")
    for k, ref in enumerate(shares):
        rows[:, pl.ds(pl.multiple_of((me ^ k) * share, share), share)] = ref[...]
    rows[...] = rms_norm(rows[...], gain_ref[0:1])
    count, page_len = out_ref.shape[1:3]
    for h in range(out_ref.shape[3] // (2 * head_dim)):
        columns = slice((3 * h + 1) * head_dim, 3 * (h + 1) * head_dim)
        out = jnp.dot(rows[...], w_ref[:, columns], preferred_element_type=F32).astype(BF16)
        out = out.reshape(count, page_len, 2 * head_dim)
        out_ref[0, :, :, 2 * h * head_dim : 2 * (h + 1) * head_dim] = out


def cache(shares, gains, w_flat, count, heads, head_dim):
    group_len, share = shares[0].shape
    return call(
        functools.partial(cache_kernel, head_dim=head_dim),
        "cache",
        array((1, count, group_len // count, heads * 2 * head_dim)),
        (*shares, gains, w_flat),
        16,
        2 * group_len * w_flat.size,
        [pltpu.VMEM((group_len, share * len(shares)), BF16)],
    )


def dispatch_kernel(own_ref, mixed_ref, far_ref, gain_ref, pick_ref, resid_ref, ffn_ref, *outs):
    resid = own_ref[...].astype(F32) + mixed_ref[...] + far_ref[...].astype(F32)
    resid = resid.astype(BF16)
    resid_ref[...] = resid
    ffn_in = rms_norm(resid, gain_ref[1:2])
    ffn_ref[...] = ffn_in
    rows = outs[0].shape[0]
    picked = jnp.dot(pick_ref[...], ffn_in, preferred_element_type=F32).astype(BF16)
    for s, out in enumerate(outs):
        out[...] = picked[s * rows : (s + 1) * rows]


def dispatch(own, mixed, far, gains, pick, count):
    rows, width = own.shape
    capacity = pick.shape[0] // count
    return call(
        dispatch_kernel,
        "dispatch",
        (array((rows, width)),) * 2 + (array((capacity, width)),) * count,
        (own, mixed, far, gains, pick),
        max(12, pick.shape[0] * width * 12 >> 20),
        2 * pick.size * width,
    )


def weigh_kernel(ffn_ref, router_ref, pick_ref, *outs, capacity):
    logits = lax.dot_general(
        router_ref[...], ffn_ref[...], (((1,), (1,)), ((), ())), preferred_element_type=F32
    )
    gates = jax.nn.sigmoid(logits).astype(BF16)
    experts = gates.shape[0]
    step = lax.broadcasted_iota(jnp.int32, (experts, experts), 0)
    expert = lax.broadcasted_iota(jnp.int32, (experts, experts), 1)
    order = jnp.where(lax.axis_index("blk") ^ step == expert, F32(1), F32(0)).astype(BF16)
    gates = jnp.dot(order, gates, preferred_element_type=F32)
    start = 0
    for out in outs:
        parts = [
            pick_ref[s * capacity : (s + 1) * capacity].astype(F32) * gates[s : s + 1]
            for s in range(start, start + out.shape[1] // capacity)
        ]
        out[...] = jnp.concatenate(parts, axis=0).T.astype(BF16)
        start += out.shape[1] // capacity


def weigh(ffn_in, router, pick, groups):
    rows = ffn_in.shape[0]
    capacity = pick.shape[0] // router.shape[0]
    return call(
        functools.partial(weigh_kernel, capacity=capacity),
        "weigh",
        tuple(array((rows, len(group) * capacity)) for group in groups),
        (ffn_in, router, pick),
        8,
        2 * router.size * rows,
    )


def expert_kernel(*refs, count):
    ins, (in_ref, down_ref) = refs[:count], refs[count : count + 2]
    outs, (rows, hidden) = refs[count + 2 : 2 * count + 2], refs[2 * count + 2 :]
    size = ins[0].shape[0]
    ff, width = down_ref.shape
    for s, ref in enumerate(ins):
        rows[s * size : (s + 1) * size] = ref[...]
    tile = min(ff, 512)
    for start in range(0, ff, tile):
        gate = jnp.dot(rows[...], in_ref[:, start : start + tile], preferred_element_type=F32)
        up = jnp.dot(
            rows[...], in_ref[:, ff + start : ff + start + tile], preferred_element_type=F32
        )
        hidden[:, start : start + tile] = (jax.nn.silu(gate) * up).astype(BF16)
    for start in range(0, width, tile):
        part = jnp.dot(hidden[...], down_ref[:, start : start + tile], preferred_element_type=F32)
        for s, out in enumerate(outs):
            out[:, start : start + tile] = part[s * size : (s + 1) * size].astype(BF16)


def expert(blocks, gate_up, down):
    count = len(blocks)
    size, width = blocks[0].shape
    ff = down.shape[0]
    return call(
        functools.partial(expert_kernel, count=count),
        "expert",
        (array((size, width)),) * count,
        (*blocks, gate_up, down),
        max(8, count * size * 20480 >> 20),
        6 * count * size * width * ff,
        [
            pltpu.VMEM((count * size, width), BF16),
            pltpu.VMEM((count * size, ff), BF16),
        ],
    )


def combine_kernel(base_ref, weigh_ref, *refs):
    ins, out_ref, rows = refs[:-2], refs[-2], refs[-1]
    size = ins[0].shape[0]
    for s, ref in enumerate(ins):
        rows[s * size : (s + 1) * size] = ref[...]
    total = jnp.dot(weigh_ref[...], rows[...], preferred_element_type=F32)
    out_ref[...] = (base_ref[...].astype(F32) + total).astype(out_ref.dtype)


def combine(base, weights, blocks, dtype):
    size, width = blocks[0].shape
    return call(
        combine_kernel,
        "combine",
        array(base.shape, dtype),
        (base, weights, *blocks),
        8,
        2 * weights.size * width,
        [pltpu.VMEM((len(blocks) * size, width), BF16)],
    )


def on_device(
    residual_in,
    segment_ids,
    attn_gain,
    w_qkv,
    w_out,
    ffn_gain,
    w_router,
    routes,
    w_gate_up,
    w_down,
    page_owner,
):
    own = residual_in[0]
    width = own.shape[1]
    heads_here = w_qkv.shape[1]
    head_dim = w_out.shape[1]
    blk_count = lax.axis_size("blk")

    far = swap(own, "seq", 2)
    core = swap(own, "seq", 1)
    w_mine = w_out.reshape(heads_here * head_dim, width)
    w_theirs = swap(w_mine, "seq", 1)
    gains = jnp.stack([attn_gain, ffn_gain])
    pick = plan(routes[0].T, blk_count)

    w_flat = held(w_qkv.reshape(width, heads_here * 3 * head_dim))
    q_near, kv_near = project(own, core, gains, w_flat, heads_here, head_dim)
    far, q_near, kv_near = lax.optimization_barrier((far, q_near, kv_near))
    far_core = swap(far, "seq", 1)
    keep, send = attend(segment_ids, q_near, kv_near, far, far_core, gains, w_flat, head_dim)
    theirs = swap(send, "seq", 1)
    w_mine, w_theirs = held(w_mine), held(w_theirs)
    far_sum = out_project(1, keep, theirs, w_mine, w_theirs, BF16)
    from_far = swap(far_sum, "seq", 2)
    mixed = out_project(0, keep, theirs, w_mine, w_theirs, F32)

    outgoing = pages_out(page_owner, (own, core, far, far_core))
    arrived = [outgoing[0]] + [swap(outgoing[s], "blk", s) for s in range(1, blk_count)]
    share = pages_in(arrived)
    share_far, share_core = swap(share, "seq", 2), swap(share, "seq", 1)
    share_far_core = swap(share_far, "seq", 1)
    kv_cache = cache(
        (share, share_core, share_far, share_far_core),
        gains,
        w_flat,
        blk_count,
        heads_here,
        head_dim,
    )

    resid, ffn_in, *sent = dispatch(own, mixed, from_far, gains, pick, blk_count)
    half, quarter = blk_count // 2, blk_count // 4
    groups = [range(half), range(half, half + quarter), range(half + quarter, blk_count)]
    weights = weigh(ffn_in, w_router.T, pick, groups)
    gate_up, down = held(w_gate_up[0]), held(w_down[0])
    total = resid
    for number, group in enumerate(groups):
        blocks = [sent[s] if s == 0 else swap(sent[s], "blk", s) for s in group]
        outs = expert(blocks, gate_up, down)
        back = [out if s == 0 else swap(out, "blk", s) for s, out in zip(group, outs)]
        last = number == len(groups) - 1
        total = combine(total, weights[number], back, BF16 if last else F32)
    return (total[None], kv_cache)


def solution(mesh):
    in_specs = (
        P("blk", "seq", None),
        P("blk", None),
        P(),
        P(None, "seq", None),
        P("seq", None, None),
        P(),
        P(),
        P("blk", "seq", None),
        P("blk", None, None),
        P("blk", None, None),
        P("blk", None),
    )
    out_specs = (P("blk", "seq", None), P("blk", None, None, "seq"))
    return jax.shard_map(
        on_device, mesh=mesh, in_specs=in_specs, out_specs=out_specs, check_vma=False
    )
```

time: 315 us -> 127 us (0.40)
  waiting for transfers between devices: 140 us -> 44.9 us
  blocking collectives: 80.4 us -> 0 us
  starting transfers between devices: 0.16 us -> 51.3 us
  local copies, waits for them, and re-layouts: 36.5 us -> 5.44 us
  Pallas kernels: 0 us -> 24.3 us
  matrix products: 23.2 us -> 0 us
  other arithmetic: 20.4 us -> 0.03 us
  between operations: 14 us -> 0.85 us
    reduce_scatter x2 -> x0, waiting for transfers between devices: 79.5 us -> none  [the longest x1 48 us: on_device(): lax.psum_scatter(jnp.where(active.reshape(-1)[:, None], per_row.astype(jn...]
    all_gather x2 -> x0, waiting for transfers between devices: 60.5 us -> none  [the longest x1 42 us: on_device(): lax.all_gather(ffn_in, 'blk', axis=0, tiled=True)]
    all_to_all x1 -> x0, blocking collectives: 53.9 us -> none  [on_device(): lax.all_to_all(outgoing, 'blk', split_axis=0, concat_axis=0, tiled=True)]
    ppermute x0 -> x30, starting transfers between devices: none -> 51.3 us  [swap(): return lax.ppermute(value, axis, [(i, i ^ step) for i in range(size)])]
    ppermute x0 -> x30, waiting for transfers between devices: none -> 44.9 us  [swap(): return lax.ppermute(value, axis, [(i, i ^ step) for i in range(size)])]
    all_gather x1 -> x0, blocking collectives: 26.6 us -> none  [on_device(): lax.all_gather(dense_gate, 'blk', axis=0, tiled=True)]
    pallas_call x0 -> x16, Pallas kernels: none -> 24.3 us  [call(): pl.pallas_call(kernel, out_shape=out_shape, in_specs=[SMEM_SPEC] * scalar...]
    dot_general x6 -> x0, matrix products: 23.2 us -> none  [the longest x1 8.07 us: on_device(): jnp.dot(lax.all_gather(normed, 'seq', axis=0, tiled=True), w_flat, prefer...]
  transfers between devices with their start and end apart: 4 -> 30, of which waited for: 4 -> 15; matrix products, arithmetic and copies ran while one was open for 6% -> 4% of each run, Pallas kernels for 0% -> 18%
where the time goes in v3:
time: 127 us
  starting transfers between devices  51.3 us (40%)
  waiting for transfers between devices  44.9 us (35%)
  Pallas kernels  24.3 us (19%)
  local copies, waits for them, and re-layouts  5.44 us (4%)
    ppermute x30, starting transfers between devices, swap(): return lax.ppermute(value, axis, [(i, i ^ step) for i in range(size)])  51.3 us
    ppermute x30, waiting for transfers between devices, swap(): return lax.ppermute(value, axis, [(i, i ^ step) for i in range(size)])  44.9 us
    pallas_call x16, Pallas kernels, call(): pl.pallas_call(kernel, out_shape=out_shape, in_specs=[SMEM_SPEC] * scalar...  24.3 us
    unnamed x19, local copies, waits for them, and re-layouts  4.05 us
  transfers between devices with their start and end apart: 30, of which 15 were waited for; matrix products, arithmetic and copies ran while one was open for 4% of the time, Pallas kernels for 18%

profile of v3, /device:TPU:0, one launch (start us, length us, event | category | flops | bytes accessed | tf_op | source)
XLA Modules:
  0.0 126.8 jit_solution(18186914644516425429)
XLA Ops:
  1.2 2.9 %collective-permute-start = (bf16[128,2048]{1,0:T(8,128)(2,1)}, bf16[128,2048]{1,0:T(8,128)(2,1)S(1)}, u32[]{:S(2)}, u32[]{:S(2)}) collective-permute-start(bf16[128,2048]{1,0:T(8,128)(2,1)} %bitcast.26), channel_id=1, source_target_pairs={{0,16},{8,24},{16,0},{24,8},{1,17},{9,25},{17,1},{25,9},{2,18},{10... | collective-permute-start | bytes 1572872 | tf_op jit(solution)/shard_map/ppermute | solution.py:26
  5.5 4.0 %copy.13 = bf16[256,8,4,384]{3,1,2,0:T(8,128)(2,1)S(1)} copy(bf16[256,8,4,384]{3,2,1,0:T(4,128)(2,1)} %bitcast.32) | data formatting | bytes 12582912
  9.6 2.6 %project.1 = (bf16[256,512]{1,0:T(8,128)(2,1)S(1)}, bf16[256,1024]{1,0:T(8,128)(2,1)S(1)}) custom-call(bf16[128,2048]{1,0:T(8,128)(2,1)S(1)} %bitcast.27, bf16[128,2048]{1,0:T(8,128)(2,1)S(1)} %collective-permute-done.1.b_ref.refs_1_, bf16[2,2048]{1,0:T(2,128)(2,1)S(1)} %pad_maximum_fusion.gain_ref.refs_4_, bf16[2048,1536]{1,0:T(8,128)(2,1)S(1)} %bitcast.16), custom_call_target="tpu_custom_call" | custom-call | flops 1610612736 | bytes 8134656 | tf_op jit(solution)/shard_map/project/pallas_call | solution.py:40
  12.2 4.3 %collective-permute-done.a_ref.refs_2_ = bf16[128,2048]{1,0:T(8,128)(2,1)S(1)} collective-permute-done((bf16[128,2048]{1,0:T(8,128)(2,1)}, bf16[128,2048]{1,0:T(8,128)(2,1)S(1)}, u32[]{:S(2)}, u32[]{:S(2)}) %collective-permute-start) | collective-permute-done | bytes 524320 | tf_op jit(solution)/shard_map/ppermute | solution.py:26
  18.4 5.2 %attend.1 = (bf16[256,512]{1,0:T(8,128)(2,1)S(1)}, bf16[256,512]{1,0:T(8,128)(2,1)S(1)}) custom-call(s32[1,512]{1,0:T(1,128)S(1)} %copy-done.4, bf16[256,512]{1,0:T(8,128)(2,1)S(1)} %get-tuple-element.40.q_near, bf16[256,1024]{1,0:T(8,128)(2,1)S(1)} %get-tuple-element.41.kv_near, bf16[128,2048]{1,0:T(8,128)(2,1)S(1)} %collective-permute-done.a_ref.refs_2_, ...), custom_call_target="tpu_custom_call" | custom-call | flops 2147483648 | bytes 8660992 | tf_op jit(solution)/shard_map/attend/pallas_call | solution.py:40
  32.0 2.6 %collective-permute-start.23 = (bf16[64,512]{1,0:T(8,128)(2,1)S(1)}, bf16[64,512]{1,0:T(8,128)(2,1)S(1)}, u32[]{:S(2)}, u32[]{:S(2)}) collective-permute-start(bf16[64,512]{1,0:T(8,128)(2,1)S(1)} %get-tuple-element.70), channel_id=1, source_target_pairs={{0,4},{1,5},{2,6},{3,7},{4,0},{5,1},{6,2},{7,3},{8,12},{9,13},{10,... | collective-permute-start | bytes 196616 | tf_op jit(solution)/shard_map/ppermute | solution.py:26
  36.4 3.1 %collective-permute-start.25 = (bf16[64,512]{1,0:T(8,128)(2,1)S(1)}, bf16[64,512]{1,0:T(8,128)(2,1)S(1)}, u32[]{:S(2)}, u32[]{:S(2)}) collective-permute-start(bf16[64,512]{1,0:T(8,128)(2,1)S(1)} %get-tuple-element.72), channel_id=1, source_target_pairs={{0,6},{1,7},{2,4},{3,5},{4,2},{5,3},{6,0},{7,1},{8,14},{9,15},{10,... | collective-permute-start | bytes 196616 | tf_op jit(solution)/shard_map/ppermute | solution.py:26
  40.1 4.7 %collective-permute-done.24.refs_5_ = bf16[64,512]{1,0:T(8,128)(2,1)S(1)} collective-permute-done((bf16[64,512]{1,0:T(8,128)(2,1)S(1)}, bf16[64,512]{1,0:T(8,128)(2,1)S(1)}, u32[]{:S(2)}, u32[]{:S(2)}) %collective-permute-start.24) | collective-permute-done | bytes 65568 | tf_op jit(solution)/shard_map/ppermute | solution.py:26
  54.1 3.5 %collective-permute-done.28.refs_2_ = bf16[512,512]{1,0:T(8,128)(2,1)S(1)} collective-permute-done((bf16[512,512]{1,0:T(8,128)(2,1)S(1)}, bf16[512,512]{1,0:T(8,128)(2,1)S(1)}, u32[]{:S(2)}, u32[]{:S(2)}) %collective-permute-start.28) | collective-permute-done | bytes 524320 | tf_op jit(solution)/shard_map/ppermute | solution.py:26
  61.0 3.1 %collective-permute-start.12 = (bf16[48,2048]{1,0:T(8,128)(2,1)S(1)}, bf16[48,2048]{1,0:T(8,128)(2,1)S(1)}, u32[]{:S(2)}, u32[]{:S(2)}) collective-permute-start(bf16[48,2048]{1,0:T(8,128)(2,1)S(1)} %get-tuple-element.57), channel_id=1, source_target_pairs={{0,4},{1,5},{2,6},{3,7},{4,0},{5,1},{6,2},{7,3},{8,12},{9,13},{10,... | collective-permute-start | bytes 589832 | tf_op jit(solution)/shard_map/ppermute | solution.py:26
  64.1 2.8 %collective-permute-start.13 = (bf16[48,2048]{1,0:T(8,128)(2,1)S(1)}, bf16[48,2048]{1,0:T(8,128)(2,1)S(1)}, u32[]{:S(2)}, u32[]{:S(2)}) collective-permute-start(bf16[48,2048]{1,0:T(8,128)(2,1)S(1)} %get-tuple-element.58), channel_id=1, source_target_pairs={{0,5},{1,4},{2,7},{3,6},{4,1},{5,0},{6,3},{7,2},{8,13},{9,12},{10,... | collective-permute-start | bytes 589832 | tf_op jit(solution)/shard_map/ppermute | solution.py:26
  66.9 2.6 %expert.3 = (bf16[48,2048]{1,0:T(8,128)(2,1)S(1)}, bf16[48,2048]{1,0:T(8,128)(2,1)S(1)}, bf16[48,2048]{1,0:T(8,128)(2,1)S(1)}, bf16[48,2048]{1,0:T(8,128)(2,1)S(1)}) custom-call(bf16[48,2048]{1,0:T(8,128)(2,1)S(1)} %get-tuple-element.48.refs_0_, bf16[48,2048]{1,0:T(8,128)(2,1)S(1)} %collective-permute-done.6.refs_1_, ...), custom_call_target="tpu_custom_call" | custom-call | flops 2415919104 | bytes 14155776 | tf_op jit(solution)/shard_map/expert/pallas_call | solution.py:40
  69.7 12.8 %collective-permute-start.10 = (bf16[48,2048]{1,0:T(8,128)(2,1)S(1)}, bf16[48,2048]{1,0:T(8,128)(2,1)S(1)}, u32[]{:S(2)}, u32[]{:S(2)}) collective-permute-start(bf16[48,2048]{1,0:T(8,128)(2,1)S(1)} %get-tuple-element.54), channel_id=1, source_target_pairs={{0,2},{1,3},{2,0},{3,1},{4,6},{5,7},{6,4},{7,5},{8,10},{9,11},{10,... | collective-permute-start | bytes 589832 | tf_op jit(solution)/shard_map/ppermute | solution.py:26
  82.4 3.2 %collective-permute-done.12.refs_0_ = bf16[48,2048]{1,0:T(8,128)(2,1)S(1)} collective-permute-done((bf16[48,2048]{1,0:T(8,128)(2,1)S(1)}, bf16[48,2048]{1,0:T(8,128)(2,1)S(1)}, u32[]{:S(2)}, u32[]{:S(2)}) %collective-permute-start.12) | collective-permute-done | bytes 196640 | tf_op jit(solution)/shard_map/ppermute | solution.py:26
  85.7 2.2 %expert.5 = (bf16[48,2048]{1,0:T(8,128)(2,1)S(1)}, bf16[48,2048]{1,0:T(8,128)(2,1)S(1)}) custom-call(bf16[48,2048]{1,0:T(8,128)(2,1)S(1)} %collective-permute-done.16.refs_0_, bf16[48,2048]{1,0:T(8,128)(2,1)S(1)} %collective-permute-done.17.refs_1_, bf16[2048,2048]{1,0:T(8,128)(2,1)S(1)} %bitcast.14, bf16[1024,2048]{1,0:T(8,128)(2,1)S(1)} %bitcast.20), custom_call_target="tpu_custom_call" | custom-call | flops 1207959552 | bytes 13369344 | tf_op jit(solution)/shard_map/expert/pallas_call | solution.py:40
  87.8 2.4 %collective-permute-done.13.refs_1_ = bf16[48,2048]{1,0:T(8,128)(2,1)S(1)} collective-permute-done((bf16[48,2048]{1,0:T(8,128)(2,1)S(1)}, bf16[48,2048]{1,0:T(8,128)(2,1)S(1)}, u32[]{:S(2)}, u32[]{:S(2)}) %collective-permute-start.13) | collective-permute-done | bytes 196640 | tf_op jit(solution)/shard_map/ppermute | solution.py:26
  90.2 2.0 %collective-permute-start.18 = (bf16[48,2048]{1,0:T(8,128)(2,1)S(1)}, bf16[48,2048]{1,0:T(8,128)(2,1)S(1)}, u32[]{:S(2)}, u32[]{:S(2)}) collective-permute-start(bf16[48,2048]{1,0:T(8,128)(2,1)S(1)} %get-tuple-element.64), channel_id=1, source_target_pairs={{0,6},{1,7},{2,4},{3,5},{4,2},{5,3},{6,0},{7,1},{8,14},{9,15},{10,... | collective-permute-start | bytes 589832 | tf_op jit(solution)/shard_map/ppermute | solution.py:26
  92.2 2.2 %expert.4 = (bf16[48,2048]{1,0:T(8,128)(2,1)S(1)}, bf16[48,2048]{1,0:T(8,128)(2,1)S(1)}) custom-call(bf16[48,2048]{1,0:T(8,128)(2,1)S(1)} %collective-permute-done.12.refs_0_, bf16[48,2048]{1,0:T(8,128)(2,1)S(1)} %collective-permute-done.13.refs_1_, bf16[2048,2048]{1,0:T(8,128)(2,1)S(1)} %bitcast.15, bf16[1024,2048]{1,0:T(8,128)(2,1)S(1)} %bitcast.21), custom_call_target="tpu_custom_call" | custom-call | flops 1207959552 | bytes 13369344 | tf_op jit(solution)/shard_map/expert/pallas_call | solution.py:40
  94.4 2.0 %collective-permute-start.19 = (bf16[48,2048]{1,0:T(8,128)(2,1)S(1)}, bf16[48,2048]{1,0:T(8,128)(2,1)S(1)}, u32[]{:S(2)}, u32[]{:S(2)}) collective-permute-start(bf16[48,2048]{1,0:T(8,128)(2,1)S(1)} %get-tuple-element.65), channel_id=1, source_target_pairs={{0,7},{1,6},{2,5},{3,4},{4,3},{5,2},{6,1},{7,0},{8,15},{9,14},{10,... | collective-permute-start | bytes 589832 | tf_op jit(solution)/shard_map/ppermute | solution.py:26
  96.4 3.7 %collective-permute-start.15 = (bf16[48,2048]{1,0:T(8,128)(2,1)S(1)}, bf16[48,2048]{1,0:T(8,128)(2,1)S(1)}, u32[]{:S(2)}, u32[]{:S(2)}) collective-permute-start(bf16[48,2048]{1,0:T(8,128)(2,1)S(1)} %get-tuple-element.60), channel_id=1, source_target_pairs={{0,5},{1,4},{2,7},{3,6},{4,1},{5,0},{6,3},{7,2},{8,13},{9,12},{10,... | collective-permute-start | bytes 589832 | tf_op jit(solution)/shard_map/ppermute | solution.py:26
  100.1 6.9 %collective-permute-done.11.refs_3_ = bf16[48,2048]{1,0:T(8,128)(2,1)S(1)} collective-permute-done((bf16[48,2048]{1,0:T(8,128)(2,1)S(1)}, bf16[48,2048]{1,0:T(8,128)(2,1)S(1)}, u32[]{:S(2)}, u32[]{:S(2)}) %collective-permute-start.11) | collective-permute-done | bytes 196640 | tf_op jit(solution)/shard_map/ppermute | solution.py:26
  107.6 4.2 %cache.1 = bf16[1,8,64,1024]{3,2,1,0:T(8,128)(2,1)} custom-call(bf16[512,512]{1,0:T(8,128)(2,1)S(1)} %pages_in.1.refs_0_, bf16[512,512]{1,0:T(8,128)(2,1)S(1)} %collective-permute-done.27.refs_1_, bf16[512,512]{1,0:T(8,128)(2,1)S(1)} %collective-permute-done.28.refs_2_, bf16[512,512]{1,0:T(8,128)(2,1)S(1)} %collective-permute-done.29.refs_3_, ...), custom_call_target="tpu_custom_call" | custom-call | flops 3221225472 | bytes 9445376 | tf_op jit(solution)/shard_map/cache/pallas_call | solution.py:40
  114.1 8.9 %collective-permute-done.14.refs_0_ = bf16[48,2048]{1,0:T(8,128)(2,1)S(1)} collective-permute-done((bf16[48,2048]{1,0:T(8,128)(2,1)S(1)}, bf16[48,2048]{1,0:T(8,128)(2,1)S(1)}, u32[]{:S(2)}, u32[]{:S(2)}) %collective-permute-start.14) | collective-permute-done | bytes 196640 | tf_op jit(solution)/shard_map/ppermute | solution.py:26
  123.0 2.5 %collective-permute-done.15.refs_1_ = bf16[48,2048]{1,0:T(8,128)(2,1)S(1)} collective-permute-done((bf16[48,2048]{1,0:T(8,128)(2,1)S(1)}, bf16[48,2048]{1,0:T(8,128)(2,1)S(1)}, u32[]{:S(2)}, u32[]{:S(2)}) %collective-permute-start.15) | collective-permute-done | bytes 196640 | tf_op jit(solution)/shard_map/ppermute | solution.py:26
  (75 shorter events, 31.7 us)
Async XLA Ops:
  0.6 24.6 %collective-permute-start.4 = (bf16[512,2048]{1,0:T(8,128)(2,1)}, bf16[512,2048]{1,0:T(8,128)(2,1)S(1)}, u32[]{:S(2)}, u32[]{:S(2)}) collective-permute-start(bf16[512,2048]{1,0:T(8,128)(2,1)} %bitcast.22), channel_id=1, source_target_pairs={{0,8},{8,0},{16,24},{24,16},{1,9},{9,1},{17,25},{25,17},{2,10},{10... | collective-permute-start | bytes 6291464 | tf_op jit(solution)/shard_map/ppermute | solution.py:26
  1.1 8.4 %collective-permute-start.1 = (bf16[128,2048]{1,0:T(8,128)(2,1)}, bf16[128,2048]{1,0:T(8,128)(2,1)S(1)}, u32[]{:S(2)}, u32[]{:S(2)}) collective-permute-start(bf16[128,2048]{1,0:T(8,128)(2,1)} %bitcast.25), channel_id=1, source_target_pairs={{0,8},{8,0},{16,24},{24,16},{1,9},{9,1},{17,25},{25,17},{2,10},{10... | collective-permute-start | bytes 1572872 | tf_op jit(solution)/shard_map/ppermute | solution.py:26
  1.2 15.3 %collective-permute-start = (bf16[128,2048]{1,0:T(8,128)(2,1)}, bf16[128,2048]{1,0:T(8,128)(2,1)S(1)}, u32[]{:S(2)}, u32[]{:S(2)}) collective-permute-start(bf16[128,2048]{1,0:T(8,128)(2,1)} %bitcast.26), channel_id=1, source_target_pairs={{0,16},{8,24},{16,0},{24,8},{1,17},{9,25},{17,1},{25,9},{2,18},{10... | collective-permute-start | bytes 1572872 | tf_op jit(solution)/shard_map/ppermute | solution.py:26
  26.0 22.1 %collective-permute-start.5 = (bf16[128,2048]{1,0:T(8,128)(2,1)S(1)}, bf16[128,2048]{1,0:T(8,128)(2,1)S(1)}, u32[]{:S(2)}, u32[]{:S(2)}) collective-permute-start(bf16[128,2048]{1,0:T(8,128)(2,1)S(1)} %out_project.3), channel_id=1, source_target_pairs={{0,16},{8,24},{16,0},{24,8},{1,17},{9,25},{17,1},{25,9},{2,18},{10... | collective-permute-start | bytes 1572872 | tf_op jit(solution)/shard_map/ppermute | solution.py:26
  31.6 7.9 %collective-permute-start.22 = (bf16[64,512]{1,0:T(8,128)(2,1)S(1)}, bf16[64,512]{1,0:T(8,128)(2,1)S(1)}, u32[]{:S(2)}, u32[]{:S(2)}) collective-permute-start(bf16[64,512]{1,0:T(8,128)(2,1)S(1)} %get-tuple-element.69), channel_id=1, source_target_pairs={{0,3},{1,2},{2,1},{3,0},{4,7},{5,6},{6,5},{7,4},{8,11},{9,10},{10,... | collective-permute-start | bytes 196616 | tf_op jit(solution)/shard_map/ppermute | solution.py:26
  32.0 8.1 %collective-permute-start.23 = (bf16[64,512]{1,0:T(8,128)(2,1)S(1)}, bf16[64,512]{1,0:T(8,128)(2,1)S(1)}, u32[]{:S(2)}, u32[]{:S(2)}) collective-permute-start(bf16[64,512]{1,0:T(8,128)(2,1)S(1)} %get-tuple-element.70), channel_id=1, source_target_pairs={{0,4},{1,5},{2,6},{3,7},{4,0},{5,1},{6,2},{7,3},{8,12},{9,13},{10,... | collective-permute-start | bytes 196616 | tf_op jit(solution)/shard_map/ppermute | solution.py:26
  34.6 10.2 %collective-permute-start.24 = (bf16[64,512]{1,0:T(8,128)(2,1)S(1)}, bf16[64,512]{1,0:T(8,128)(2,1)S(1)}, u32[]{:S(2)}, u32[]{:S(2)}) collective-permute-start(bf16[64,512]{1,0:T(8,128)(2,1)S(1)} %get-tuple-element.71), channel_id=1, source_target_pairs={{0,5},{1,4},{2,7},{3,6},{4,1},{5,0},{6,3},{7,2},{8,13},{9,12},{10,... | collective-permute-start | bytes 196616 | tf_op jit(solution)/shard_map/ppermute | solution.py:26
  36.4 8.5 %collective-permute-start.25 = (bf16[64,512]{1,0:T(8,128)(2,1)S(1)}, bf16[64,512]{1,0:T(8,128)(2,1)S(1)}, u32[]{:S(2)}, u32[]{:S(2)}) collective-permute-start(bf16[64,512]{1,0:T(8,128)(2,1)S(1)} %get-tuple-element.72), channel_id=1, source_target_pairs={{0,6},{1,7},{2,4},{3,5},{4,2},{5,3},{6,0},{7,1},{8,14},{9,15},{10,... | collective-permute-start | bytes 196616 | tf_op jit(solution)/shard_map/ppermute | solution.py:26
  46.6 10.9 %collective-permute-start.28 = (bf16[512,512]{1,0:T(8,128)(2,1)S(1)}, bf16[512,512]{1,0:T(8,128)(2,1)S(1)}, u32[]{:S(2)}, u32[]{:S(2)}) collective-permute-start(bf16[512,512]{1,0:T(8,128)(2,1)S(1)} %pages_in.1.refs_0_), channel_id=1, source_target_pairs={{0,16},{8,24},{16,0},{24,8},{1,17},{9,25},{17,1},{25,9},{2,18},{10... | collective-permute-start | bytes 1572872 | tf_op jit(solution)/shard_map/ppermute | solution.py:26
  49.1 9.6 %collective-permute-start.16 = (bf16[48,2048]{1,0:T(8,128)(2,1)S(1)}, bf16[48,2048]{1,0:T(8,128)(2,1)S(1)}, u32[]{:S(2)}, u32[]{:S(2)}) collective-permute-start(bf16[48,2048]{1,0:T(8,128)(2,1)S(1)} %get-tuple-element.62), channel_id=1, source_target_pairs={{0,6},{1,7},{2,4},{3,5},{4,2},{5,3},{6,0},{7,1},{8,14},{9,15},{10,... | collective-permute-start | bytes 589832 | tf_op jit(solution)/shard_map/ppermute | solution.py:26
  50.6 8.1 %collective-permute-start.6 = (bf16[48,2048]{1,0:T(8,128)(2,1)S(1)}, bf16[48,2048]{1,0:T(8,128)(2,1)S(1)}, u32[]{:S(2)}, u32[]{:S(2)}) collective-permute-start(bf16[48,2048]{1,0:T(8,128)(2,1)S(1)} %get-tuple-element.49), channel_id=1, source_target_pairs={{0,1},{1,0},{2,3},{3,2},{4,5},{5,4},{6,7},{7,6},{8,9},{9,8},{10,11... | collective-permute-start | bytes 589832 | tf_op jit(solution)/shard_map/ppermute | solution.py:26
  51.5 9.5 %collective-permute-start.7 = (bf16[48,2048]{1,0:T(8,128)(2,1)S(1)}, bf16[48,2048]{1,0:T(8,128)(2,1)S(1)}, u32[]{:S(2)}, u32[]{:S(2)}) collective-permute-start(bf16[48,2048]{1,0:T(8,128)(2,1)S(1)} %get-tuple-element.50), channel_id=1, source_target_pairs={{0,2},{1,3},{2,0},{3,1},{4,6},{5,7},{6,4},{7,5},{8,10},{9,11},{10,... | collective-permute-start | bytes 589832 | tf_op jit(solution)/shard_map/ppermute | solution.py:26
  53.2 10.8 %collective-permute-start.8 = (bf16[48,2048]{1,0:T(8,128)(2,1)S(1)}, bf16[48,2048]{1,0:T(8,128)(2,1)S(1)}, u32[]{:S(2)}, u32[]{:S(2)}) collective-permute-start(bf16[48,2048]{1,0:T(8,128)(2,1)S(1)} %get-tuple-element.51), channel_id=1, source_target_pairs={{0,3},{1,2},{2,1},{3,0},{4,7},{5,6},{6,5},{7,4},{8,11},{9,10},{10,... | collective-permute-start | bytes 589832 | tf_op jit(solution)/shard_map/ppermute | solution.py:26
  57.6 36.8 %collective-permute-start.27 = (bf16[512,512]{1,0:T(8,128)(2,1)S(1)}, bf16[512,512]{1,0:T(8,128)(2,1)S(1)}, u32[]{:S(2)}, u32[]{:S(2)}) collective-permute-start(bf16[512,512]{1,0:T(8,128)(2,1)S(1)} %pages_in.1.refs_0_), channel_id=1, source_target_pairs={{0,8},{8,0},{16,24},{24,16},{1,9},{9,1},{17,25},{25,17},{2,10},{10... | collective-permute-start | bytes 1572872 | tf_op jit(solution)/shard_map/ppermute | solution.py:26
  58.6 37.8 %collective-permute-start.29 = (bf16[512,512]{1,0:T(8,128)(2,1)S(1)}, bf16[512,512]{1,0:T(8,128)(2,1)S(1)}, u32[]{:S(2)}, u32[]{:S(2)}) collective-permute-start(bf16[512,512]{1,0:T(8,128)(2,1)S(1)} %collective-permute-done.28.refs_2_), channel_id=1, source_target_pairs={{0,8},{8,0},{16,24},{24,16},{1,9},{9,1},{17,25},{25,17},{2,10},{10... | collective-permute-start | bytes 1572872 | tf_op jit(solution)/shard_map/ppermute | solution.py:26
  58.6 11.0 %collective-permute-start.17 = (bf16[48,2048]{1,0:T(8,128)(2,1)S(1)}, bf16[48,2048]{1,0:T(8,128)(2,1)S(1)}, u32[]{:S(2)}, u32[]{:S(2)}) collective-permute-start(bf16[48,2048]{1,0:T(8,128)(2,1)S(1)} %get-tuple-element.63), channel_id=1, source_target_pairs={{0,7},{1,6},{2,5},{3,4},{4,3},{5,2},{6,1},{7,0},{8,15},{9,14},{10,... | collective-permute-start | bytes 589832 | tf_op jit(solution)/shard_map/ppermute | solution.py:26
  61.0 24.7 %collective-permute-start.12 = (bf16[48,2048]{1,0:T(8,128)(2,1)S(1)}, bf16[48,2048]{1,0:T(8,128)(2,1)S(1)}, u32[]{:S(2)}, u32[]{:S(2)}) collective-permute-start(bf16[48,2048]{1,0:T(8,128)(2,1)S(1)} %get-tuple-element.57), channel_id=1, source_target_pairs={{0,4},{1,5},{2,6},{3,7},{4,0},{5,1},{6,2},{7,3},{8,12},{9,13},{10,... | collective-permute-start | bytes 589832 | tf_op jit(solution)/shard_map/ppermute | solution.py:26
  64.1 26.2 %collective-permute-start.13 = (bf16[48,2048]{1,0:T(8,128)(2,1)S(1)}, bf16[48,2048]{1,0:T(8,128)(2,1)S(1)}, u32[]{:S(2)}, u32[]{:S(2)}) collective-permute-start(bf16[48,2048]{1,0:T(8,128)(2,1)S(1)} %get-tuple-element.58), channel_id=1, source_target_pairs={{0,5},{1,4},{2,7},{3,6},{4,1},{5,0},{6,3},{7,2},{8,13},{9,12},{10,... | collective-permute-start | bytes 589832 | tf_op jit(solution)/shard_map/ppermute | solution.py:26
  69.7 26.7 %collective-permute-start.10 = (bf16[48,2048]{1,0:T(8,128)(2,1)S(1)}, bf16[48,2048]{1,0:T(8,128)(2,1)S(1)}, u32[]{:S(2)}, u32[]{:S(2)}) collective-permute-start(bf16[48,2048]{1,0:T(8,128)(2,1)S(1)} %get-tuple-element.54), channel_id=1, source_target_pairs={{0,2},{1,3},{2,0},{3,1},{4,6},{5,7},{6,4},{7,5},{8,10},{9,11},{10,... | collective-permute-start | bytes 589832 | tf_op jit(solution)/shard_map/ppermute | solution.py:26
  85.6 21.3 %collective-permute-start.11 = (bf16[48,2048]{1,0:T(8,128)(2,1)S(1)}, bf16[48,2048]{1,0:T(8,128)(2,1)S(1)}, u32[]{:S(2)}, u32[]{:S(2)}) collective-permute-start(bf16[48,2048]{1,0:T(8,128)(2,1)S(1)} %get-tuple-element.55), channel_id=1, source_target_pairs={{0,3},{1,2},{2,1},{3,0},{4,7},{5,6},{6,5},{7,4},{8,11},{9,10},{10,... | collective-permute-start | bytes 589832 | tf_op jit(solution)/shard_map/ppermute | solution.py:26
  90.2 35.5 %collective-permute-start.18 = (bf16[48,2048]{1,0:T(8,128)(2,1)S(1)}, bf16[48,2048]{1,0:T(8,128)(2,1)S(1)}, u32[]{:S(2)}, u32[]{:S(2)}) collective-permute-start(bf16[48,2048]{1,0:T(8,128)(2,1)S(1)} %get-tuple-element.64), channel_id=1, source_target_pairs={{0,6},{1,7},{2,4},{3,5},{4,2},{5,3},{6,0},{7,1},{8,14},{9,15},{10,... | collective-permute-start | bytes 589832 | tf_op jit(solution)/shard_map/ppermute | solution.py:26
  94.4 31.4 %collective-permute-start.19 = (bf16[48,2048]{1,0:T(8,128)(2,1)S(1)}, bf16[48,2048]{1,0:T(8,128)(2,1)S(1)}, u32[]{:S(2)}, u32[]{:S(2)}) collective-permute-start(bf16[48,2048]{1,0:T(8,128)(2,1)S(1)} %get-tuple-element.65), channel_id=1, source_target_pairs={{0,7},{1,6},{2,5},{3,4},{4,3},{5,2},{6,1},{7,0},{8,15},{9,14},{10,... | collective-permute-start | bytes 589832 | tf_op jit(solution)/shard_map/ppermute | solution.py:26
  96.4 26.6 %collective-permute-start.14 = (bf16[48,2048]{1,0:T(8,128)(2,1)S(1)}, bf16[48,2048]{1,0:T(8,128)(2,1)S(1)}, u32[]{:S(2)}, u32[]{:S(2)}) collective-permute-start(bf16[48,2048]{1,0:T(8,128)(2,1)S(1)} %get-tuple-element.59), channel_id=1, source_target_pairs={{0,4},{1,5},{2,6},{3,7},{4,0},{5,1},{6,2},{7,3},{8,12},{9,13},{10,... | collective-permute-start | bytes 589832 | tf_op jit(solution)/shard_map/ppermute | solution.py:26
  96.4 29.0 %collective-permute-start.15 = (bf16[48,2048]{1,0:T(8,128)(2,1)S(1)}, bf16[48,2048]{1,0:T(8,128)(2,1)S(1)}, u32[]{:S(2)}, u32[]{:S(2)}) collective-permute-start(bf16[48,2048]{1,0:T(8,128)(2,1)S(1)} %get-tuple-element.60), channel_id=1, source_target_pairs={{0,5},{1,4},{2,7},{3,6},{4,1},{5,0},{6,3},{7,2},{8,13},{9,12},{10,... | collective-permute-start | bytes 589832 | tf_op jit(solution)/shard_map/ppermute | solution.py:26
  (15 other events, 220.7 us)

commit v4 on v3

v4 whole, which is shorter than its diff:
```python
import functools
import math

import jax
import jax.numpy as jnp
from jax import lax
from jax.experimental import pallas as pl
from jax.experimental.pallas import tpu as pltpu
from jax.sharding import PartitionSpec as P

EPS = 1e-06
F32 = jnp.float32
BF16 = jnp.bfloat16
VMEM_SPEC = pl.BlockSpec(memory_space=pltpu.VMEM)
SMEM_SPEC = pl.BlockSpec(memory_space=pltpu.SMEM)


def rms_norm(value, gain):
    wide = value.astype(F32)
    scale = lax.rsqrt(jnp.mean(wide * wide, axis=-1, keepdims=True) + EPS)
    return (wide * scale * gain.astype(F32)).astype(BF16)


def swap(value, axis, step):
    size = lax.axis_size(axis)
    return lax.ppermute(value, axis, [(i, i ^ step) for i in range(size)])


def held(value):
    return pltpu.with_memory_space_constraint(value, pltpu.VMEM)


def array(shape, dtype=BF16):
    return jax.ShapeDtypeStruct(shape, dtype)


def call(kernel, name, out_shape, args, mib, flops, scratch=(), scalars=0):
    return pl.pallas_call(
        kernel,
        out_shape=out_shape,
        in_specs=[SMEM_SPEC] * scalars + [VMEM_SPEC] * (len(args) - scalars),
        scratch_shapes=scratch,
        compiler_params=pltpu.CompilerParams(vmem_limit_bytes=mib << 20),
        cost_estimate=pl.CostEstimate(flops=flops, bytes_accessed=0, transcendentals=0),
        name=name,
    )(*args)


def plan_kernel(routes_ref, *outs, groups):
    top, rows = routes_ref.shape
    count = sum(map(len, groups))
    capacity = outs[0].shape[0] // len(groups[0])
    expert = lax.axis_index("blk") ^ lax.broadcasted_iota(jnp.int32, (count, rows), 0)
    chosen = jnp.zeros((count, rows), F32)
    for t in range(top):
        chosen = jnp.maximum(chosen, jnp.where(routes_ref[t : t + 1] == expert, F32(1), F32(0)))
    before = lax.broadcasted_iota(jnp.int32, (rows, rows), 0)
    after = lax.broadcasted_iota(jnp.int32, (rows, rows), 1)
    upto = jnp.where(before <= after, F32(1), F32(0)).astype(BF16)
    rank = jnp.dot(chosen.astype(BF16), upto, preferred_element_type=F32) - 1
    slot = jnp.where(chosen > 0, rank, F32(-1))
    place = lax.broadcasted_iota(jnp.int32, (capacity, rows), 0).astype(F32)
    for group, out in zip(groups, outs):
        for i, s in enumerate(group):
            hit = jnp.where(slot[s : s + 1] == place, F32(1), F32(0))
            out[i * capacity : (i + 1) * capacity] = hit.astype(BF16)


def plan(routes, groups):
    top, rows = routes.shape
    capacity = rows * 3 // 8
    return call(
        functools.partial(plan_kernel, groups=groups),
        "plan",
        tuple(array((len(group) * capacity, rows)) for group in groups),
        (routes,),
        4,
        0,
    )


def project_rows(blocks, gain_ref, w_ref, q_ref, kv_ref, normed, head_dim):
    rows = blocks[0].shape[0]
    for i, block in enumerate(blocks):
        normed[i * rows : (i + 1) * rows] = rms_norm(block[...], gain_ref[0:1])
    for h in range(q_ref.shape[1] // head_dim):
        columns = slice(3 * h * head_dim, 3 * (h + 1) * head_dim)
        out = jnp.dot(normed[...], w_ref[:, columns], preferred_element_type=F32).astype(BF16)
        q_ref[:, h * head_dim : (h + 1) * head_dim] = out[:, :head_dim]
        kv_ref[:, 2 * h * head_dim : 2 * (h + 1) * head_dim] = out[:, head_dim:]


def project_kernel(*refs, head_dim):
    *blocks, gain_ref, w_ref, q_ref, kv_ref, normed = refs
    project_rows(blocks, gain_ref, w_ref, q_ref, kv_ref, normed, head_dim)


def project(blocks, gains, w_flat, heads, head_dim):
    rows, width = len(blocks) * blocks[0].shape[0], blocks[0].shape[1]
    return call(
        functools.partial(project_kernel, head_dim=head_dim),
        "project",
        (array((rows, heads * head_dim)), array((rows, heads * 2 * head_dim))),
        (*blocks, gains, w_flat),
        12,
        0,
        [pltpu.VMEM((rows, width), BF16)],
    )


def attend_rows(first, seg_ref, queries, kvs, keep_ref, send_ref, bias, head_dim):
    block = keep_ref.shape[0]
    me = lax.axis_index("seq")
    row = jnp.concatenate(
        [
            seg_ref[:, pl.ds(pl.multiple_of((me ^ k) * block, block), block)]
            for k in range(seg_ref.shape[1] // block)
        ],
        axis=1,
    ).astype(F32)
    column = jnp.broadcast_to(row, (8, row.shape[1])).T[first : first + 2 * block, 0:1]
    bias[...] = jnp.where(column == row, F32(0), F32(-1e30))
    factor = math.log2(math.e) / math.sqrt(head_dim)
    for h in range(queries[0].shape[1] // head_dim):
        q_cols = slice(h * head_dim, (h + 1) * head_dim)
        k_cols = slice(2 * h * head_dim, (2 * h + 1) * head_dim)
        v_cols = slice((2 * h + 1) * head_dim, (2 * h + 2) * head_dim)
        query = jnp.concatenate([ref[:, q_cols] for ref in queries], axis=0)
        key = jnp.concatenate([ref[:, k_cols] for ref in kvs], axis=0)
        value = jnp.concatenate([ref[:, v_cols] for ref in kvs], axis=0)
        scores = lax.dot_general(
            query, key, (((1,), (1,)), ((), ())), preferred_element_type=F32
        )
        scores = scores + bias[...]
        top = jnp.max(scores, axis=-1, keepdims=True)
        weights = jnp.exp2((scores - top) * factor)
        total = jnp.sum(weights, axis=-1, keepdims=True)
        context = jnp.dot(weights.astype(BF16), value, preferred_element_type=F32)
        context = (context / total).astype(BF16)
        keep_ref[:, q_cols] = context[:block]
        send_ref[:, q_cols] = context[block:]


def attend_near_kernel(seg, q, kv_near, kv_far, kv_last, keep, send, bias, *, head_dim):
    attend_rows(0, seg, [q], [kv_near, kv_far, kv_last], keep, send, bias, head_dim)


def attend_near(segments, q, kvs, head_dim):
    rows, cols = q.shape
    group_len = segments.shape[1]
    return call(
        functools.partial(attend_near_kernel, head_dim=head_dim),
        "attend_near",
        (array((rows // 2, cols)),) * 2,
        (segments, q, *kvs),
        12,
        1 << 34,
        [pltpu.VMEM((rows, group_len), F32)],
    )


def attend_far_kernel(
    seg, q_far, kv_near, kv_far, block, gain, w_ref, keep, send, kv, q, normed, bias, *, head_dim
):
    project_rows([block], gain, w_ref, q, kv, normed, head_dim)
    first = kv_near.shape[0]
    attend_rows(first, seg, [q_far, q], [kv_near, kv_far, kv], keep, send, bias, head_dim)


def attend_far(segments, q_far, kv_near, kv_far, block, gains, w_flat, head_dim):
    rows, cols = q_far.shape
    group_len = segments.shape[1]
    return call(
        functools.partial(attend_far_kernel, head_dim=head_dim),
        "attend_far",
        (array((rows, cols)),) * 2 + (array((rows, 2 * cols)),),
        (segments, q_far, kv_near, kv_far, block, gains, w_flat),
        12,
        0,
        [
            pltpu.VMEM((rows, cols), BF16),
            pltpu.VMEM(block.shape, BF16),
            pltpu.VMEM((2 * rows, group_len), F32),
        ],
    )


def out_project_kernel(mine_ref, theirs_ref, w_mine, w_theirs, out_ref):
    out = jnp.dot(mine_ref[...], w_mine[...], preferred_element_type=F32)
    out = out + jnp.dot(theirs_ref[...], w_theirs[...], preferred_element_type=F32)
    out_ref[...] = out.astype(out_ref.dtype)


def out_project(mine, theirs, w_mine, w_theirs, dtype):
    rows, depth = mine.shape
    width = w_mine.shape[1]
    return call(
        out_project_kernel,
        "out_project",
        array((rows, width), dtype),
        (mine, theirs, w_mine, w_theirs),
        8,
        0,
    )


def join_rows(refs, spans, out):
    at = 0
    for ref, (low, high) in zip(refs, spans):
        out[at : at + high - low] = ref[low:high]
        at += high - low


def join_kernel(*refs, spans):
    join_rows(refs[:-1], spans, refs[-1])


def split(parts):
    arrays = tuple(part[0] for part in parts)
    spans = tuple((low, high) for _, low, high in parts)
    return arrays, spans, sum(high - low for low, high in spans)


def full(value):
    return (value, 0, value.shape[0])


def join(parts):
    arrays, spans, rows = split(parts)
    return call(
        functools.partial(join_kernel, spans=spans),
        "join",
        array((rows, arrays[0].shape[1])),
        arrays,
        4,
        0,
    )


def pages_out_kernel(owner_ref, *refs, count):
    *blocks, rows, pages = refs
    blocks, outs = blocks[: -(count // 4)], blocks[-(count // 4) :]
    size = blocks[0].shape[0]
    page_len = outs[0].shape[0]
    seq_me, blk_me = lax.axis_index("seq"), lax.axis_index("blk")
    for k, block in enumerate(blocks):
        rows[pl.ds(pl.multiple_of((seq_me ^ k) * size, size), size)] = block[...]
    for j in range(count):
        step = owner_ref[0, j] ^ blk_me

        @pl.when(step % 4 == seq_me)
        def _(j=j, step=step):
            pages[step // 4] = rows[j * page_len : (j + 1) * page_len]

    for k, out in enumerate(outs):
        out[...] = pages[k]


def pages_out(owners, blocks):
    count = owners.shape[1]
    size, width = blocks[0].shape
    group_len = len(blocks) * size
    page_len = group_len // count
    return call(
        functools.partial(pages_out_kernel, count=count),
        "pages_out",
        (array((page_len, width)),) * (count // 4),
        (owners, *blocks),
        8,
        0,
        [pltpu.VMEM((group_len, width), BF16), pltpu.VMEM((count // 4, page_len, width), BF16)],
        scalars=1,
    )


def to_owner(page, number):
    seq_count, blk_count = lax.axis_size("seq"), lax.axis_size("blk")
    pairs = [
        (i * blk_count + b, i * blk_count + (b ^ (4 * number + i)))
        for i in range(seq_count)
        for b in range(blk_count)
    ]
    return lax.ppermute(page, ("seq", "blk"), pairs)


def cache_kernel(mine_ref, theirs_ref, gain_ref, w_ref, out_ref, rows, *, head_dim):
    count, page_len = out_ref.shape[1:3]
    seq_me, blk_me = lax.axis_index("seq"), lax.axis_index("blk")
    half = count // 4 * page_len
    for core, ref in enumerate((mine_ref, theirs_ref)):
        for chip in range(2):
            for k in range(count // 4):
                start = (blk_me ^ (4 * k + (seq_me ^ (2 * chip + core)))) * page_len
                page = ref[chip * half + k * page_len : chip * half + (k + 1) * page_len]
                rows[pl.ds(pl.multiple_of(start, page_len), page_len)] = page
    rows[...] = rms_norm(rows[...], gain_ref[0:1])
    for h in range(out_ref.shape[3] // (2 * head_dim)):
        columns = slice((3 * h + 1) * head_dim, 3 * (h + 1) * head_dim)
        out = jnp.dot(rows[...], w_ref[:, columns], preferred_element_type=F32).astype(BF16)
        out = out.reshape(count, page_len, 2 * head_dim)
        out_ref[0, :, :, 2 * h * head_dim : 2 * (h + 1) * head_dim] = out


def cache(mine, theirs, gains, w_flat, count, heads, head_dim):
    rows, width = mine.shape
    return call(
        functools.partial(cache_kernel, head_dim=head_dim),
        "cache",
        array((1, count, 2 * rows // count, heads * 2 * head_dim)),
        (mine, theirs, gains, w_flat),
        16,
        0,
        [pltpu.VMEM((2 * rows, width), BF16)],
    )


def pick_rows(pick, ffn_in, outs):
    picked = jnp.dot(pick, ffn_in, preferred_element_type=F32).astype(BF16)
    at = 0
    for out in outs:
        out[...] = picked[at : at + out.shape[0]]
        at += out.shape[0]


def dispatch_kernel(own_ref, mixed_ref, far_ref, gain_ref, pick_ref, resid_ref, ffn_ref, *outs):
    resid = own_ref[...].astype(F32) + mixed_ref[...] + far_ref[...].astype(F32)
    resid = resid.astype(BF16)
    resid_ref[...] = resid
    ffn_in = rms_norm(resid, gain_ref[1:2])
    ffn_ref[...] = ffn_in
    pick_rows(pick_ref[...], ffn_in, outs)


def dispatch(own, mixed, far, gains, pick, count):
    rows, width = own.shape
    capacity = pick.shape[0] // count
    return call(
        dispatch_kernel,
        "dispatch",
        (array((rows, width)),) * 2 + (array((capacity, width)),) * count,
        (own, mixed, far, gains, pick),
        max(10, pick.shape[0] * width * 12 >> 20),
        0,
    )


def dispatch_more_kernel(ffn_ref, pick_ref, *outs):
    pick_rows(pick_ref[...], ffn_ref[...], outs)


def dispatch_more(ffn_in, pick, sizes):
    width = ffn_in.shape[1]
    return call(
        dispatch_more_kernel,
        "dispatch_more",
        tuple(array((size, width)) for size in sizes),
        (ffn_in, pick),
        max(10, pick.shape[0] * width * 12 >> 20),
        1 << 34,
    )


def weigh_kernel(ffn_ref, router_ref, *refs, groups):
    logits = lax.dot_general(
        router_ref[...], ffn_ref[...], (((1,), (1,)), ((), ())), preferred_element_type=F32
    )
    gates = jax.nn.sigmoid(logits).astype(BF16)
    experts = gates.shape[0]
    step = lax.broadcasted_iota(jnp.int32, (experts, experts), 0)
    expert = lax.broadcasted_iota(jnp.int32, (experts, experts), 1)
    order = jnp.where(lax.axis_index("blk") ^ step == expert, F32(1), F32(0)).astype(BF16)
    gates = jnp.dot(order, gates, preferred_element_type=F32)
    for group, pick, out in zip(groups, refs[: len(groups)], refs[len(groups) :]):
        capacity = pick.shape[0] // len(group)
        parts = [
            pick[i * capacity : (i + 1) * capacity].astype(F32) * gates[s : s + 1]
            for i, s in enumerate(group)
        ]
        out[...] = jnp.concatenate(parts, axis=0).T.astype(BF16)


def weigh(ffn_in, router, picks, groups):
    return call(
        functools.partial(weigh_kernel, groups=groups),
        "weigh",
        tuple(array(pick.shape[::-1]) for pick in picks),
        (ffn_in, router, *picks),
        8,
        0,
    )


def expert_kernel(*refs, spans):
    count = len(spans)
    in_ref, down_ref = refs[count : count + 2]
    *outs, rows, hidden = refs[count + 2 :]
    ff, width = down_ref.shape
    join_rows(refs[:count], spans, rows)
    tile = min(ff, 512)
    for start in range(0, ff, tile):
        gate = jnp.dot(rows[...], in_ref[:, start : start + tile], preferred_element_type=F32)
        up = jnp.dot(
            rows[...], in_ref[:, ff + start : ff + start + tile], preferred_element_type=F32
        )
        hidden[:, start : start + tile] = (jax.nn.silu(gate) * up).astype(BF16)
    for start in range(0, width, tile):
        part = jnp.dot(hidden[...], down_ref[:, start : start + tile], preferred_element_type=F32)
        at = 0
        for out in outs:
            out[:, start : start + tile] = part[at : at + out.shape[0]].astype(BF16)
            at += out.shape[0]


def expert(parts, gate_up, down):
    arrays, spans, rows = split(parts)
    ff, width = down.shape
    return call(
        functools.partial(expert_kernel, spans=spans),
        "expert",
        tuple(array((high - low, width)) for low, high in spans),
        (*arrays, gate_up, down),
        max(8, rows * 20480 >> 20),
        1 << 35,
        [pltpu.VMEM((rows, width), BF16), pltpu.VMEM((rows, ff), BF16)],
    )


def combine_kernel(base_ref, weigh_ref, *refs, spans):
    *ins, out_ref, rows = refs
    join_rows(ins, spans, rows)
    total = jnp.dot(weigh_ref[...], rows[...], preferred_element_type=F32)
    out_ref[...] = (base_ref[...].astype(F32) + total).astype(out_ref.dtype)


def combine(base, weights, parts, dtype):
    arrays, spans, rows = split(parts)
    return call(
        functools.partial(combine_kernel, spans=spans),
        "combine",
        array(base.shape, dtype),
        (base, weights, *arrays),
        max(8, rows * 16384 >> 20),
        0,
        [pltpu.VMEM((rows, base.shape[1]), BF16)],
    )


def on_device(
    residual_in,
    segment_ids,
    attn_gain,
    w_qkv,
    w_out,
    ffn_gain,
    w_router,
    routes,
    w_gate_up,
    w_down,
    page_owner,
):
    own = residual_in[0]
    width = own.shape[1]
    heads_here = w_qkv.shape[1]
    head_dim = w_out.shape[1]
    blk_count = lax.axis_size("blk")

    slots = own.shape[0] * 3 // 8
    half = (4 + blk_count) // 2
    near, first, last = tuple(range(4)), tuple(range(4, half)), tuple(range(half, blk_count))
    groups = (first, (*near, *last))
    picks = plan(routes[0].T, groups)

    far = swap(own, "seq", 2)
    w_mine = w_out.reshape(heads_here * head_dim, width)
    picks, w_mine, to_core = lax.optimization_barrier((picks, w_mine, own))
    core = swap(to_core, "seq", 1)
    w_theirs = swap(w_mine, "seq", 1)
    gains = jnp.stack([attn_gain, ffn_gain])

    w_flat = held(w_qkv.reshape(width, heads_here * 3 * head_dim))
    q_near, kv_near = project((own, core), gains, w_flat, heads_here, head_dim)
    far, q_near, kv_near = lax.optimization_barrier((far, q_near, kv_near))
    far_core = swap(far, "seq", 1)
    q_far, kv_far = project((far,), gains, w_flat, heads_here, head_dim)
    keep_far, send_far, kv_last = attend_far(
        segment_ids, q_far, kv_near, kv_far, far_core, gains, w_flat, head_dim
    )
    w_mine, w_theirs = held(w_mine), held(w_theirs)
    theirs_far = swap(send_far, "seq", 1)
    outgoing = pages_out(page_owner, (own, core, far, far_core))
    theirs_far, outgoing = lax.optimization_barrier((theirs_far, outgoing))
    far_sum = out_project(keep_far, theirs_far, w_mine, w_theirs, BF16)
    far_sum, outgoing = lax.optimization_barrier((far_sum, outgoing))
    from_far = swap(far_sum, "seq", 2)
    arrived = [to_owner(page, k) for k, page in enumerate(outgoing)]
    keep, send = attend_near(segment_ids, q_near, (kv_near, kv_far, kv_last), head_dim)
    mixed = out_project(keep, swap(send, "seq", 1), w_mine, w_theirs, F32)

    gate_up, down = held(w_gate_up[0]), held(w_down[0])

    def there(group, blocks):
        pairs = zip(group, blocks)
        return tuple(swap(block, "blk", step) if step else block for step, block in pairs)

    def work(blocks):
        return expert([full(block) for block in blocks], gate_up, down)

    from_far, arrived = lax.optimization_barrier((from_far, arrived))
    resid, ffn_in, *sent_first = dispatch(own, mixed, from_far, gains, picks[0], len(first))
    rows_first = there(first, sent_first)
    sent = dispatch_more(ffn_in, picks[1], (slots,) * len(groups[1]))
    sent_near, sent_last = sent[: len(near)], sent[len(near) :]
    rows_near = there(near, sent_near)
    share = join([full(page) for page in arrived])
    share_far = swap(share, "seq", 2)
    rows_last = there(last, sent_last)
    first_out = work(rows_first)
    back_first = there(first, first_out)
    rows_near, first_out, share_far = lax.optimization_barrier((rows_near, first_out, share_far))
    both = join([full(share), full(share_far)])
    both_core = swap(both, "seq", 1)
    near_out = work(rows_near)
    rows_last, both_core = lax.optimization_barrier((rows_last, both_core))
    last_out = work(rows_last)
    back_last = there(last, last_out)
    near_out, last_out, both_core = lax.optimization_barrier((near_out, last_out, both_core))
    back_near = there(near, near_out)
    kv_cache = cache(both, both_core, gains, w_flat, blk_count, heads_here, head_dim)

    weights = weigh(ffn_in, w_router.T, picks, groups)
    total = combine(resid, weights[0], [full(block) for block in back_first], F32)
    kv_cache, total = lax.optimization_barrier((kv_cache, total))
    parts = [full(block) for block in (*back_near, *back_last)]
    total = combine(total, weights[1], parts, BF16)
    return (total[None], kv_cache)


def solution(mesh):
    in_specs = (
        P("blk", "seq", None),
        P("blk", None),
        P(),
        P(None, "seq", None),
        P("seq", None, None),
        P(),
        P(),
        P("blk", "seq", None),
        P("blk", None, None),
        P("blk", None, None),
        P("blk", None),
    )
    out_specs = (P("blk", "seq", None), P("blk", None, None, "seq"))
    return jax.shard_map(
        on_device, mesh=mesh, in_specs=in_specs, out_specs=out_specs, check_vma=False
    )
```

time: 127 us -> 119 us (0.937)
  starting transfers between devices: 51.3 us -> 46.4 us
  waiting for transfers between devices: 44.9 us -> 40.4 us
    ppermute x30 -> x23, starting transfers between devices: 51.3 us -> 42.6 us  [swap(): return lax.ppermute(value, axis, [(i, i ^ step) for i in range(size)])]
    ppermute x30 -> x23, waiting for transfers between devices: 44.9 us -> 36.8 us  [swap(): return lax.ppermute(value, axis, [(i, i ^ step) for i in range(size)])]
    ppermute x0 -> x2, starting transfers between devices: none -> 3.76 us  [to_owner(): return lax.ppermute(page, ('seq', 'blk'), pairs)]
    ppermute x0 -> x2, waiting for transfers between devices: none -> 3.6 us  [to_owner(): return lax.ppermute(page, ('seq', 'blk'), pairs)]
    pallas_call x16 -> x19, Pallas kernels: 24.3 us -> 25 us  [call(): pl.pallas_call(kernel, out_shape=out_shape, in_specs=[SMEM_SPEC] * scalar...]
  transfers between devices with their start and end apart: 30 -> 25, of which waited for: 15 -> 12; matrix products, arithmetic and copies ran while one was open for 4% -> 5% of each run, Pallas kernels for 18% -> 19%
where the time goes in v4:
time: 119 us
  starting transfers between devices  46.4 us (39%)
  waiting for transfers between devices  40.4 us (34%)
  Pallas kernels  25 us (21%)
  local copies, waits for them, and re-layouts  6.1 us (5%)
    ppermute x23, starting transfers between devices, swap(): return lax.ppermute(value, axis, [(i, i ^ step) for i in range(size)])  42.6 us
    ppermute x23, waiting for transfers between devices, swap(): return lax.ppermute(value, axis, [(i, i ^ step) for i in range(size)])  36.8 us
    pallas_call x19, Pallas kernels, call(): pl.pallas_call(kernel, out_shape=out_shape, in_specs=[SMEM_SPEC] * scalar...  25 us
    unnamed x19, local copies, waits for them, and re-layouts  4.72 us
    ppermute x2, starting transfers between devices, to_owner(): return lax.ppermute(page, ('seq', 'blk'), pairs)  3.76 us
    ppermute x2, waiting for transfers between devices, to_owner(): return lax.ppermute(page, ('seq', 'blk'), pairs)  3.6 us
  transfers between devices with their start and end apart: 25, of which 12 were waited for; matrix products, arithmetic and copies ran while one was open for 5% of the time, Pallas kernels for 19%

profile of v4, /device:TPU:0, one launch (start us, length us, event | category | flops | bytes accessed | tf_op | source)
XLA Modules:
  0.0 118.8 jit_solution(9354803931700108314)
XLA Ops:
  2.1 2.9 %collective-permute-start = (bf16[128,2048]{1,0:T(8,128)(2,1)}, bf16[128,2048]{1,0:T(8,128)(2,1)S(1)}, u32[]{:S(2)}, u32[]{:S(2)}) collective-permute-start(bf16[128,2048]{1,0:T(8,128)(2,1)} %bitcast.19), channel_id=1, source_target_pairs={{0,16},{8,24},{16,0},{24,8},{1,17},{9,25},{17,1},{25,9},{2,18},{10... | collective-permute-start | bytes 1572872 | tf_op jit(solution)/shard_map/ppermute | solution.py:26
  6.4 4.0 %copy.13 = bf16[256,8,4,384]{3,1,2,0:T(8,128)(2,1)S(1)} copy(bf16[256,8,4,384]{3,2,1,0:T(4,128)(2,1)} %bitcast.33) | data formatting | bytes 12582912
  10.4 2.6 %project.2 = (bf16[256,512]{1,0:T(8,128)(2,1)S(1)}, bf16[256,1024]{1,0:T(8,128)(2,1)S(1)}) custom-call(bf16[128,2048]{1,0:T(8,128)(2,1)S(1)} %bitcast.20, bf16[128,2048]{1,0:T(8,128)(2,1)S(1)} %collective-permute-done.1.refs_1_, bf16[2,2048]{1,0:T(2,128)(2,1)S(1)} %pad_maximum_fusion.refs_2_.refs_1_.gain.gain_ref, bf16[2048,1536]{1,0:T(8,128)(2,1)S(1)} %bitcast.11), custom_call_target="tpu_custom_call" | custom-call | tf_op jit(solution)/shard_map/project/pallas_call | solution.py:38
  13.1 4.3 %collective-permute-done.refs_0_.refs_2_ = bf16[128,2048]{1,0:T(8,128)(2,1)S(1)} collective-permute-done((bf16[128,2048]{1,0:T(8,128)(2,1)}, bf16[128,2048]{1,0:T(8,128)(2,1)S(1)}, u32[]{:S(2)}, u32[]{:S(2)}) %collective-permute-start) | collective-permute-done | bytes 524320 | tf_op jit(solution)/shard_map/ppermute | solution.py:26
  19.3 2.7 %attend_far.1 = (bf16[128,512]{1,0:T(8,128)(2,1)S(1)}, bf16[128,512]{1,0:T(8,128)(2,1)S(1)}, bf16[128,1024]{1,0:T(8,128)(2,1)S(1)}) custom-call(s32[1,512]{1,0:T(1,128)S(1)} %copy-done.3, bf16[128,512]{1,0:T(8,128)(2,1)S(1)} %get-tuple-element.72.q_far, bf16[256,1024]{1,0:T(8,128)(2,1)S(1)} %get-tuple-element.73.kv_near, ...), custom_call_target="tpu_custom_call" | custom-call | tf_op jit(solution)/shard_map/attend_far/pallas_call | solution.py:38
  25.0 2.9 %collective-permute-start.7 = (bf16[64,2048]{1,0:T(8,128)(2,1)S(1)}, bf16[64,2048]{1,0:T(8,128)(2,1)S(1)}, u32[]{:S(2)}, u32[]{:S(2)}) collective-permute-start(bf16[64,2048]{1,0:T(8,128)(2,1)S(1)} %get-tuple-element.85), channel_id=1, source_target_pairs={{0,4},{1,5},{2,6},{3,7},{4,0},{5,1},{6,2},{7,3},{8,13},{9,12},{10,... | collective-permute-start | bytes 786440 | tf_op jit(solution)/shard_map/ppermute | solution.py:283
  27.9 4.2 %collective-permute-start.5 = (bf16[128,2048]{1,0:T(8,128)(2,1)S(1)}, bf16[128,2048]{1,0:T(8,128)(2,1)S(1)}, u32[]{:S(2)}, u32[]{:S(2)}) collective-permute-start(bf16[128,2048]{1,0:T(8,128)(2,1)S(1)} %out_project.2), channel_id=1, source_target_pairs={{0,16},{8,24},{16,0},{24,8},{1,17},{9,25},{17,1},{25,9},{2,18},{10... | collective-permute-start | bytes 1572872 | tf_op jit(solution)/shard_map/ppermute | solution.py:26
  35.8 3.6 %collective-permute-done.7.refs_1_ = bf16[64,2048]{1,0:T(8,128)(2,1)S(1)} collective-permute-done((bf16[64,2048]{1,0:T(8,128)(2,1)S(1)}, bf16[64,2048]{1,0:T(8,128)(2,1)S(1)}, u32[]{:S(2)}, u32[]{:S(2)}) %collective-permute-start.7) | collective-permute-done | bytes 262176 | tf_op jit(solution)/shard_map/ppermute | solution.py:283
  39.3 5.3 %collective-permute-done.5.far_ref = bf16[128,2048]{1,0:T(8,128)(2,1)S(1)} collective-permute-done((bf16[128,2048]{1,0:T(8,128)(2,1)S(1)}, bf16[128,2048]{1,0:T(8,128)(2,1)S(1)}, u32[]{:S(2)}, u32[]{:S(2)}) %collective-permute-start.5) | collective-permute-done | bytes 524320 | tf_op jit(solution)/shard_map/ppermute | solution.py:26
  45.6 3.6 %collective-permute-start.13 = (bf16[48,2048]{1,0:T(8,128)(2,1)S(1)}, bf16[48,2048]{1,0:T(8,128)(2,1)S(1)}, u32[]{:S(2)}, u32[]{:S(2)}) collective-permute-start(bf16[48,2048]{1,0:T(8,128)(2,1)S(1)} %get-tuple-element.101), channel_id=1, source_target_pairs={{0,5},{1,4},{2,7},{3,6},{4,1},{5,0},{6,3},{7,2},{8,13},{9,12},{10,... | collective-permute-start | bytes 589832 | tf_op jit(solution)/shard_map/ppermute | solution.py:26
  49.3 1.8 %collective-permute-start.14 = (bf16[128,2048]{1,0:T(8,128)(2,1)S(1)}, bf16[128,2048]{1,0:T(8,128)(2,1)S(1)}, u32[]{:S(2)}, u32[]{:S(2)}) collective-permute-start(bf16[128,2048]{1,0:T(8,128)(2,1)S(1)} %join.2.refs_0_), channel_id=1, source_target_pairs={{0,16},{8,24},{16,0},{24,8},{1,17},{9,25},{17,1},{25,9},{2,18},{10... | collective-permute-start | bytes 1572872 | tf_op jit(solution)/shard_map/ppermute | solution.py:26
  52.8 9.2 %collective-permute-done.12.refs_0_ = bf16[48,2048]{1,0:T(8,128)(2,1)S(1)} collective-permute-done((bf16[48,2048]{1,0:T(8,128)(2,1)S(1)}, bf16[48,2048]{1,0:T(8,128)(2,1)S(1)}, u32[]{:S(2)}, u32[]{:S(2)}) %collective-permute-start.12) | collective-permute-done | bytes 196640 | tf_op jit(solution)/shard_map/ppermute | solution.py:26
  62.0 4.7 %collective-permute-done.13.refs_1_ = bf16[48,2048]{1,0:T(8,128)(2,1)S(1)} collective-permute-done((bf16[48,2048]{1,0:T(8,128)(2,1)S(1)}, bf16[48,2048]{1,0:T(8,128)(2,1)S(1)}, u32[]{:S(2)}, u32[]{:S(2)}) %collective-permute-start.13) | collective-permute-done | bytes 196640 | tf_op jit(solution)/shard_map/ppermute | solution.py:26
  67.8 2.2 %expert.3 = (bf16[48,2048]{1,0:T(8,128)(2,1)S(1)}, bf16[48,2048]{1,0:T(8,128)(2,1)S(1)}) custom-call(bf16[48,2048]{1,0:T(8,128)(2,1)S(1)} %collective-permute-done.12.refs_0_, bf16[48,2048]{1,0:T(8,128)(2,1)S(1)} %collective-permute-done.13.refs_1_, bf16[2048,2048]{1,0:T(8,128)(2,1)S(1)} %bitcast.26, bf16[1024,2048]{1,0:T(8,128)(2,1)S(1)} %bitcast.29), custom_call_target="tpu_custom_call" | custom-call | flops 34359738368 | tf_op jit(solution)/shard_map/expert/pallas_call | solution.py:38
  70.1 2.6 %collective-permute-start.16 = (bf16[48,2048]{1,0:T(8,128)(2,1)S(1)}, bf16[48,2048]{1,0:T(8,128)(2,1)S(1)}, u32[]{:S(2)}, u32[]{:S(2)}) collective-permute-start(bf16[48,2048]{1,0:T(8,128)(2,1)S(1)} %get-tuple-element.114), channel_id=1, source_target_pairs={{0,7},{1,6},{2,5},{3,4},{4,3},{5,2},{6,1},{7,0},{8,15},{9,14},{10,... | collective-permute-start | bytes 589832 | tf_op jit(solution)/shard_map/ppermute | solution.py:26
  72.7 2.3 %collective-permute-done.11.refs_3_ = bf16[48,2048]{1,0:T(8,128)(2,1)S(1)} collective-permute-done((bf16[48,2048]{1,0:T(8,128)(2,1)S(1)}, bf16[48,2048]{1,0:T(8,128)(2,1)S(1)}, u32[]{:S(2)}, u32[]{:S(2)}) %collective-permute-start.11) | collective-permute-done | bytes 196640 | tf_op jit(solution)/shard_map/ppermute | solution.py:26
  75.0 1.6 %collective-permute-start.19 = (bf16[48,2048]{1,0:T(8,128)(2,1)S(1)}, bf16[48,2048]{1,0:T(8,128)(2,1)S(1)}, u32[]{:S(2)}, u32[]{:S(2)}) collective-permute-start(bf16[48,2048]{1,0:T(8,128)(2,1)S(1)} %get-tuple-element.103), channel_id=1, source_target_pairs={{0,5},{1,4},{2,7},{3,6},{4,1},{5,0},{6,3},{7,2},{8,13},{9,12},{10,... | collective-permute-start | bytes 589832 | tf_op jit(solution)/shard_map/ppermute | solution.py:26
  76.7 2.7 %expert.4 = (bf16[48,2048]{1,0:T(8,128)(2,1)S(1)}, bf16[48,2048]{1,0:T(8,128)(2,1)S(1)}, bf16[48,2048]{1,0:T(8,128)(2,1)S(1)}, bf16[48,2048]{1,0:T(8,128)(2,1)S(1)}) custom-call(bf16[48,2048]{1,0:T(8,128)(2,1)S(1)} %get-tuple-element.105.refs_0_, bf16[48,2048]{1,0:T(8,128)(2,1)S(1)} %collective-permute-done.9.refs_1_, ...), custom_call_target="tpu_custom_call" | custom-call | flops 34359738368 | tf_op jit(solution)/shard_map/expert/pallas_call | solution.py:38
  80.6 2.2 %expert.5 = (bf16[48,2048]{1,0:T(8,128)(2,1)S(1)}, bf16[48,2048]{1,0:T(8,128)(2,1)S(1)}) custom-call(bf16[48,2048]{1,0:T(8,128)(2,1)S(1)} %collective-permute-done.15.refs_0_, bf16[48,2048]{1,0:T(8,128)(2,1)S(1)} %collective-permute-done.16.refs_1_, bf16[2048,2048]{1,0:T(8,128)(2,1)S(1)} %bitcast.28, bf16[1024,2048]{1,0:T(8,128)(2,1)S(1)} %bitcast.31), custom_call_target="tpu_custom_call" | custom-call | flops 34359738368 | tf_op jit(solution)/shard_map/expert/pallas_call | solution.py:38
  82.8 2.8 %collective-permute-start.23 = (bf16[48,2048]{1,0:T(8,128)(2,1)S(1)}, bf16[48,2048]{1,0:T(8,128)(2,1)S(1)}, u32[]{:S(2)}, u32[]{:S(2)}) collective-permute-start(bf16[48,2048]{1,0:T(8,128)(2,1)S(1)} %get-tuple-element.117), channel_id=1, source_target_pairs={{0,6},{1,7},{2,4},{3,5},{4,2},{5,3},{6,0},{7,1},{8,14},{9,15},{10,... | collective-permute-start | bytes 589832 | tf_op jit(solution)/shard_map/ppermute | solution.py:26
  86.1 15.7 %collective-permute-start.21 = (bf16[48,2048]{1,0:T(8,128)(2,1)S(1)}, bf16[48,2048]{1,0:T(8,128)(2,1)S(1)}, u32[]{:S(2)}, u32[]{:S(2)}) collective-permute-start(bf16[48,2048]{1,0:T(8,128)(2,1)S(1)} %get-tuple-element.127), channel_id=1, source_target_pairs={{0,2},{1,3},{2,0},{3,1},{4,6},{5,7},{6,4},{7,5},{8,10},{9,11},{10,... | collective-permute-start | bytes 589832 | tf_op jit(solution)/shard_map/ppermute | solution.py:26
  103.3 2.6 %collective-permute-done.19.refs_1_ = bf16[48,2048]{1,0:T(8,128)(2,1)S(1)} collective-permute-done((bf16[48,2048]{1,0:T(8,128)(2,1)S(1)}, bf16[48,2048]{1,0:T(8,128)(2,1)S(1)}, u32[]{:S(2)}, u32[]{:S(2)}) %collective-permute-start.19) | collective-permute-done | bytes 196640 | tf_op jit(solution)/shard_map/ppermute | solution.py:26
  108.2 4.1 %cache.1 = bf16[1,8,64,1024]{3,2,1,0:T(8,128)(2,1)} custom-call(bf16[256,2048]{1,0:T(8,128)(2,1)S(1)} %join.3.mine_ref, bf16[256,2048]{1,0:T(8,128)(2,1)S(1)} %collective-permute-done.17.theirs_ref, bf16[2,2048]{1,0:T(2,128)(2,1)S(1)} %pad_maximum_fusion.refs_2_.refs_1_.gain.gain_ref, bf16[2048,1536]{1,0:T(8,128)(2,1)S(1)} %bitcast.14), custom_call_target="tpu_custom_call" | custom-call | tf_op jit(solution)/shard_map/cache/pallas_call | solution.py:38
  112.4 5.2 %collective-permute-done.22.refs_3_ = bf16[48,2048]{1,0:T(8,128)(2,1)S(1)} collective-permute-done((bf16[48,2048]{1,0:T(8,128)(2,1)S(1)}, bf16[48,2048]{1,0:T(8,128)(2,1)S(1)}, u32[]{:S(2)}, u32[]{:S(2)}) %collective-permute-start.22) | collective-permute-done | bytes 196640 | tf_op jit(solution)/shard_map/ppermute | solution.py:26
  (68 shorter events, 22.1 us)
Async XLA Ops:
  1.5 21.9 %collective-permute-start.4 = (bf16[512,2048]{1,0:T(8,128)(2,1)}, bf16[512,2048]{1,0:T(8,128)(2,1)S(1)}, u32[]{:S(2)}, u32[]{:S(2)}) collective-permute-start(bf16[512,2048]{1,0:T(8,128)(2,1)} %bitcast.15), channel_id=1, source_target_pairs={{0,8},{8,0},{16,24},{24,16},{1,9},{9,1},{17,25},{25,17},{2,10},{10... | collective-permute-start | bytes 6291464 | tf_op jit(solution)/shard_map/ppermute | solution.py:26
  2.0 8.4 %collective-permute-start.1 = (bf16[128,2048]{1,0:T(8,128)(2,1)}, bf16[128,2048]{1,0:T(8,128)(2,1)S(1)}, u32[]{:S(2)}, u32[]{:S(2)}) collective-permute-start(bf16[128,2048]{1,0:T(8,128)(2,1)} %bitcast.18), channel_id=1, source_target_pairs={{0,8},{8,0},{16,24},{24,16},{1,9},{9,1},{17,25},{25,17},{2,10},{10... | collective-permute-start | bytes 1572872 | tf_op jit(solution)/shard_map/ppermute | solution.py:26
  2.1 15.3 %collective-permute-start = (bf16[128,2048]{1,0:T(8,128)(2,1)}, bf16[128,2048]{1,0:T(8,128)(2,1)S(1)}, u32[]{:S(2)}, u32[]{:S(2)}) collective-permute-start(bf16[128,2048]{1,0:T(8,128)(2,1)} %bitcast.19), channel_id=1, source_target_pairs={{0,16},{8,24},{16,0},{24,8},{1,17},{9,25},{17,1},{25,9},{2,18},{10... | collective-permute-start | bytes 1572872 | tf_op jit(solution)/shard_map/ppermute | solution.py:26
  17.4 1.9 %collective-permute-start.2 = (bf16[128,2048]{1,0:T(8,128)(2,1)S(1)}, bf16[128,2048]{1,0:T(8,128)(2,1)S(1)}, u32[]{:S(2)}, u32[]{:S(2)}) collective-permute-start(bf16[128,2048]{1,0:T(8,128)(2,1)S(1)} %collective-permute-done.refs_0_.refs_2_), channel_id=1, source_target_pairs={{0,8},{8,0},{16,24},{24,16},{1,9},{9,1},{17,25},{25,17},{2,10},{10... | collective-permute-start | bytes 1572872 | tf_op jit(solution)/shard_map/ppermute | solution.py:26
  22.0 1.4 %collective-permute-start.3 = (bf16[128,512]{1,0:T(8,128)(2,1)S(1)}, bf16[128,512]{1,0:T(8,128)(2,1)S(1)}, u32[]{:S(2)}, u32[]{:S(2)}) collective-permute-start(bf16[128,512]{1,0:T(8,128)(2,1)S(1)} %get-tuple-element.76), channel_id=1, source_target_pairs={{0,8},{8,0},{16,24},{24,16},{1,9},{9,1},{17,25},{25,17},{2,10},{10... | collective-permute-start | bytes 393224 | tf_op jit(solution)/shard_map/ppermute | solution.py:26
  24.1 11.6 %collective-permute-start.6 = (bf16[64,2048]{1,0:T(8,128)(2,1)S(1)}, bf16[64,2048]{1,0:T(8,128)(2,1)S(1)}, u32[]{:S(2)}, u32[]{:S(2)}) collective-permute-start(bf16[64,2048]{1,0:T(8,128)(2,1)S(1)} %get-tuple-element.84), channel_id=1, source_target_pairs={{0,0},{1,1},{2,2},{3,3},{4,4},{5,5},{6,6},{7,7},{8,9},{9,8},{10,11... | collective-permute-start | bytes 786440 | tf_op jit(solution)/shard_map/ppermute | solution.py:283
  25.0 14.3 %collective-permute-start.7 = (bf16[64,2048]{1,0:T(8,128)(2,1)S(1)}, bf16[64,2048]{1,0:T(8,128)(2,1)S(1)}, u32[]{:S(2)}, u32[]{:S(2)}) collective-permute-start(bf16[64,2048]{1,0:T(8,128)(2,1)S(1)} %get-tuple-element.85), channel_id=1, source_target_pairs={{0,4},{1,5},{2,6},{3,7},{4,0},{5,1},{6,2},{7,3},{8,13},{9,12},{10,... | collective-permute-start | bytes 786440 | tf_op jit(solution)/shard_map/ppermute | solution.py:283
  27.9 16.8 %collective-permute-start.5 = (bf16[128,2048]{1,0:T(8,128)(2,1)S(1)}, bf16[128,2048]{1,0:T(8,128)(2,1)S(1)}, u32[]{:S(2)}, u32[]{:S(2)}) collective-permute-start(bf16[128,2048]{1,0:T(8,128)(2,1)S(1)} %out_project.2), channel_id=1, source_target_pairs={{0,16},{8,24},{16,0},{24,8},{1,17},{9,25},{17,1},{25,9},{2,18},{10... | collective-permute-start | bytes 1572872 | tf_op jit(solution)/shard_map/ppermute | solution.py:26
  45.3 16.7 %collective-permute-start.12 = (bf16[48,2048]{1,0:T(8,128)(2,1)S(1)}, bf16[48,2048]{1,0:T(8,128)(2,1)S(1)}, u32[]{:S(2)}, u32[]{:S(2)}) collective-permute-start(bf16[48,2048]{1,0:T(8,128)(2,1)S(1)} %get-tuple-element.100), channel_id=1, source_target_pairs={{0,4},{1,5},{2,6},{3,7},{4,0},{5,1},{6,2},{7,3},{8,12},{9,13},{10,... | collective-permute-start | bytes 589832 | tf_op jit(solution)/shard_map/ppermute | solution.py:26
  45.6 21.0 %collective-permute-start.13 = (bf16[48,2048]{1,0:T(8,128)(2,1)S(1)}, bf16[48,2048]{1,0:T(8,128)(2,1)S(1)}, u32[]{:S(2)}, u32[]{:S(2)}) collective-permute-start(bf16[48,2048]{1,0:T(8,128)(2,1)S(1)} %get-tuple-element.101), channel_id=1, source_target_pairs={{0,5},{1,4},{2,7},{3,6},{4,1},{5,0},{6,3},{7,2},{8,13},{9,12},{10,... | collective-permute-start | bytes 589832 | tf_op jit(solution)/shard_map/ppermute | solution.py:26
  49.3 27.3 %collective-permute-start.14 = (bf16[128,2048]{1,0:T(8,128)(2,1)S(1)}, bf16[128,2048]{1,0:T(8,128)(2,1)S(1)}, u32[]{:S(2)}, u32[]{:S(2)}) collective-permute-start(bf16[128,2048]{1,0:T(8,128)(2,1)S(1)} %join.2.refs_0_), channel_id=1, source_target_pairs={{0,16},{8,24},{16,0},{24,8},{1,17},{9,25},{17,1},{25,9},{2,18},{10... | collective-permute-start | bytes 1572872 | tf_op jit(solution)/shard_map/ppermute | solution.py:26
  51.5 18.5 %collective-permute-start.9 = (bf16[48,2048]{1,0:T(8,128)(2,1)S(1)}, bf16[48,2048]{1,0:T(8,128)(2,1)S(1)}, u32[]{:S(2)}, u32[]{:S(2)}) collective-permute-start(bf16[48,2048]{1,0:T(8,128)(2,1)S(1)} %get-tuple-element.97), channel_id=1, source_target_pairs={{0,1},{1,0},{2,3},{3,2},{4,5},{5,4},{6,7},{7,6},{8,9},{9,8},{10,11... | collective-permute-start | bytes 589832 | tf_op jit(solution)/shard_map/ppermute | solution.py:26
  52.1 20.6 %collective-permute-start.10 = (bf16[48,2048]{1,0:T(8,128)(2,1)S(1)}, bf16[48,2048]{1,0:T(8,128)(2,1)S(1)}, u32[]{:S(2)}, u32[]{:S(2)}) collective-permute-start(bf16[48,2048]{1,0:T(8,128)(2,1)S(1)} %get-tuple-element.98), channel_id=1, source_target_pairs={{0,2},{1,3},{2,0},{3,1},{4,6},{5,7},{6,4},{7,5},{8,10},{9,11},{10,... | collective-permute-start | bytes 589832 | tf_op jit(solution)/shard_map/ppermute | solution.py:26
  62.0 13.0 %collective-permute-start.11 = (bf16[48,2048]{1,0:T(8,128)(2,1)S(1)}, bf16[48,2048]{1,0:T(8,128)(2,1)S(1)}, u32[]{:S(2)}, u32[]{:S(2)}) collective-permute-start(bf16[48,2048]{1,0:T(8,128)(2,1)S(1)} %get-tuple-element.99), channel_id=1, source_target_pairs={{0,3},{1,2},{2,1},{3,0},{4,7},{5,6},{6,5},{7,4},{8,11},{9,10},{10,... | collective-permute-start | bytes 589832 | tf_op jit(solution)/shard_map/ppermute | solution.py:26
  66.7 12.8 %collective-permute-start.15 = (bf16[48,2048]{1,0:T(8,128)(2,1)S(1)}, bf16[48,2048]{1,0:T(8,128)(2,1)S(1)}, u32[]{:S(2)}, u32[]{:S(2)}) collective-permute-start(bf16[48,2048]{1,0:T(8,128)(2,1)S(1)} %get-tuple-element.113), channel_id=1, source_target_pairs={{0,6},{1,7},{2,4},{3,5},{4,2},{5,3},{6,0},{7,1},{8,14},{9,15},{10,... | collective-permute-start | bytes 589832 | tf_op jit(solution)/shard_map/ppermute | solution.py:26
  70.1 10.6 %collective-permute-start.16 = (bf16[48,2048]{1,0:T(8,128)(2,1)S(1)}, bf16[48,2048]{1,0:T(8,128)(2,1)S(1)}, u32[]{:S(2)}, u32[]{:S(2)}) collective-permute-start(bf16[48,2048]{1,0:T(8,128)(2,1)S(1)} %get-tuple-element.114), channel_id=1, source_target_pairs={{0,7},{1,6},{2,5},{3,4},{4,3},{5,2},{6,1},{7,0},{8,15},{9,14},{10,... | collective-permute-start | bytes 589832 | tf_op jit(solution)/shard_map/ppermute | solution.py:26
  72.7 29.1 %collective-permute-start.18 = (bf16[48,2048]{1,0:T(8,128)(2,1)S(1)}, bf16[48,2048]{1,0:T(8,128)(2,1)S(1)}, u32[]{:S(2)}, u32[]{:S(2)}) collective-permute-start(bf16[48,2048]{1,0:T(8,128)(2,1)S(1)} %get-tuple-element.102), channel_id=1, source_target_pairs={{0,4},{1,5},{2,6},{3,7},{4,0},{5,1},{6,2},{7,3},{8,12},{9,13},{10,... | collective-permute-start | bytes 589832 | tf_op jit(solution)/shard_map/ppermute | solution.py:26
  75.0 30.9 %collective-permute-start.19 = (bf16[48,2048]{1,0:T(8,128)(2,1)S(1)}, bf16[48,2048]{1,0:T(8,128)(2,1)S(1)}, u32[]{:S(2)}, u32[]{:S(2)}) collective-permute-start(bf16[48,2048]{1,0:T(8,128)(2,1)S(1)} %get-tuple-element.103), channel_id=1, source_target_pairs={{0,5},{1,4},{2,7},{3,6},{4,1},{5,0},{6,3},{7,2},{8,13},{9,12},{10,... | collective-permute-start | bytes 589832 | tf_op jit(solution)/shard_map/ppermute | solution.py:26
  76.7 4.0 %collective-permute-start.17 = (bf16[256,2048]{1,0:T(8,128)(2,1)S(1)}, bf16[256,2048]{1,0:T(8,128)(2,1)S(1)}, u32[]{:S(2)}, u32[]{:S(2)}) collective-permute-start(bf16[256,2048]{1,0:T(8,128)(2,1)S(1)} %join.3.mine_ref), channel_id=1, source_target_pairs={{0,8},{8,0},{16,24},{24,16},{1,9},{9,1},{17,25},{25,17},{2,10},{10... | collective-permute-start | bytes 3145736 | tf_op jit(solution)/shard_map/ppermute | solution.py:26
  82.8 34.8 %collective-permute-start.23 = (bf16[48,2048]{1,0:T(8,128)(2,1)S(1)}, bf16[48,2048]{1,0:T(8,128)(2,1)S(1)}, u32[]{:S(2)}, u32[]{:S(2)}) collective-permute-start(bf16[48,2048]{1,0:T(8,128)(2,1)S(1)} %get-tuple-element.117), channel_id=1, source_target_pairs={{0,6},{1,7},{2,4},{3,5},{4,2},{5,3},{6,0},{7,1},{8,14},{9,15},{10,... | collective-permute-start | bytes 589832 | tf_op jit(solution)/shard_map/ppermute | solution.py:26
  85.6 26.8 %collective-permute-start.20 = (bf16[48,2048]{1,0:T(8,128)(2,1)S(1)}, bf16[48,2048]{1,0:T(8,128)(2,1)S(1)}, u32[]{:S(2)}, u32[]{:S(2)}) collective-permute-start(bf16[48,2048]{1,0:T(8,128)(2,1)S(1)} %get-tuple-element.126), channel_id=1, source_target_pairs={{0,1},{1,0},{2,3},{3,2},{4,5},{5,4},{6,7},{7,6},{8,9},{9,8},{10,11... | collective-permute-start | bytes 589832 | tf_op jit(solution)/shard_map/ppermute | solution.py:26
  86.1 26.2 %collective-permute-start.21 = (bf16[48,2048]{1,0:T(8,128)(2,1)S(1)}, bf16[48,2048]{1,0:T(8,128)(2,1)S(1)}, u32[]{:S(2)}, u32[]{:S(2)}) collective-permute-start(bf16[48,2048]{1,0:T(8,128)(2,1)S(1)} %get-tuple-element.127), channel_id=1, source_target_pairs={{0,2},{1,3},{2,0},{3,1},{4,6},{5,7},{6,4},{7,5},{8,10},{9,11},{10,... | collective-permute-start | bytes 589832 | tf_op jit(solution)/shard_map/ppermute | solution.py:26
  101.8 15.8 %collective-permute-start.22 = (bf16[48,2048]{1,0:T(8,128)(2,1)S(1)}, bf16[48,2048]{1,0:T(8,128)(2,1)S(1)}, u32[]{:S(2)}, u32[]{:S(2)}) collective-permute-start(bf16[48,2048]{1,0:T(8,128)(2,1)S(1)} %get-tuple-element.128), channel_id=1, source_target_pairs={{0,3},{1,2},{2,1},{3,0},{4,7},{5,6},{6,5},{7,4},{8,11},{9,10},{10,... | collective-permute-start | bytes 589832 | tf_op jit(solution)/shard_map/ppermute | solution.py:26
  105.9 11.7 %collective-permute-start.24 = (bf16[48,2048]{1,0:T(8,128)(2,1)S(1)}, bf16[48,2048]{1,0:T(8,128)(2,1)S(1)}, u32[]{:S(2)}, u32[]{:S(2)}) collective-permute-start(bf16[48,2048]{1,0:T(8,128)(2,1)S(1)} %get-tuple-element.118), channel_id=1, source_target_pairs={{0,7},{1,6},{2,5},{3,4},{4,3},{5,2},{6,1},{7,0},{8,15},{9,14},{10,... | collective-permute-start | bytes 589832 | tf_op jit(solution)/shard_map/ppermute | solution.py:26
  (10 other events, 109.1 us)

commit v5 on v4

--- a/solution.py
+++ b/solution.py
@@ -472,8 +472,7 @@
 
     far = swap(own, "seq", 2)
     w_mine = w_out.reshape(heads_here * head_dim, width)
-    picks, w_mine, to_core = lax.optimization_barrier((picks, w_mine, own))
-    core = swap(to_core, "seq", 1)
+    core = swap(own, "seq", 1)
     w_theirs = swap(w_mine, "seq", 1)
     gains = jnp.stack([attn_gain, ffn_gain])
 
@@ -490,10 +489,10 @@
     outgoing = pages_out(page_owner, (own, core, far, far_core))
     theirs_far, outgoing = lax.optimization_barrier((theirs_far, outgoing))
     far_sum = out_project(keep_far, theirs_far, w_mine, w_theirs, BF16)
-    far_sum, outgoing = lax.optimization_barrier((far_sum, outgoing))
     from_far = swap(far_sum, "seq", 2)
+    keep, send = attend_near(segment_ids, q_near, (kv_near, kv_far, kv_last), head_dim)
+    send, outgoing = lax.optimization_barrier((send, outgoing))
     arrived = [to_owner(page, k) for k, page in enumerate(outgoing)]
-    keep, send = attend_near(segment_ids, q_near, (kv_near, kv_far, kv_last), head_dim)
     mixed = out_project(keep, swap(send, "seq", 1), w_mine, w_theirs, F32)
 
     gate_up, down = held(w_gate_up[0]), held(w_down[0])
@@ -505,11 +504,11 @@
     def work(blocks):
         return expert([full(block) for block in blocks], gate_up, down)
 
-    from_far, arrived = lax.optimization_barrier((from_far, arrived))
     resid, ffn_in, *sent_first = dispatch(own, mixed, from_far, gains, picks[0], len(first))
     rows_first = there(first, sent_first)
     sent = dispatch_more(ffn_in, picks[1], (slots,) * len(groups[1]))
     sent_near, sent_last = sent[: len(near)], sent[len(near) :]
+    sent_near, arrived = lax.optimization_barrier((sent_near, arrived))
     rows_near = there(near, sent_near)
     share = join([full(page) for page in arrived])
     share_far = swap(share, "seq", 2)

time: 119 us -> 115 us (0.966)
  starting transfers between devices: 46.4 us -> 41 us
  waiting for transfers between devices: 40.4 us -> 42 us
    ppermute x23, starting transfers between devices: 42.6 us -> 37.5 us  [swap(): return lax.ppermute(value, axis, [(i, i ^ step) for i in range(size)])]
    ppermute x2, waiting for transfers between devices: 3.6 us -> 8.14 us  [to_owner(): return lax.ppermute(page, ('seq', 'blk'), pairs)]
    ppermute x23, waiting for transfers between devices: 36.8 us -> 33.9 us  [swap(): return lax.ppermute(value, axis, [(i, i ^ step) for i in range(size)])]
  transfers between devices with their start and end apart: 25 -> 25, of which waited for: 12 -> 11; matrix products, arithmetic and copies ran while one was open for 5% -> 5% of each run, Pallas kernels for 19% -> 20%
where the time goes in v5:
time: 115 us; the launch traced here: 114 us
  waiting for transfers between devices  42 us (37%)
  starting transfers between devices  41 us (36%)
  Pallas kernels  25 us (22%)
  local copies, waits for them, and re-layouts  5.43 us (5%)
    ppermute x23, starting transfers between devices, swap(): return lax.ppermute(value, axis, [(i, i ^ step) for i in range(size)])  37.5 us
    ppermute x23, waiting for transfers between devices, swap(): return lax.ppermute(value, axis, [(i, i ^ step) for i in range(size)])  33.9 us
    pallas_call x19, Pallas kernels, call(): pl.pallas_call(kernel, out_shape=out_shape, in_specs=[SMEM_SPEC] * scalar...  25 us
    ppermute x2, waiting for transfers between devices, to_owner(): return lax.ppermute(page, ('seq', 'blk'), pairs)  8.14 us
    unnamed x19, local copies, waits for them, and re-layouts  4.05 us
    ppermute x2, starting transfers between devices, to_owner(): return lax.ppermute(page, ('seq', 'blk'), pairs)  3.51 us
  transfers between devices with their start and end apart: 25, of which 11 were waited for; matrix products, arithmetic and copies ran while one was open for 5% of the time, Pallas kernels for 20%

profile of v5, /device:TPU:0, one launch (start us, length us, event | category | flops | bytes accessed | tf_op | source)
XLA Modules:
  0.0 114.4 jit_solution(9460378242302850945)
XLA Ops:
  1.2 2.9 %collective-permute-start = (bf16[128,2048]{1,0:T(8,128)(2,1)}, bf16[128,2048]{1,0:T(8,128)(2,1)S(1)}, u32[]{:S(2)}, u32[]{:S(2)}) collective-permute-start(bf16[128,2048]{1,0:T(8,128)(2,1)} %bitcast.19), channel_id=1, source_target_pairs={{0,16},{8,24},{16,0},{24,8},{1,17},{9,25},{17,1},{25,9},{2,18},{10... | collective-permute-start | bytes 1572872 | tf_op jit(solution)/shard_map/ppermute | solution.py:26
  5.5 4.0 %copy.13 = bf16[256,8,4,384]{3,1,2,0:T(8,128)(2,1)S(1)} copy(bf16[256,8,4,384]{3,2,1,0:T(4,128)(2,1)} %bitcast.33) | data formatting | bytes 12582912
  9.6 2.6 %project.2 = (bf16[256,512]{1,0:T(8,128)(2,1)S(1)}, bf16[256,1024]{1,0:T(8,128)(2,1)S(1)}) custom-call(bf16[128,2048]{1,0:T(8,128)(2,1)S(1)} %bitcast.20, bf16[128,2048]{1,0:T(8,128)(2,1)S(1)} %collective-permute-done.1.refs_1_, bf16[2,2048]{1,0:T(2,128)(2,1)S(1)} %pad_maximum_fusion.refs_2_.refs_1_.gain.gain_ref, bf16[2048,1536]{1,0:T(8,128)(2,1)S(1)} %bitcast.11), custom_call_target="tpu_custom_call" | custom-call | tf_op jit(solution)/shard_map/project/pallas_call | solution.py:38
  12.2 4.3 %collective-permute-done.refs_0_.refs_2_ = bf16[128,2048]{1,0:T(8,128)(2,1)S(1)} collective-permute-done((bf16[128,2048]{1,0:T(8,128)(2,1)}, bf16[128,2048]{1,0:T(8,128)(2,1)S(1)}, u32[]{:S(2)}, u32[]{:S(2)}) %collective-permute-start) | collective-permute-done | bytes 524320 | tf_op jit(solution)/shard_map/ppermute | solution.py:26
  18.4 2.7 %attend_far.1 = (bf16[128,512]{1,0:T(8,128)(2,1)S(1)}, bf16[128,512]{1,0:T(8,128)(2,1)S(1)}, bf16[128,1024]{1,0:T(8,128)(2,1)S(1)}) custom-call(s32[1,512]{1,0:T(1,128)S(1)} %copy-done.3, bf16[128,512]{1,0:T(8,128)(2,1)S(1)} %get-tuple-element.71.q_far, bf16[256,1024]{1,0:T(8,128)(2,1)S(1)} %get-tuple-element.68.kv_near, ...), custom_call_target="tpu_custom_call" | custom-call | tf_op jit(solution)/shard_map/attend_far/pallas_call | solution.py:38
  23.3 1.8 %collective-permute-start.6 = (bf16[128,2048]{1,0:T(8,128)(2,1)S(1)}, bf16[128,2048]{1,0:T(8,128)(2,1)S(1)}, u32[]{:S(2)}, u32[]{:S(2)}) collective-permute-start(bf16[128,2048]{1,0:T(8,128)(2,1)S(1)} %out_project.3), channel_id=1, source_target_pairs={{0,16},{8,24},{16,0},{24,8},{1,17},{9,25},{17,1},{25,9},{2,18},{10... | collective-permute-start | bytes 1572872 | tf_op jit(solution)/shard_map/ppermute | solution.py:26
  27.7 2.7 %collective-permute-start.8 = (bf16[64,2048]{1,0:T(8,128)(2,1)S(1)}, bf16[64,2048]{1,0:T(8,128)(2,1)S(1)}, u32[]{:S(2)}, u32[]{:S(2)}) collective-permute-start(bf16[64,2048]{1,0:T(8,128)(2,1)S(1)} %get-tuple-element.91), channel_id=1, source_target_pairs={{0,4},{1,5},{2,6},{3,7},{4,0},{5,1},{6,2},{7,3},{8,13},{9,12},{10,... | collective-permute-start | bytes 786440 | tf_op jit(solution)/shard_map/ppermute | solution.py:283
  31.1 6.2 %collective-permute-done.6.far_ref = bf16[128,2048]{1,0:T(8,128)(2,1)S(1)} collective-permute-done((bf16[128,2048]{1,0:T(8,128)(2,1)S(1)}, bf16[128,2048]{1,0:T(8,128)(2,1)S(1)}, u32[]{:S(2)}, u32[]{:S(2)}) %collective-permute-start.6) | collective-permute-done | bytes 524320 | tf_op jit(solution)/shard_map/ppermute | solution.py:26
  38.0 2.9 %collective-permute-start.12 = (bf16[48,2048]{1,0:T(8,128)(2,1)S(1)}, bf16[48,2048]{1,0:T(8,128)(2,1)S(1)}, u32[]{:S(2)}, u32[]{:S(2)}) collective-permute-start(bf16[48,2048]{1,0:T(8,128)(2,1)S(1)} %get-tuple-element.98), channel_id=1, source_target_pairs={{0,4},{1,5},{2,6},{3,7},{4,0},{5,1},{6,2},{7,3},{8,12},{9,13},{10,... | collective-permute-start | bytes 589832 | tf_op jit(solution)/shard_map/ppermute | solution.py:26
  42.6 8.1 %collective-permute-done.8.refs_1_ = bf16[64,2048]{1,0:T(8,128)(2,1)S(1)} collective-permute-done((bf16[64,2048]{1,0:T(8,128)(2,1)S(1)}, bf16[64,2048]{1,0:T(8,128)(2,1)S(1)}, u32[]{:S(2)}, u32[]{:S(2)}) %collective-permute-start.8) | collective-permute-done | bytes 262176 | tf_op jit(solution)/shard_map/ppermute | solution.py:283
  55.0 4.6 %collective-permute-start.15 = (bf16[48,2048]{1,0:T(8,128)(2,1)S(1)}, bf16[48,2048]{1,0:T(8,128)(2,1)S(1)}, u32[]{:S(2)}, u32[]{:S(2)}) collective-permute-start(bf16[48,2048]{1,0:T(8,128)(2,1)S(1)} %get-tuple-element.111), channel_id=1, source_target_pairs={{0,6},{1,7},{2,4},{3,5},{4,2},{5,3},{6,0},{7,1},{8,14},{9,15},{10,... | collective-permute-start | bytes 589832 | tf_op jit(solution)/shard_map/ppermute | solution.py:26
  60.3 3.7 %collective-permute-start.14 = (bf16[128,2048]{1,0:T(8,128)(2,1)S(1)}, bf16[128,2048]{1,0:T(8,128)(2,1)S(1)}, u32[]{:S(2)}, u32[]{:S(2)}) collective-permute-start(bf16[128,2048]{1,0:T(8,128)(2,1)S(1)} %join.2.refs_0_), channel_id=1, source_target_pairs={{0,16},{8,24},{16,0},{24,8},{1,17},{9,25},{17,1},{25,9},{2,18},{10... | collective-permute-start | bytes 1572872 | tf_op jit(solution)/shard_map/ppermute | solution.py:26
  64.1 2.2 %expert.3 = (bf16[48,2048]{1,0:T(8,128)(2,1)S(1)}, bf16[48,2048]{1,0:T(8,128)(2,1)S(1)}) custom-call(bf16[48,2048]{1,0:T(8,128)(2,1)S(1)} %collective-permute-done.12.refs_0_, bf16[48,2048]{1,0:T(8,128)(2,1)S(1)} %collective-permute-done.13.refs_1_, bf16[2048,2048]{1,0:T(8,128)(2,1)S(1)} %bitcast.26, bf16[1024,2048]{1,0:T(8,128)(2,1)S(1)} %bitcast.29), custom_call_target="tpu_custom_call" | custom-call | flops 34359738368 | tf_op jit(solution)/shard_map/expert/pallas_call | solution.py:38
  66.3 3.2 %collective-permute-start.16 = (bf16[48,2048]{1,0:T(8,128)(2,1)S(1)}, bf16[48,2048]{1,0:T(8,128)(2,1)S(1)}, u32[]{:S(2)}, u32[]{:S(2)}) collective-permute-start(bf16[48,2048]{1,0:T(8,128)(2,1)S(1)} %get-tuple-element.112), channel_id=1, source_target_pairs={{0,7},{1,6},{2,5},{3,4},{4,3},{5,2},{6,1},{7,0},{8,15},{9,14},{10,... | collective-permute-start | bytes 589832 | tf_op jit(solution)/shard_map/ppermute | solution.py:26
  70.5 7.6 %collective-permute-done.11.refs_3_ = bf16[48,2048]{1,0:T(8,128)(2,1)S(1)} collective-permute-done((bf16[48,2048]{1,0:T(8,128)(2,1)S(1)}, bf16[48,2048]{1,0:T(8,128)(2,1)S(1)}, u32[]{:S(2)}, u32[]{:S(2)}) %collective-permute-start.11) | collective-permute-done | bytes 196640 | tf_op jit(solution)/shard_map/ppermute | solution.py:26
  79.9 2.7 %expert.4 = (bf16[48,2048]{1,0:T(8,128)(2,1)S(1)}, bf16[48,2048]{1,0:T(8,128)(2,1)S(1)}, bf16[48,2048]{1,0:T(8,128)(2,1)S(1)}, bf16[48,2048]{1,0:T(8,128)(2,1)S(1)}) custom-call(bf16[48,2048]{1,0:T(8,128)(2,1)S(1)} %get-tuple-element.103.refs_0_, bf16[48,2048]{1,0:T(8,128)(2,1)S(1)} %collective-permute-done.9.refs_1_, ...), custom_call_target="tpu_custom_call" | custom-call | flops 34359738368 | tf_op jit(solution)/shard_map/expert/pallas_call | solution.py:38
  82.6 2.2 %expert.5 = (bf16[48,2048]{1,0:T(8,128)(2,1)S(1)}, bf16[48,2048]{1,0:T(8,128)(2,1)S(1)}) custom-call(bf16[48,2048]{1,0:T(8,128)(2,1)S(1)} %collective-permute-done.15.refs_0_, bf16[48,2048]{1,0:T(8,128)(2,1)S(1)} %collective-permute-done.16.refs_1_, bf16[2048,2048]{1,0:T(8,128)(2,1)S(1)} %bitcast.28, bf16[1024,2048]{1,0:T(8,128)(2,1)S(1)} %bitcast.31), custom_call_target="tpu_custom_call" | custom-call | flops 34359738368 | tf_op jit(solution)/shard_map/expert/pallas_call | solution.py:38
  84.8 2.0 %collective-permute-start.23 = (bf16[48,2048]{1,0:T(8,128)(2,1)S(1)}, bf16[48,2048]{1,0:T(8,128)(2,1)S(1)}, u32[]{:S(2)}, u32[]{:S(2)}) collective-permute-start(bf16[48,2048]{1,0:T(8,128)(2,1)S(1)} %get-tuple-element.115), channel_id=1, source_target_pairs={{0,6},{1,7},{2,4},{3,5},{4,2},{5,3},{6,0},{7,1},{8,14},{9,15},{10,... | collective-permute-start | bytes 589832 | tf_op jit(solution)/shard_map/ppermute | solution.py:26
  87.3 5.2 %collective-permute-start.21 = (bf16[48,2048]{1,0:T(8,128)(2,1)S(1)}, bf16[48,2048]{1,0:T(8,128)(2,1)S(1)}, u32[]{:S(2)}, u32[]{:S(2)}) collective-permute-start(bf16[48,2048]{1,0:T(8,128)(2,1)S(1)} %get-tuple-element.125), channel_id=1, source_target_pairs={{0,2},{1,3},{2,0},{3,1},{4,6},{5,7},{6,4},{7,5},{8,10},{9,11},{10,... | collective-permute-start | bytes 589832 | tf_op jit(solution)/shard_map/ppermute | solution.py:26
  92.5 3.0 %collective-permute-done.18.refs_0_ = bf16[48,2048]{1,0:T(8,128)(2,1)S(1)} collective-permute-done((bf16[48,2048]{1,0:T(8,128)(2,1)S(1)}, bf16[48,2048]{1,0:T(8,128)(2,1)S(1)}, u32[]{:S(2)}, u32[]{:S(2)}) %collective-permute-start.18) | collective-permute-done | bytes 196640 | tf_op jit(solution)/shard_map/ppermute | solution.py:26
  95.7 4.9 %collective-permute-done.19.refs_1_ = bf16[48,2048]{1,0:T(8,128)(2,1)S(1)} collective-permute-done((bf16[48,2048]{1,0:T(8,128)(2,1)S(1)}, bf16[48,2048]{1,0:T(8,128)(2,1)S(1)}, u32[]{:S(2)}, u32[]{:S(2)}) %collective-permute-start.19) | collective-permute-done | bytes 196640 | tf_op jit(solution)/shard_map/ppermute | solution.py:26
  100.6 2.1 %collective-permute-start.24 = (bf16[48,2048]{1,0:T(8,128)(2,1)S(1)}, bf16[48,2048]{1,0:T(8,128)(2,1)S(1)}, u32[]{:S(2)}, u32[]{:S(2)}) collective-permute-start(bf16[48,2048]{1,0:T(8,128)(2,1)S(1)} %get-tuple-element.116), channel_id=1, source_target_pairs={{0,7},{1,6},{2,5},{3,4},{4,3},{5,2},{6,1},{7,0},{8,15},{9,14},{10,... | collective-permute-start | bytes 589832 | tf_op jit(solution)/shard_map/ppermute | solution.py:26
  103.5 4.1 %cache.1 = bf16[1,8,64,1024]{3,2,1,0:T(8,128)(2,1)} custom-call(bf16[256,2048]{1,0:T(8,128)(2,1)S(1)} %join.3.mine_ref, bf16[256,2048]{1,0:T(8,128)(2,1)S(1)} %collective-permute-done.17.theirs_ref, bf16[2,2048]{1,0:T(2,128)(2,1)S(1)} %pad_maximum_fusion.refs_2_.refs_1_.gain.gain_ref, bf16[2048,1536]{1,0:T(8,128)(2,1)S(1)} %bitcast.14), custom_call_target="tpu_custom_call" | custom-call | tf_op jit(solution)/shard_map/cache/pallas_call | solution.py:38
  107.7 5.5 %collective-permute-done.22.refs_3_ = bf16[48,2048]{1,0:T(8,128)(2,1)S(1)} collective-permute-done((bf16[48,2048]{1,0:T(8,128)(2,1)S(1)}, bf16[48,2048]{1,0:T(8,128)(2,1)S(1)}, u32[]{:S(2)}, u32[]{:S(2)}) %collective-permute-start.22) | collective-permute-done | bytes 196640 | tf_op jit(solution)/shard_map/ppermute | solution.py:26
  (68 shorter events, 22.2 us)
Async XLA Ops:
  0.6 22.0 %collective-permute-start.5 = (bf16[512,2048]{1,0:T(8,128)(2,1)}, bf16[512,2048]{1,0:T(8,128)(2,1)S(1)}, u32[]{:S(2)}, u32[]{:S(2)}) collective-permute-start(bf16[512,2048]{1,0:T(8,128)(2,1)} %bitcast.15), channel_id=1, source_target_pairs={{0,8},{8,0},{16,24},{24,16},{1,9},{9,1},{17,25},{25,17},{2,10},{10... | collective-permute-start | bytes 6291464 | tf_op jit(solution)/shard_map/ppermute | solution.py:26
  1.1 8.4 %collective-permute-start.1 = (bf16[128,2048]{1,0:T(8,128)(2,1)}, bf16[128,2048]{1,0:T(8,128)(2,1)S(1)}, u32[]{:S(2)}, u32[]{:S(2)}) collective-permute-start(bf16[128,2048]{1,0:T(8,128)(2,1)} %bitcast.18), channel_id=1, source_target_pairs={{0,8},{8,0},{16,24},{24,16},{1,9},{9,1},{17,25},{25,17},{2,10},{10... | collective-permute-start | bytes 1572872 | tf_op jit(solution)/shard_map/ppermute | solution.py:26
  1.2 15.3 %collective-permute-start = (bf16[128,2048]{1,0:T(8,128)(2,1)}, bf16[128,2048]{1,0:T(8,128)(2,1)S(1)}, u32[]{:S(2)}, u32[]{:S(2)}) collective-permute-start(bf16[128,2048]{1,0:T(8,128)(2,1)} %bitcast.19), channel_id=1, source_target_pairs={{0,16},{8,24},{16,0},{24,8},{1,17},{9,25},{17,1},{25,9},{2,18},{10... | collective-permute-start | bytes 1572872 | tf_op jit(solution)/shard_map/ppermute | solution.py:26
  16.5 1.9 %collective-permute-start.2 = (bf16[128,2048]{1,0:T(8,128)(2,1)S(1)}, bf16[128,2048]{1,0:T(8,128)(2,1)S(1)}, u32[]{:S(2)}, u32[]{:S(2)}) collective-permute-start(bf16[128,2048]{1,0:T(8,128)(2,1)S(1)} %collective-permute-done.refs_0_.refs_2_), channel_id=1, source_target_pairs={{0,8},{8,0},{16,24},{24,16},{1,9},{9,1},{17,25},{25,17},{2,10},{10... | collective-permute-start | bytes 1572872 | tf_op jit(solution)/shard_map/ppermute | solution.py:26
  23.3 14.0 %collective-permute-start.6 = (bf16[128,2048]{1,0:T(8,128)(2,1)S(1)}, bf16[128,2048]{1,0:T(8,128)(2,1)S(1)}, u32[]{:S(2)}, u32[]{:S(2)}) collective-permute-start(bf16[128,2048]{1,0:T(8,128)(2,1)S(1)} %out_project.3), channel_id=1, source_target_pairs={{0,16},{8,24},{16,0},{24,8},{1,17},{9,25},{17,1},{25,9},{2,18},{10... | collective-permute-start | bytes 1572872 | tf_op jit(solution)/shard_map/ppermute | solution.py:26
  26.6 3.8 %collective-permute-start.4 = (bf16[128,512]{1,0:T(8,128)(2,1)S(1)}, bf16[128,512]{1,0:T(8,128)(2,1)S(1)}, u32[]{:S(2)}, u32[]{:S(2)}) collective-permute-start(bf16[128,512]{1,0:T(8,128)(2,1)S(1)} %get-tuple-element.80), channel_id=1, source_target_pairs={{0,8},{8,0},{16,24},{24,16},{1,9},{9,1},{17,25},{25,17},{2,10},{10... | collective-permute-start | bytes 393224 | tf_op jit(solution)/shard_map/ppermute | solution.py:26
  26.9 15.7 %collective-permute-start.7 = (bf16[64,2048]{1,0:T(8,128)(2,1)S(1)}, bf16[64,2048]{1,0:T(8,128)(2,1)S(1)}, u32[]{:S(2)}, u32[]{:S(2)}) collective-permute-start(bf16[64,2048]{1,0:T(8,128)(2,1)S(1)} %get-tuple-element.90), channel_id=1, source_target_pairs={{0,0},{1,1},{2,2},{3,3},{4,4},{5,5},{6,6},{7,7},{8,9},{9,8},{10,11... | collective-permute-start | bytes 786440 | tf_op jit(solution)/shard_map/ppermute | solution.py:283
  27.7 23.0 %collective-permute-start.8 = (bf16[64,2048]{1,0:T(8,128)(2,1)S(1)}, bf16[64,2048]{1,0:T(8,128)(2,1)S(1)}, u32[]{:S(2)}, u32[]{:S(2)}) collective-permute-start(bf16[64,2048]{1,0:T(8,128)(2,1)S(1)} %get-tuple-element.91), channel_id=1, source_target_pairs={{0,4},{1,5},{2,6},{3,7},{4,0},{5,1},{6,2},{7,3},{8,13},{9,12},{10,... | collective-permute-start | bytes 786440 | tf_op jit(solution)/shard_map/ppermute | solution.py:283
  38.0 17.0 %collective-permute-start.12 = (bf16[48,2048]{1,0:T(8,128)(2,1)S(1)}, bf16[48,2048]{1,0:T(8,128)(2,1)S(1)}, u32[]{:S(2)}, u32[]{:S(2)}) collective-permute-start(bf16[48,2048]{1,0:T(8,128)(2,1)S(1)} %get-tuple-element.98), channel_id=1, source_target_pairs={{0,4},{1,5},{2,6},{3,7},{4,0},{5,1},{6,2},{7,3},{8,12},{9,13},{10,... | collective-permute-start | bytes 589832 | tf_op jit(solution)/shard_map/ppermute | solution.py:26
  40.9 19.5 %collective-permute-start.13 = (bf16[48,2048]{1,0:T(8,128)(2,1)S(1)}, bf16[48,2048]{1,0:T(8,128)(2,1)S(1)}, u32[]{:S(2)}, u32[]{:S(2)}) collective-permute-start(bf16[48,2048]{1,0:T(8,128)(2,1)S(1)} %get-tuple-element.99), channel_id=1, source_target_pairs={{0,5},{1,4},{2,7},{3,6},{4,1},{5,0},{6,3},{7,2},{8,13},{9,12},{10,... | collective-permute-start | bytes 589832 | tf_op jit(solution)/shard_map/ppermute | solution.py:26
  50.8 15.5 %collective-permute-start.9 = (bf16[48,2048]{1,0:T(8,128)(2,1)S(1)}, bf16[48,2048]{1,0:T(8,128)(2,1)S(1)}, u32[]{:S(2)}, u32[]{:S(2)}) collective-permute-start(bf16[48,2048]{1,0:T(8,128)(2,1)S(1)} %get-tuple-element.95), channel_id=1, source_target_pairs={{0,1},{1,0},{2,3},{3,2},{4,5},{5,4},{6,7},{7,6},{8,9},{9,8},{10,11... | collective-permute-start | bytes 589832 | tf_op jit(solution)/shard_map/ppermute | solution.py:26
  52.3 17.2 %collective-permute-start.10 = (bf16[48,2048]{1,0:T(8,128)(2,1)S(1)}, bf16[48,2048]{1,0:T(8,128)(2,1)S(1)}, u32[]{:S(2)}, u32[]{:S(2)}) collective-permute-start(bf16[48,2048]{1,0:T(8,128)(2,1)S(1)} %get-tuple-element.96), channel_id=1, source_target_pairs={{0,2},{1,3},{2,0},{3,1},{4,6},{5,7},{6,4},{7,5},{8,10},{9,11},{10,... | collective-permute-start | bytes 589832 | tf_op jit(solution)/shard_map/ppermute | solution.py:26
  54.0 24.0 %collective-permute-start.11 = (bf16[48,2048]{1,0:T(8,128)(2,1)S(1)}, bf16[48,2048]{1,0:T(8,128)(2,1)S(1)}, u32[]{:S(2)}, u32[]{:S(2)}) collective-permute-start(bf16[48,2048]{1,0:T(8,128)(2,1)S(1)} %get-tuple-element.97), channel_id=1, source_target_pairs={{0,3},{1,2},{2,1},{3,0},{4,7},{5,6},{6,5},{7,4},{8,11},{9,10},{10,... | collective-permute-start | bytes 589832 | tf_op jit(solution)/shard_map/ppermute | solution.py:26
  55.0 27.7 %collective-permute-start.15 = (bf16[48,2048]{1,0:T(8,128)(2,1)S(1)}, bf16[48,2048]{1,0:T(8,128)(2,1)S(1)}, u32[]{:S(2)}, u32[]{:S(2)}) collective-permute-start(bf16[48,2048]{1,0:T(8,128)(2,1)S(1)} %get-tuple-element.111), channel_id=1, source_target_pairs={{0,6},{1,7},{2,4},{3,5},{4,2},{5,3},{6,0},{7,1},{8,14},{9,15},{10,... | collective-permute-start | bytes 589832 | tf_op jit(solution)/shard_map/ppermute | solution.py:26
  60.3 19.4 %collective-permute-start.14 = (bf16[128,2048]{1,0:T(8,128)(2,1)S(1)}, bf16[128,2048]{1,0:T(8,128)(2,1)S(1)}, u32[]{:S(2)}, u32[]{:S(2)}) collective-permute-start(bf16[128,2048]{1,0:T(8,128)(2,1)S(1)} %join.2.refs_0_), channel_id=1, source_target_pairs={{0,16},{8,24},{16,0},{24,8},{1,17},{9,25},{17,1},{25,9},{2,18},{10... | collective-permute-start | bytes 1572872 | tf_op jit(solution)/shard_map/ppermute | solution.py:26
  66.3 16.4 %collective-permute-start.16 = (bf16[48,2048]{1,0:T(8,128)(2,1)S(1)}, bf16[48,2048]{1,0:T(8,128)(2,1)S(1)}, u32[]{:S(2)}, u32[]{:S(2)}) collective-permute-start(bf16[48,2048]{1,0:T(8,128)(2,1)S(1)} %get-tuple-element.112), channel_id=1, source_target_pairs={{0,7},{1,6},{2,5},{3,4},{4,3},{5,2},{6,1},{7,0},{8,15},{9,14},{10,... | collective-permute-start | bytes 589832 | tf_op jit(solution)/shard_map/ppermute | solution.py:26
  69.4 26.1 %collective-permute-start.18 = (bf16[48,2048]{1,0:T(8,128)(2,1)S(1)}, bf16[48,2048]{1,0:T(8,128)(2,1)S(1)}, u32[]{:S(2)}, u32[]{:S(2)}) collective-permute-start(bf16[48,2048]{1,0:T(8,128)(2,1)S(1)} %get-tuple-element.100), channel_id=1, source_target_pairs={{0,4},{1,5},{2,6},{3,7},{4,0},{5,1},{6,2},{7,3},{8,12},{9,13},{10,... | collective-permute-start | bytes 589832 | tf_op jit(solution)/shard_map/ppermute | solution.py:26
  78.1 22.5 %collective-permute-start.19 = (bf16[48,2048]{1,0:T(8,128)(2,1)S(1)}, bf16[48,2048]{1,0:T(8,128)(2,1)S(1)}, u32[]{:S(2)}, u32[]{:S(2)}) collective-permute-start(bf16[48,2048]{1,0:T(8,128)(2,1)S(1)} %get-tuple-element.101), channel_id=1, source_target_pairs={{0,5},{1,4},{2,7},{3,6},{4,1},{5,0},{6,3},{7,2},{8,13},{9,12},{10,... | collective-permute-start | bytes 589832 | tf_op jit(solution)/shard_map/ppermute | solution.py:26
  79.8 2.8 %collective-permute-start.17 = (bf16[256,2048]{1,0:T(8,128)(2,1)S(1)}, bf16[256,2048]{1,0:T(8,128)(2,1)S(1)}, u32[]{:S(2)}, u32[]{:S(2)}) collective-permute-start(bf16[256,2048]{1,0:T(8,128)(2,1)S(1)} %join.3.mine_ref), channel_id=1, source_target_pairs={{0,8},{8,0},{16,24},{24,16},{1,9},{9,1},{17,25},{25,17},{2,10},{10... | collective-permute-start | bytes 3145736 | tf_op jit(solution)/shard_map/ppermute | solution.py:26
  84.8 28.3 %collective-permute-start.23 = (bf16[48,2048]{1,0:T(8,128)(2,1)S(1)}, bf16[48,2048]{1,0:T(8,128)(2,1)S(1)}, u32[]{:S(2)}, u32[]{:S(2)}) collective-permute-start(bf16[48,2048]{1,0:T(8,128)(2,1)S(1)} %get-tuple-element.115), channel_id=1, source_target_pairs={{0,6},{1,7},{2,4},{3,5},{4,2},{5,3},{6,0},{7,1},{8,14},{9,15},{10,... | collective-permute-start | bytes 589832 | tf_op jit(solution)/shard_map/ppermute | solution.py:26
  86.9 20.8 %collective-permute-start.20 = (bf16[48,2048]{1,0:T(8,128)(2,1)S(1)}, bf16[48,2048]{1,0:T(8,128)(2,1)S(1)}, u32[]{:S(2)}, u32[]{:S(2)}) collective-permute-start(bf16[48,2048]{1,0:T(8,128)(2,1)S(1)} %get-tuple-element.124), channel_id=1, source_target_pairs={{0,1},{1,0},{2,3},{3,2},{4,5},{5,4},{6,7},{7,6},{8,9},{9,8},{10,11... | collective-permute-start | bytes 589832 | tf_op jit(solution)/shard_map/ppermute | solution.py:26
  87.3 20.4 %collective-permute-start.21 = (bf16[48,2048]{1,0:T(8,128)(2,1)S(1)}, bf16[48,2048]{1,0:T(8,128)(2,1)S(1)}, u32[]{:S(2)}, u32[]{:S(2)}) collective-permute-start(bf16[48,2048]{1,0:T(8,128)(2,1)S(1)} %get-tuple-element.125), channel_id=1, source_target_pairs={{0,2},{1,3},{2,0},{3,1},{4,6},{5,7},{6,4},{7,5},{8,10},{9,11},{10,... | collective-permute-start | bytes 589832 | tf_op jit(solution)/shard_map/ppermute | solution.py:26
  95.5 17.6 %collective-permute-start.22 = (bf16[48,2048]{1,0:T(8,128)(2,1)S(1)}, bf16[48,2048]{1,0:T(8,128)(2,1)S(1)}, u32[]{:S(2)}, u32[]{:S(2)}) collective-permute-start(bf16[48,2048]{1,0:T(8,128)(2,1)S(1)} %get-tuple-element.126), channel_id=1, source_target_pairs={{0,3},{1,2},{2,1},{3,0},{4,7},{5,6},{6,5},{7,4},{8,11},{9,10},{10,... | collective-permute-start | bytes 589832 | tf_op jit(solution)/shard_map/ppermute | solution.py:26
  100.6 12.5 %collective-permute-start.24 = (bf16[48,2048]{1,0:T(8,128)(2,1)S(1)}, bf16[48,2048]{1,0:T(8,128)(2,1)S(1)}, u32[]{:S(2)}, u32[]{:S(2)}) collective-permute-start(bf16[48,2048]{1,0:T(8,128)(2,1)S(1)} %get-tuple-element.116), channel_id=1, source_target_pairs={{0,7},{1,6},{2,5},{3,4},{4,3},{5,2},{6,1},{7,0},{8,15},{9,14},{10,... | collective-permute-start | bytes 589832 | tf_op jit(solution)/shard_map/ppermute | solution.py:26
  (10 other events, 116.0 us)

commit v6 on v5

--- a/solution.py
+++ b/solution.py
@@ -250,7 +250,7 @@
 
         @pl.when(step % 4 == seq_me)
         def _(j=j, step=step):
-            pages[step // 4] = rows[j * page_len : (j + 1) * page_len]
+            pages[count // 4 - 1 - step // 4] = rows[j * page_len : (j + 1) * page_len]
 
     for k, out in enumerate(outs):
         out[...] = pages[k]
@@ -275,8 +275,9 @@
 
 def to_owner(page, number):
     seq_count, blk_count = lax.axis_size("seq"), lax.axis_size("blk")
+    k = blk_count // 4 - 1 - number
     pairs = [
-        (i * blk_count + b, i * blk_count + (b ^ (4 * number + i)))
+        (i * blk_count + b, i * blk_count + (b ^ (4 * k + i)))
         for i in range(seq_count)
         for b in range(blk_count)
     ]
@@ -290,7 +291,8 @@
     for core, ref in enumerate((mine_ref, theirs_ref)):
         for chip in range(2):
             for k in range(count // 4):
-                start = (blk_me ^ (4 * k + (seq_me ^ (2 * chip + core)))) * page_len
+                step = 4 * (count // 4 - 1 - k) + (seq_me ^ (2 * chip + core))
+                start = (blk_me ^ step) * page_len
                 page = ref[chip * half + k * page_len : chip * half + (k + 1) * page_len]
                 rows[pl.ds(pl.multiple_of(start, page_len), page_len)] = page
     rows[...] = rms_norm(rows[...], gain_ref[0:1])
@@ -360,7 +362,7 @@
     )
 
 
-def weigh_kernel(ffn_ref, router_ref, *refs, groups):
+def weigh_kernel(ffn_ref, router_ref, *refs, groups, sums):
     logits = lax.dot_general(
         router_ref[...], ffn_ref[...], (((1,), (1,)), ((), ())), preferred_element_type=F32
     )
@@ -370,20 +372,24 @@
     expert = lax.broadcasted_iota(jnp.int32, (experts, experts), 1)
     order = jnp.where(lax.axis_index("blk") ^ step == expert, F32(1), F32(0)).astype(BF16)
     gates = jnp.dot(order, gates, preferred_element_type=F32)
-    for group, pick, out in zip(groups, refs[: len(groups)], refs[len(groups) :]):
-        capacity = pick.shape[0] // len(group)
-        parts = [
-            pick[i * capacity : (i + 1) * capacity].astype(F32) * gates[s : s + 1]
-            for i, s in enumerate(group)
-        ]
+    picks, outs = refs[: len(groups)], refs[len(groups) :]
+    capacity = picks[0].shape[0] // len(groups[0])
+    pick_of = {
+        step: pick[i * capacity : (i + 1) * capacity]
+        for group, pick in zip(groups, picks)
+        for i, step in enumerate(group)
+    }
+    for steps, out in zip(sums, outs):
+        parts = [pick_of[s].astype(F32) * gates[s : s + 1] for s in steps]
         out[...] = jnp.concatenate(parts, axis=0).T.astype(BF16)
 
 
-def weigh(ffn_in, router, picks, groups):
-    return call(
-        functools.partial(weigh_kernel, groups=groups),
+def weigh(ffn_in, router, picks, groups, sums):
+    capacity, rows = picks[0].shape[0] // len(groups[0]), ffn_in.shape[0]
+    return call(
+        functools.partial(weigh_kernel, groups=groups, sums=sums),
         "weigh",
-        tuple(array(pick.shape[::-1]) for pick in picks),
+        tuple(array((rows, len(steps) * capacity)) for steps in sums),
         (ffn_in, router, *picks),
         8,
         0,
@@ -526,10 +532,10 @@
     back_near = there(near, near_out)
     kv_cache = cache(both, both_core, gains, w_flat, blk_count, heads_here, head_dim)
 
-    weights = weigh(ffn_in, w_router.T, picks, groups)
+    weights = weigh(ffn_in, w_router.T, picks, groups, (first, (*last, *near)))
     total = combine(resid, weights[0], [full(block) for block in back_first], F32)
     kv_cache, total = lax.optimization_barrier((kv_cache, total))
-    parts = [full(block) for block in (*back_near, *back_last)]
+    parts = [full(block) for block in (*back_last, *back_near)]
     total = combine(total, weights[1], parts, BF16)
     return (total[None], kv_cache)
 

time: 115 us -> 113 us (0.983)
  waiting for transfers between devices: 42 us -> 37.1 us
  starting transfers between devices: 41 us -> 44.1 us
    ppermute x23, waiting for transfers between devices: 33.9 us -> 29 us  [swap(): return lax.ppermute(value, axis, [(i, i ^ step) for i in range(size)])]
    ppermute x23, starting transfers between devices: 37.5 us -> 40.6 us  [swap(): return lax.ppermute(value, axis, [(i, i ^ step) for i in range(size)])]
  transfers between devices with their start and end apart: 25 -> 25, of which waited for: 11 -> 11; matrix products, arithmetic and copies ran while one was open for 5% -> 5% of each run, Pallas kernels for 20% -> 21%
where the time goes in v6:
time: 113 us
  starting transfers between devices  44.1 us (39%)
  waiting for transfers between devices  37.1 us (33%)
  Pallas kernels  25 us (22%)
  local copies, waits for them, and re-layouts  5.43 us (5%)
    ppermute x23, starting transfers between devices, swap(): return lax.ppermute(value, axis, [(i, i ^ step) for i in range(size)])  40.6 us
    ppermute x23, waiting for transfers between devices, swap(): return lax.ppermute(value, axis, [(i, i ^ step) for i in range(size)])  29 us
    pallas_call x19, Pallas kernels, call(): pl.pallas_call(kernel, out_shape=out_shape, in_specs=[SMEM_SPEC] * scalar...  25 us
    ppermute x2, waiting for transfers between devices, to_owner(): return lax.ppermute(page, ('seq', 'blk'), pairs)  8.06 us
    unnamed x19, local copies, waits for them, and re-layouts  4.05 us
    ppermute x2, starting transfers between devices, to_owner(): return lax.ppermute(page, ('seq', 'blk'), pairs)  3.5 us
  transfers between devices with their start and end apart: 25, of which 11 were waited for; matrix products, arithmetic and copies ran while one was open for 5% of the time, Pallas kernels for 21%

profile of v6, /device:TPU:0, one launch (start us, length us, event | category | flops | bytes accessed | tf_op | source)
XLA Modules:
  0.0 112.6 jit_solution(8705156765540079168)
XLA Ops:
  1.2 2.9 %collective-permute-start = (bf16[128,2048]{1,0:T(8,128)(2,1)}, bf16[128,2048]{1,0:T(8,128)(2,1)S(1)}, u32[]{:S(2)}, u32[]{:S(2)}) collective-permute-start(bf16[128,2048]{1,0:T(8,128)(2,1)} %bitcast.19), channel_id=1, source_target_pairs={{0,16},{8,24},{16,0},{24,8},{1,17},{9,25},{17,1},{25,9},{2,18},{10... | collective-permute-start | bytes 1572872 | tf_op jit(solution)/shard_map/ppermute | solution.py:26
  5.5 4.0 %copy.13 = bf16[256,8,4,384]{3,1,2,0:T(8,128)(2,1)S(1)} copy(bf16[256,8,4,384]{3,2,1,0:T(4,128)(2,1)} %bitcast.33) | data formatting | bytes 12582912
  9.6 2.6 %project.2 = (bf16[256,512]{1,0:T(8,128)(2,1)S(1)}, bf16[256,1024]{1,0:T(8,128)(2,1)S(1)}) custom-call(bf16[128,2048]{1,0:T(8,128)(2,1)S(1)} %bitcast.20, bf16[128,2048]{1,0:T(8,128)(2,1)S(1)} %collective-permute-done.1.refs_1_, bf16[2,2048]{1,0:T(2,128)(2,1)S(1)} %pad_maximum_fusion.refs_2_.refs_1_.gain.gain_ref, bf16[2048,1536]{1,0:T(8,128)(2,1)S(1)} %bitcast.11), custom_call_target="tpu_custom_call" | custom-call | tf_op jit(solution)/shard_map/project/pallas_call | solution.py:38
  12.2 4.3 %collective-permute-done.refs_0_.refs_2_ = bf16[128,2048]{1,0:T(8,128)(2,1)S(1)} collective-permute-done((bf16[128,2048]{1,0:T(8,128)(2,1)}, bf16[128,2048]{1,0:T(8,128)(2,1)S(1)}, u32[]{:S(2)}, u32[]{:S(2)}) %collective-permute-start) | collective-permute-done | bytes 524320 | tf_op jit(solution)/shard_map/ppermute | solution.py:26
  18.4 2.7 %attend_far.1 = (bf16[128,512]{1,0:T(8,128)(2,1)S(1)}, bf16[128,512]{1,0:T(8,128)(2,1)S(1)}, bf16[128,1024]{1,0:T(8,128)(2,1)S(1)}) custom-call(s32[1,512]{1,0:T(1,128)S(1)} %copy-done.3, bf16[128,512]{1,0:T(8,128)(2,1)S(1)} %get-tuple-element.71.q_far, bf16[256,1024]{1,0:T(8,128)(2,1)S(1)} %get-tuple-element.68.kv_near, ...), custom_call_target="tpu_custom_call" | custom-call | tf_op jit(solution)/shard_map/attend_far/pallas_call | solution.py:38
  26.9 2.7 %collective-permute-start.7 = (bf16[64,2048]{1,0:T(8,128)(2,1)S(1)}, bf16[64,2048]{1,0:T(8,128)(2,1)S(1)}, u32[]{:S(2)}, u32[]{:S(2)}) collective-permute-start(bf16[64,2048]{1,0:T(8,128)(2,1)S(1)} %get-tuple-element.90), channel_id=1, source_target_pairs={{0,4},{1,5},{2,6},{3,7},{4,0},{5,1},{6,2},{7,3},{8,13},{9,12},{10,... | collective-permute-start | bytes 786440 | tf_op jit(solution)/shard_map/ppermute | solution.py:284
  31.1 6.2 %collective-permute-done.6.far_ref = bf16[128,2048]{1,0:T(8,128)(2,1)S(1)} collective-permute-done((bf16[128,2048]{1,0:T(8,128)(2,1)S(1)}, bf16[128,2048]{1,0:T(8,128)(2,1)S(1)}, u32[]{:S(2)}, u32[]{:S(2)}) %collective-permute-start.6) | collective-permute-done | bytes 524320 | tf_op jit(solution)/shard_map/ppermute | solution.py:26
  38.0 2.9 %collective-permute-start.12 = (bf16[48,2048]{1,0:T(8,128)(2,1)S(1)}, bf16[48,2048]{1,0:T(8,128)(2,1)S(1)}, u32[]{:S(2)}, u32[]{:S(2)}) collective-permute-start(bf16[48,2048]{1,0:T(8,128)(2,1)S(1)} %get-tuple-element.98), channel_id=1, source_target_pairs={{0,4},{1,5},{2,6},{3,7},{4,0},{5,1},{6,2},{7,3},{8,12},{9,13},{10,... | collective-permute-start | bytes 589832 | tf_op jit(solution)/shard_map/ppermute | solution.py:26
  42.6 8.1 %collective-permute-done.7.refs_0_ = bf16[64,2048]{1,0:T(8,128)(2,1)S(1)} collective-permute-done((bf16[64,2048]{1,0:T(8,128)(2,1)S(1)}, bf16[64,2048]{1,0:T(8,128)(2,1)S(1)}, u32[]{:S(2)}, u32[]{:S(2)}) %collective-permute-start.7) | collective-permute-done | bytes 262176 | tf_op jit(solution)/shard_map/ppermute | solution.py:284
  54.9 3.9 %collective-permute-start.15 = (bf16[48,2048]{1,0:T(8,128)(2,1)S(1)}, bf16[48,2048]{1,0:T(8,128)(2,1)S(1)}, u32[]{:S(2)}, u32[]{:S(2)}) collective-permute-start(bf16[48,2048]{1,0:T(8,128)(2,1)S(1)} %get-tuple-element.111), channel_id=1, source_target_pairs={{0,6},{1,7},{2,4},{3,5},{4,2},{5,3},{6,0},{7,1},{8,14},{9,15},{10,... | collective-permute-start | bytes 589832 | tf_op jit(solution)/shard_map/ppermute | solution.py:26
  60.5 5.4 %collective-permute-start.14 = (bf16[128,2048]{1,0:T(8,128)(2,1)S(1)}, bf16[128,2048]{1,0:T(8,128)(2,1)S(1)}, u32[]{:S(2)}, u32[]{:S(2)}) collective-permute-start(bf16[128,2048]{1,0:T(8,128)(2,1)S(1)} %join.2.refs_0_), channel_id=1, source_target_pairs={{0,16},{8,24},{16,0},{24,8},{1,17},{9,25},{17,1},{25,9},{2,18},{10... | collective-permute-start | bytes 1572872 | tf_op jit(solution)/shard_map/ppermute | solution.py:26
  65.9 2.2 %expert.3 = (bf16[48,2048]{1,0:T(8,128)(2,1)S(1)}, bf16[48,2048]{1,0:T(8,128)(2,1)S(1)}) custom-call(bf16[48,2048]{1,0:T(8,128)(2,1)S(1)} %collective-permute-done.12.refs_0_, bf16[48,2048]{1,0:T(8,128)(2,1)S(1)} %collective-permute-done.13.refs_1_, bf16[2048,2048]{1,0:T(8,128)(2,1)S(1)} %bitcast.26, bf16[1024,2048]{1,0:T(8,128)(2,1)S(1)} %bitcast.29), custom_call_target="tpu_custom_call" | custom-call | flops 34359738368 | tf_op jit(solution)/shard_map/expert/pallas_call | solution.py:38
  68.2 3.4 %collective-permute-start.18 = (bf16[48,2048]{1,0:T(8,128)(2,1)S(1)}, bf16[48,2048]{1,0:T(8,128)(2,1)S(1)}, u32[]{:S(2)}, u32[]{:S(2)}) collective-permute-start(bf16[48,2048]{1,0:T(8,128)(2,1)S(1)} %get-tuple-element.100), channel_id=1, source_target_pairs={{0,4},{1,5},{2,6},{3,7},{4,0},{5,1},{6,2},{7,3},{8,12},{9,13},{10,... | collective-permute-start | bytes 589832 | tf_op jit(solution)/shard_map/ppermute | solution.py:26
  71.6 3.4 %collective-permute-done.11.refs_3_ = bf16[48,2048]{1,0:T(8,128)(2,1)S(1)} collective-permute-done((bf16[48,2048]{1,0:T(8,128)(2,1)S(1)}, bf16[48,2048]{1,0:T(8,128)(2,1)S(1)}, u32[]{:S(2)}, u32[]{:S(2)}) %collective-permute-start.11) | collective-permute-done | bytes 196640 | tf_op jit(solution)/shard_map/ppermute | solution.py:26
  76.4 2.7 %expert.4 = (bf16[48,2048]{1,0:T(8,128)(2,1)S(1)}, bf16[48,2048]{1,0:T(8,128)(2,1)S(1)}, bf16[48,2048]{1,0:T(8,128)(2,1)S(1)}, bf16[48,2048]{1,0:T(8,128)(2,1)S(1)}) custom-call(bf16[48,2048]{1,0:T(8,128)(2,1)S(1)} %get-tuple-element.103.refs_0_, bf16[48,2048]{1,0:T(8,128)(2,1)S(1)} %collective-permute-done.9.refs_1_, ...), custom_call_target="tpu_custom_call" | custom-call | flops 34359738368 | tf_op jit(solution)/shard_map/expert/pallas_call | solution.py:38
  79.1 2.2 %expert.5 = (bf16[48,2048]{1,0:T(8,128)(2,1)S(1)}, bf16[48,2048]{1,0:T(8,128)(2,1)S(1)}) custom-call(bf16[48,2048]{1,0:T(8,128)(2,1)S(1)} %collective-permute-done.15.refs_0_, bf16[48,2048]{1,0:T(8,128)(2,1)S(1)} %collective-permute-done.16.refs_1_, bf16[2048,2048]{1,0:T(8,128)(2,1)S(1)} %bitcast.28, bf16[1024,2048]{1,0:T(8,128)(2,1)S(1)} %bitcast.31), custom_call_target="tpu_custom_call" | custom-call | flops 34359738368 | tf_op jit(solution)/shard_map/expert/pallas_call | solution.py:38
  81.3 2.0 %collective-permute-start.20 = (bf16[48,2048]{1,0:T(8,128)(2,1)S(1)}, bf16[48,2048]{1,0:T(8,128)(2,1)S(1)}, u32[]{:S(2)}, u32[]{:S(2)}) collective-permute-start(bf16[48,2048]{1,0:T(8,128)(2,1)S(1)} %get-tuple-element.115), channel_id=1, source_target_pairs={{0,6},{1,7},{2,4},{3,5},{4,2},{5,3},{6,0},{7,1},{8,14},{9,15},{10,... | collective-permute-start | bytes 589832 | tf_op jit(solution)/shard_map/ppermute | solution.py:26
  83.3 3.1 %collective-permute-start.22 = (bf16[48,2048]{1,0:T(8,128)(2,1)S(1)}, bf16[48,2048]{1,0:T(8,128)(2,1)S(1)}, u32[]{:S(2)}, u32[]{:S(2)}) collective-permute-start(bf16[48,2048]{1,0:T(8,128)(2,1)S(1)} %get-tuple-element.124), channel_id=1, source_target_pairs={{0,1},{1,0},{2,3},{3,2},{4,5},{5,4},{6,7},{7,6},{8,9},{9,8},{10,11... | collective-permute-start | bytes 589832 | tf_op jit(solution)/shard_map/ppermute | solution.py:26
  86.5 5.2 %collective-permute-start.23 = (bf16[48,2048]{1,0:T(8,128)(2,1)S(1)}, bf16[48,2048]{1,0:T(8,128)(2,1)S(1)}, u32[]{:S(2)}, u32[]{:S(2)}) collective-permute-start(bf16[48,2048]{1,0:T(8,128)(2,1)S(1)} %get-tuple-element.125), channel_id=1, source_target_pairs={{0,2},{1,3},{2,0},{3,1},{4,6},{5,7},{6,4},{7,5},{8,10},{9,11},{10,... | collective-permute-start | bytes 589832 | tf_op jit(solution)/shard_map/ppermute | solution.py:26
  91.7 2.9 %collective-permute-done.18.refs_0_ = bf16[48,2048]{1,0:T(8,128)(2,1)S(1)} collective-permute-done((bf16[48,2048]{1,0:T(8,128)(2,1)S(1)}, bf16[48,2048]{1,0:T(8,128)(2,1)S(1)}, u32[]{:S(2)}, u32[]{:S(2)}) %collective-permute-start.18) | collective-permute-done | bytes 196640 | tf_op jit(solution)/shard_map/ppermute | solution.py:26
  94.6 4.5 %collective-permute-done.19.refs_1_ = bf16[48,2048]{1,0:T(8,128)(2,1)S(1)} collective-permute-done((bf16[48,2048]{1,0:T(8,128)(2,1)S(1)}, bf16[48,2048]{1,0:T(8,128)(2,1)S(1)}, u32[]{:S(2)}, u32[]{:S(2)}) %collective-permute-start.19) | collective-permute-done | bytes 196640 | tf_op jit(solution)/shard_map/ppermute | solution.py:26
  99.1 2.9 %collective-permute-start.21 = (bf16[48,2048]{1,0:T(8,128)(2,1)S(1)}, bf16[48,2048]{1,0:T(8,128)(2,1)S(1)}, u32[]{:S(2)}, u32[]{:S(2)}) collective-permute-start(bf16[48,2048]{1,0:T(8,128)(2,1)S(1)} %get-tuple-element.116), channel_id=1, source_target_pairs={{0,7},{1,6},{2,5},{3,4},{4,3},{5,2},{6,1},{7,0},{8,15},{9,14},{10,... | collective-permute-start | bytes 589832 | tf_op jit(solution)/shard_map/ppermute | solution.py:26
  102.7 4.1 %cache.1 = bf16[1,8,64,1024]{3,2,1,0:T(8,128)(2,1)} custom-call(bf16[256,2048]{1,0:T(8,128)(2,1)S(1)} %join.3.mine_ref, bf16[256,2048]{1,0:T(8,128)(2,1)S(1)} %collective-permute-done.17.theirs_ref, bf16[2,2048]{1,0:T(2,128)(2,1)S(1)} %pad_maximum_fusion.refs_2_.refs_1_.gain.gain_ref, bf16[2048,1536]{1,0:T(8,128)(2,1)S(1)} %bitcast.14), custom_call_target="tpu_custom_call" | custom-call | tf_op jit(solution)/shard_map/cache/pallas_call | solution.py:38
  106.9 4.4 %collective-permute-done.24.refs_5_ = bf16[48,2048]{1,0:T(8,128)(2,1)S(1)} collective-permute-done((bf16[48,2048]{1,0:T(8,128)(2,1)S(1)}, bf16[48,2048]{1,0:T(8,128)(2,1)S(1)}, u32[]{:S(2)}, u32[]{:S(2)}) %collective-permute-start.24) | collective-permute-done | bytes 196640 | tf_op jit(solution)/shard_map/ppermute | solution.py:26
  (68 shorter events, 22.8 us)
Async XLA Ops:
  0.6 22.0 %collective-permute-start.5 = (bf16[512,2048]{1,0:T(8,128)(2,1)}, bf16[512,2048]{1,0:T(8,128)(2,1)S(1)}, u32[]{:S(2)}, u32[]{:S(2)}) collective-permute-start(bf16[512,2048]{1,0:T(8,128)(2,1)} %bitcast.15), channel_id=1, source_target_pairs={{0,8},{8,0},{16,24},{24,16},{1,9},{9,1},{17,25},{25,17},{2,10},{10... | collective-permute-start | bytes 6291464 | tf_op jit(solution)/shard_map/ppermute | solution.py:26
  1.1 8.4 %collective-permute-start.1 = (bf16[128,2048]{1,0:T(8,128)(2,1)}, bf16[128,2048]{1,0:T(8,128)(2,1)S(1)}, u32[]{:S(2)}, u32[]{:S(2)}) collective-permute-start(bf16[128,2048]{1,0:T(8,128)(2,1)} %bitcast.18), channel_id=1, source_target_pairs={{0,8},{8,0},{16,24},{24,16},{1,9},{9,1},{17,25},{25,17},{2,10},{10... | collective-permute-start | bytes 1572872 | tf_op jit(solution)/shard_map/ppermute | solution.py:26
  1.2 15.3 %collective-permute-start = (bf16[128,2048]{1,0:T(8,128)(2,1)}, bf16[128,2048]{1,0:T(8,128)(2,1)S(1)}, u32[]{:S(2)}, u32[]{:S(2)}) collective-permute-start(bf16[128,2048]{1,0:T(8,128)(2,1)} %bitcast.19), channel_id=1, source_target_pairs={{0,16},{8,24},{16,0},{24,8},{1,17},{9,25},{17,1},{25,9},{2,18},{10... | collective-permute-start | bytes 1572872 | tf_op jit(solution)/shard_map/ppermute | solution.py:26
  16.5 1.9 %collective-permute-start.2 = (bf16[128,2048]{1,0:T(8,128)(2,1)S(1)}, bf16[128,2048]{1,0:T(8,128)(2,1)S(1)}, u32[]{:S(2)}, u32[]{:S(2)}) collective-permute-start(bf16[128,2048]{1,0:T(8,128)(2,1)S(1)} %collective-permute-done.refs_0_.refs_2_), channel_id=1, source_target_pairs={{0,8},{8,0},{16,24},{24,16},{1,9},{9,1},{17,25},{25,17},{2,10},{10... | collective-permute-start | bytes 1572872 | tf_op jit(solution)/shard_map/ppermute | solution.py:26
  23.3 14.0 %collective-permute-start.6 = (bf16[128,2048]{1,0:T(8,128)(2,1)S(1)}, bf16[128,2048]{1,0:T(8,128)(2,1)S(1)}, u32[]{:S(2)}, u32[]{:S(2)}) collective-permute-start(bf16[128,2048]{1,0:T(8,128)(2,1)S(1)} %out_project.3), channel_id=1, source_target_pairs={{0,16},{8,24},{16,0},{24,8},{1,17},{9,25},{17,1},{25,9},{2,18},{10... | collective-permute-start | bytes 1572872 | tf_op jit(solution)/shard_map/ppermute | solution.py:26
  26.6 3.8 %collective-permute-start.4 = (bf16[128,512]{1,0:T(8,128)(2,1)S(1)}, bf16[128,512]{1,0:T(8,128)(2,1)S(1)}, u32[]{:S(2)}, u32[]{:S(2)}) collective-permute-start(bf16[128,512]{1,0:T(8,128)(2,1)S(1)} %get-tuple-element.80), channel_id=1, source_target_pairs={{0,8},{8,0},{16,24},{24,16},{1,9},{9,1},{17,25},{25,17},{2,10},{10... | collective-permute-start | bytes 393224 | tf_op jit(solution)/shard_map/ppermute | solution.py:26
  26.9 23.8 %collective-permute-start.7 = (bf16[64,2048]{1,0:T(8,128)(2,1)S(1)}, bf16[64,2048]{1,0:T(8,128)(2,1)S(1)}, u32[]{:S(2)}, u32[]{:S(2)}) collective-permute-start(bf16[64,2048]{1,0:T(8,128)(2,1)S(1)} %get-tuple-element.90), channel_id=1, source_target_pairs={{0,4},{1,5},{2,6},{3,7},{4,0},{5,1},{6,2},{7,3},{8,13},{9,12},{10,... | collective-permute-start | bytes 786440 | tf_op jit(solution)/shard_map/ppermute | solution.py:284
  29.5 21.1 %collective-permute-start.8 = (bf16[64,2048]{1,0:T(8,128)(2,1)S(1)}, bf16[64,2048]{1,0:T(8,128)(2,1)S(1)}, u32[]{:S(2)}, u32[]{:S(2)}) collective-permute-start(bf16[64,2048]{1,0:T(8,128)(2,1)S(1)} %get-tuple-element.91), channel_id=1, source_target_pairs={{0,0},{1,1},{2,2},{3,3},{4,4},{5,5},{6,6},{7,7},{8,9},{9,8},{10,11... | collective-permute-start | bytes 786440 | tf_op jit(solution)/shard_map/ppermute | solution.py:284
  38.0 16.9 %collective-permute-start.12 = (bf16[48,2048]{1,0:T(8,128)(2,1)S(1)}, bf16[48,2048]{1,0:T(8,128)(2,1)S(1)}, u32[]{:S(2)}, u32[]{:S(2)}) collective-permute-start(bf16[48,2048]{1,0:T(8,128)(2,1)S(1)} %get-tuple-element.98), channel_id=1, source_target_pairs={{0,4},{1,5},{2,6},{3,7},{4,0},{5,1},{6,2},{7,3},{8,12},{9,13},{10,... | collective-permute-start | bytes 589832 | tf_op jit(solution)/shard_map/ppermute | solution.py:26
  40.9 19.6 %collective-permute-start.13 = (bf16[48,2048]{1,0:T(8,128)(2,1)S(1)}, bf16[48,2048]{1,0:T(8,128)(2,1)S(1)}, u32[]{:S(2)}, u32[]{:S(2)}) collective-permute-start(bf16[48,2048]{1,0:T(8,128)(2,1)S(1)} %get-tuple-element.99), channel_id=1, source_target_pairs={{0,5},{1,4},{2,7},{3,6},{4,1},{5,0},{6,3},{7,2},{8,13},{9,12},{10,... | collective-permute-start | bytes 589832 | tf_op jit(solution)/shard_map/ppermute | solution.py:26
  50.7 17.4 %collective-permute-start.9 = (bf16[48,2048]{1,0:T(8,128)(2,1)S(1)}, bf16[48,2048]{1,0:T(8,128)(2,1)S(1)}, u32[]{:S(2)}, u32[]{:S(2)}) collective-permute-start(bf16[48,2048]{1,0:T(8,128)(2,1)S(1)} %get-tuple-element.95), channel_id=1, source_target_pairs={{0,1},{1,0},{2,3},{3,2},{4,5},{5,4},{6,7},{7,6},{8,9},{9,8},{10,11... | collective-permute-start | bytes 589832 | tf_op jit(solution)/shard_map/ppermute | solution.py:26
  52.5 15.7 %collective-permute-start.10 = (bf16[48,2048]{1,0:T(8,128)(2,1)S(1)}, bf16[48,2048]{1,0:T(8,128)(2,1)S(1)}, u32[]{:S(2)}, u32[]{:S(2)}) collective-permute-start(bf16[48,2048]{1,0:T(8,128)(2,1)S(1)} %get-tuple-element.96), channel_id=1, source_target_pairs={{0,2},{1,3},{2,0},{3,1},{4,6},{5,7},{6,4},{7,5},{8,10},{9,11},{10,... | collective-permute-start | bytes 589832 | tf_op jit(solution)/shard_map/ppermute | solution.py:26
  52.8 22.3 %collective-permute-start.11 = (bf16[48,2048]{1,0:T(8,128)(2,1)S(1)}, bf16[48,2048]{1,0:T(8,128)(2,1)S(1)}, u32[]{:S(2)}, u32[]{:S(2)}) collective-permute-start(bf16[48,2048]{1,0:T(8,128)(2,1)S(1)} %get-tuple-element.97), channel_id=1, source_target_pairs={{0,3},{1,2},{2,1},{3,0},{4,7},{5,6},{6,5},{7,4},{8,11},{9,10},{10,... | collective-permute-start | bytes 589832 | tf_op jit(solution)/shard_map/ppermute | solution.py:26
  54.9 24.2 %collective-permute-start.15 = (bf16[48,2048]{1,0:T(8,128)(2,1)S(1)}, bf16[48,2048]{1,0:T(8,128)(2,1)S(1)}, u32[]{:S(2)}, u32[]{:S(2)}) collective-permute-start(bf16[48,2048]{1,0:T(8,128)(2,1)S(1)} %get-tuple-element.111), channel_id=1, source_target_pairs={{0,6},{1,7},{2,4},{3,5},{4,2},{5,3},{6,0},{7,1},{8,14},{9,15},{10,... | collective-permute-start | bytes 589832 | tf_op jit(solution)/shard_map/ppermute | solution.py:26
  60.5 15.8 %collective-permute-start.14 = (bf16[128,2048]{1,0:T(8,128)(2,1)S(1)}, bf16[128,2048]{1,0:T(8,128)(2,1)S(1)}, u32[]{:S(2)}, u32[]{:S(2)}) collective-permute-start(bf16[128,2048]{1,0:T(8,128)(2,1)S(1)} %join.2.refs_0_), channel_id=1, source_target_pairs={{0,16},{8,24},{16,0},{24,8},{1,17},{9,25},{17,1},{25,9},{2,18},{10... | collective-permute-start | bytes 1572872 | tf_op jit(solution)/shard_map/ppermute | solution.py:26
  68.1 11.0 %collective-permute-start.16 = (bf16[48,2048]{1,0:T(8,128)(2,1)S(1)}, bf16[48,2048]{1,0:T(8,128)(2,1)S(1)}, u32[]{:S(2)}, u32[]{:S(2)}) collective-permute-start(bf16[48,2048]{1,0:T(8,128)(2,1)S(1)} %get-tuple-element.112), channel_id=1, source_target_pairs={{0,7},{1,6},{2,5},{3,4},{4,3},{5,2},{6,1},{7,0},{8,15},{9,14},{10,... | collective-permute-start | bytes 589832 | tf_op jit(solution)/shard_map/ppermute | solution.py:26
  68.2 26.4 %collective-permute-start.18 = (bf16[48,2048]{1,0:T(8,128)(2,1)S(1)}, bf16[48,2048]{1,0:T(8,128)(2,1)S(1)}, u32[]{:S(2)}, u32[]{:S(2)}) collective-permute-start(bf16[48,2048]{1,0:T(8,128)(2,1)S(1)} %get-tuple-element.100), channel_id=1, source_target_pairs={{0,4},{1,5},{2,6},{3,7},{4,0},{5,1},{6,2},{7,3},{8,12},{9,13},{10,... | collective-permute-start | bytes 589832 | tf_op jit(solution)/shard_map/ppermute | solution.py:26
  75.1 24.0 %collective-permute-start.19 = (bf16[48,2048]{1,0:T(8,128)(2,1)S(1)}, bf16[48,2048]{1,0:T(8,128)(2,1)S(1)}, u32[]{:S(2)}, u32[]{:S(2)}) collective-permute-start(bf16[48,2048]{1,0:T(8,128)(2,1)S(1)} %get-tuple-element.101), channel_id=1, source_target_pairs={{0,5},{1,4},{2,7},{3,6},{4,1},{5,0},{6,3},{7,2},{8,13},{9,12},{10,... | collective-permute-start | bytes 589832 | tf_op jit(solution)/shard_map/ppermute | solution.py:26
  76.3 2.8 %collective-permute-start.17 = (bf16[256,2048]{1,0:T(8,128)(2,1)S(1)}, bf16[256,2048]{1,0:T(8,128)(2,1)S(1)}, u32[]{:S(2)}, u32[]{:S(2)}) collective-permute-start(bf16[256,2048]{1,0:T(8,128)(2,1)S(1)} %join.3.mine_ref), channel_id=1, source_target_pairs={{0,8},{8,0},{16,24},{24,16},{1,9},{9,1},{17,25},{25,17},{2,10},{10... | collective-permute-start | bytes 3145736 | tf_op jit(solution)/shard_map/ppermute | solution.py:26
  81.3 30.0 %collective-permute-start.20 = (bf16[48,2048]{1,0:T(8,128)(2,1)S(1)}, bf16[48,2048]{1,0:T(8,128)(2,1)S(1)}, u32[]{:S(2)}, u32[]{:S(2)}) collective-permute-start(bf16[48,2048]{1,0:T(8,128)(2,1)S(1)} %get-tuple-element.115), channel_id=1, source_target_pairs={{0,6},{1,7},{2,4},{3,5},{4,2},{5,3},{6,0},{7,1},{8,14},{9,15},{10,... | collective-permute-start | bytes 589832 | tf_op jit(solution)/shard_map/ppermute | solution.py:26
  83.3 23.6 %collective-permute-start.22 = (bf16[48,2048]{1,0:T(8,128)(2,1)S(1)}, bf16[48,2048]{1,0:T(8,128)(2,1)S(1)}, u32[]{:S(2)}, u32[]{:S(2)}) collective-permute-start(bf16[48,2048]{1,0:T(8,128)(2,1)S(1)} %get-tuple-element.124), channel_id=1, source_target_pairs={{0,1},{1,0},{2,3},{3,2},{4,5},{5,4},{6,7},{7,6},{8,9},{9,8},{10,11... | collective-permute-start | bytes 589832 | tf_op jit(solution)/shard_map/ppermute | solution.py:26
  86.5 20.4 %collective-permute-start.23 = (bf16[48,2048]{1,0:T(8,128)(2,1)S(1)}, bf16[48,2048]{1,0:T(8,128)(2,1)S(1)}, u32[]{:S(2)}, u32[]{:S(2)}) collective-permute-start(bf16[48,2048]{1,0:T(8,128)(2,1)S(1)} %get-tuple-element.125), channel_id=1, source_target_pairs={{0,2},{1,3},{2,0},{3,1},{4,6},{5,7},{6,4},{7,5},{8,10},{9,11},{10,... | collective-permute-start | bytes 589832 | tf_op jit(solution)/shard_map/ppermute | solution.py:26
  94.6 16.7 %collective-permute-start.24 = (bf16[48,2048]{1,0:T(8,128)(2,1)S(1)}, bf16[48,2048]{1,0:T(8,128)(2,1)S(1)}, u32[]{:S(2)}, u32[]{:S(2)}) collective-permute-start(bf16[48,2048]{1,0:T(8,128)(2,1)S(1)} %get-tuple-element.126), channel_id=1, source_target_pairs={{0,3},{1,2},{2,1},{3,0},{4,7},{5,6},{6,5},{7,4},{8,11},{9,10},{10,... | collective-permute-start | bytes 589832 | tf_op jit(solution)/shard_map/ppermute | solution.py:26
  99.1 12.3 %collective-permute-start.21 = (bf16[48,2048]{1,0:T(8,128)(2,1)S(1)}, bf16[48,2048]{1,0:T(8,128)(2,1)S(1)}, u32[]{:S(2)}, u32[]{:S(2)}) collective-permute-start(bf16[48,2048]{1,0:T(8,128)(2,1)S(1)} %get-tuple-element.116), channel_id=1, source_target_pairs={{0,7},{1,6},{2,5},{3,4},{4,3},{5,2},{6,1},{7,0},{8,15},{9,14},{10,... | collective-permute-start | bytes 589832 | tf_op jit(solution)/shard_map/ppermute | solution.py:26
  (10 other events, 124.3 us)

commit v7 on v6

--- a/solution.py
+++ b/solution.py
@@ -83,11 +83,13 @@
     rows = blocks[0].shape[0]
     for i, block in enumerate(blocks):
         normed[i * rows : (i + 1) * rows] = rms_norm(block[...], gain_ref[0:1])
+    out = jnp.dot(normed[...], w_ref[...], preferred_element_type=F32).astype(BF16)
     for h in range(q_ref.shape[1] // head_dim):
-        columns = slice(3 * h * head_dim, 3 * (h + 1) * head_dim)
-        out = jnp.dot(normed[...], w_ref[:, columns], preferred_element_type=F32).astype(BF16)
-        q_ref[:, h * head_dim : (h + 1) * head_dim] = out[:, :head_dim]
-        kv_ref[:, 2 * h * head_dim : 2 * (h + 1) * head_dim] = out[:, head_dim:]
+        at = 3 * h * head_dim
+        q_ref[:, h * head_dim : (h + 1) * head_dim] = out[:, at : at + head_dim]
+        kv_ref[:, 2 * h * head_dim : 2 * (h + 1) * head_dim] = out[
+            :, at + head_dim : at + 3 * head_dim
+        ]
 
 
 def project_kernel(*refs, head_dim):
@@ -121,24 +123,31 @@
     column = jnp.broadcast_to(row, (8, row.shape[1])).T[first : first + 2 * block, 0:1]
     bias[...] = jnp.where(column == row, F32(0), F32(-1e30))
     factor = math.log2(math.e) / math.sqrt(head_dim)
-    for h in range(queries[0].shape[1] // head_dim):
-        q_cols = slice(h * head_dim, (h + 1) * head_dim)
-        k_cols = slice(2 * h * head_dim, (2 * h + 1) * head_dim)
-        v_cols = slice((2 * h + 1) * head_dim, (2 * h + 2) * head_dim)
-        query = jnp.concatenate([ref[:, q_cols] for ref in queries], axis=0)
-        key = jnp.concatenate([ref[:, k_cols] for ref in kvs], axis=0)
-        value = jnp.concatenate([ref[:, v_cols] for ref in kvs], axis=0)
-        scores = lax.dot_general(
-            query, key, (((1,), (1,)), ((), ())), preferred_element_type=F32
+    heads = range(queries[0].shape[1] // head_dim)
+    columns = [slice(h * head_dim, (h + 1) * head_dim) for h in range(2 * len(heads))]
+
+    def rows_of(refs, cols):
+        return jnp.concatenate([ref[:, cols] for ref in refs], axis=0)
+
+    scores = [
+        lax.dot_general(
+            rows_of(queries, columns[h]),
+            rows_of(kvs, columns[2 * h]),
+            (((1,), (1,)), ((), ())),
+            preferred_element_type=F32,
         )
-        scores = scores + bias[...]
-        top = jnp.max(scores, axis=-1, keepdims=True)
-        weights = jnp.exp2((scores - top) * factor)
-        total = jnp.sum(weights, axis=-1, keepdims=True)
-        context = jnp.dot(weights.astype(BF16), value, preferred_element_type=F32)
-        context = (context / total).astype(BF16)
-        keep_ref[:, q_cols] = context[:block]
-        send_ref[:, q_cols] = context[block:]
+        for h in heads
+    ]
+    scores = [score + bias[...] for score in scores]
+    tops = [jnp.max(score, axis=-1, keepdims=True) for score in scores]
+    weights = [jnp.exp2((score - top) * factor) for score, top in zip(scores, tops)]
+    totals = [jnp.sum(weight, axis=-1, keepdims=True) for weight in weights]
+    for h in heads:
+        value = rows_of(kvs, columns[2 * h + 1])
+        context = jnp.dot(weights[h].astype(BF16), value, preferred_element_type=F32)
+        context = (context / totals[h]).astype(BF16)
+        keep_ref[:, columns[h]] = context[:block]
+        send_ref[:, columns[h]] = context[block:]
 
 
 def attend_near_kernel(seg, q, kv_near, kv_far, kv_last, keep, send, bias, *, head_dim):
@@ -449,6 +458,42 @@
         0,
         [pltpu.VMEM((rows, base.shape[1]), BF16)],
     )
+
+
+def combine_last_kernel(base_ref, weigh_ref, *refs, spans):
+    *ins, out_ref, rows, result, sems = refs
+    join_rows(ins, spans, rows)
+    tile = result.shape[1] // sems.shape[0]
+    copies = []
+    for n in range(sems.shape[0]):
+        columns = slice(n * tile, (n + 1) * tile)
+        total = jnp.dot(weigh_ref[...], rows[:, columns], preferred_element_type=F32)
+        result[:, columns] = (base_ref[:, columns].astype(F32) + total).astype(BF16)
+        window = pl.ds(n * tile, tile)
+        copies.append(
+            pltpu.make_async_copy(result.at[:, window], out_ref.at[0, :, window], sems.at[n])
+        )
+        copies[-1].start()
+    for copy in copies:
+        copy.wait()
+
+
+def combine_last(base, weights, parts):
+    arrays, spans, rows = split(parts)
+    return pl.pallas_call(
+        functools.partial(combine_last_kernel, spans=spans),
+        out_shape=array((1,) + base.shape),
+        in_specs=[VMEM_SPEC] * (2 + len(arrays)),
+        out_specs=pl.BlockSpec(memory_space=pl.ANY),
+        scratch_shapes=[
+            pltpu.VMEM((rows, base.shape[1]), BF16),
+            pltpu.VMEM(base.shape, BF16),
+            pltpu.SemaphoreType.DMA((4,)),
+        ],
+        compiler_params=pltpu.CompilerParams(vmem_limit_bytes=max(8, rows * 16384 >> 20) << 20),
+        cost_estimate=pl.CostEstimate(flops=0, bytes_accessed=0, transcendentals=0),
+        name="combine_last",
+    )(base, weights, *arrays)
 
 
 def on_device(
@@ -536,8 +581,8 @@
     total = combine(resid, weights[0], [full(block) for block in back_first], F32)
     kv_cache, total = lax.optimization_barrier((kv_cache, total))
     parts = [full(block) for block in (*back_last, *back_near)]
-    total = combine(total, weights[1], parts, BF16)
-    return (total[None], kv_cache)
+    residual_out = combine_last(total, weights[1], parts)
+    return (residual_out, kv_cache)
 
 
 def solution(mesh):

time: 113 us -> 112 us (level)
  starting transfers between devices: 44.1 us -> 56 us
  waiting for transfers between devices: 37.1 us -> 26.1 us
  Pallas kernels: 25 us -> 23 us
    ppermute x23, starting transfers between devices: 40.6 us -> 52.5 us  [swap(): return lax.ppermute(value, axis, [(i, i ^ step) for i in range(size)])]
    ppermute x2, waiting for transfers between devices: 8.06 us -> 0.01 us  [to_owner(): return lax.ppermute(page, ('seq', 'blk'), pairs)]
    pallas_call x19 -> x18, Pallas kernels: 25 us -> 21.9 us  [call(): pl.pallas_call(kernel, out_shape=out_shape, in_specs=[SMEM_SPEC] * scalar...]
    ppermute x23, waiting for transfers between devices: 29 us -> 26.1 us  [swap(): return lax.ppermute(value, axis, [(i, i ^ step) for i in range(size)])]
    pallas_call x0 -> x1, Pallas kernels: none -> 1.14 us  [combine_last(): pl.pallas_call(functools.partial(combine_last_kernel, spans=spans), out_s...]
  transfers between devices with their start and end apart: 25 -> 25, of which waited for: 11 -> 9; matrix products, arithmetic and copies ran while one was open for 5% -> 5% of each run, Pallas kernels for 21% -> 19%
where the time goes in v7:
time: 112 us
  starting transfers between devices  56 us (50%)
  waiting for transfers between devices  26.1 us (23%)
  Pallas kernels  23 us (21%)
  local copies, waits for them, and re-layouts  5.43 us (5%)
    ppermute x23, starting transfers between devices, swap(): return lax.ppermute(value, axis, [(i, i ^ step) for i in range(size)])  52.5 us
    ppermute x23, waiting for transfers between devices, swap(): return lax.ppermute(value, axis, [(i, i ^ step) for i in range(size)])  26.1 us
    pallas_call x18, Pallas kernels, call(): pl.pallas_call(kernel, out_shape=out_shape, in_specs=[SMEM_SPEC] * scalar...  21.9 us
    unnamed x19, local copies, waits for them, and re-layouts  4.05 us
    ppermute x2, starting transfers between devices, to_owner(): return lax.ppermute(page, ('seq', 'blk'), pairs)  3.5 us
  transfers between devices with their start and end apart: 25, of which 9 were waited for; matrix products, arithmetic and copies ran while one was open for 5% of the time, Pallas kernels for 19%

profile of v7, /device:TPU:0, one launch (start us, length us, event | category | flops | bytes accessed | tf_op | source)
XLA Modules:
  0.0 111.7 jit_solution(1394901380577663410)
XLA Ops:
  1.2 2.9 %collective-permute-start = (bf16[128,2048]{1,0:T(8,128)(2,1)}, bf16[128,2048]{1,0:T(8,128)(2,1)S(1)}, u32[]{:S(2)}, u32[]{:S(2)}) collective-permute-start(bf16[128,2048]{1,0:T(8,128)(2,1)} %bitcast.18), channel_id=1, source_target_pairs={{0,16},{8,24},{16,0},{24,8},{1,17},{9,25},{17,1},{25,9},{2,18},{10... | collective-permute-start | bytes 1572872 | tf_op jit(solution)/shard_map/ppermute | solution.py:26
  5.5 4.0 %copy.13 = bf16[256,8,4,384]{3,1,2,0:T(8,128)(2,1)S(1)} copy(bf16[256,8,4,384]{3,2,1,0:T(4,128)(2,1)} %bitcast.32) | data formatting | bytes 12582912
  9.6 2.0 %project.2 = (bf16[256,512]{1,0:T(8,128)(2,1)S(1)}, bf16[256,1024]{1,0:T(8,128)(2,1)S(1)}) custom-call(bf16[128,2048]{1,0:T(8,128)(2,1)S(1)} %bitcast.19, bf16[128,2048]{1,0:T(8,128)(2,1)S(1)} %collective-permute-done.1.refs_1_, bf16[2,2048]{1,0:T(2,128)(2,1)S(1)} %pad_maximum_fusion.refs_2_.refs_1_.gain.gain_ref, bf16[2048,1536]{1,0:T(8,128)(2,1)S(1)} %bitcast.10), custom_call_target="tpu_custom_call" | custom-call | tf_op jit(solution)/shard_map/project/pallas_call | solution.py:38
  11.6 4.9 %collective-permute-done.refs_0_.refs_2_ = bf16[128,2048]{1,0:T(8,128)(2,1)S(1)} collective-permute-done((bf16[128,2048]{1,0:T(8,128)(2,1)}, bf16[128,2048]{1,0:T(8,128)(2,1)S(1)}, u32[]{:S(2)}, u32[]{:S(2)}) %collective-permute-start) | collective-permute-done | bytes 524320 | tf_op jit(solution)/shard_map/ppermute | solution.py:26
  18.4 2.1 %attend_far.1 = (bf16[128,512]{1,0:T(8,128)(2,1)S(1)}, bf16[128,512]{1,0:T(8,128)(2,1)S(1)}, bf16[128,1024]{1,0:T(8,128)(2,1)S(1)}) custom-call(s32[1,512]{1,0:T(1,128)S(1)} %copy-done.3, bf16[128,512]{1,0:T(8,128)(2,1)S(1)} %get-tuple-element.71.q_far, bf16[256,1024]{1,0:T(8,128)(2,1)S(1)} %get-tuple-element.68.kv_near, ...), custom_call_target="tpu_custom_call" | custom-call | tf_op jit(solution)/shard_map/attend_far/pallas_call | solution.py:38
  22.6 1.8 %collective-permute-start.6 = (bf16[128,2048]{1,0:T(8,128)(2,1)S(1)}, bf16[128,2048]{1,0:T(8,128)(2,1)S(1)}, u32[]{:S(2)}, u32[]{:S(2)}) collective-permute-start(bf16[128,2048]{1,0:T(8,128)(2,1)S(1)} %out_project.3), channel_id=1, source_target_pairs={{0,16},{8,24},{16,0},{24,8},{1,17},{9,25},{17,1},{25,9},{2,18},{10... | collective-permute-start | bytes 1572872 | tf_op jit(solution)/shard_map/ppermute | solution.py:26
  25.8 2.7 %collective-permute-start.7 = (bf16[64,2048]{1,0:T(8,128)(2,1)S(1)}, bf16[64,2048]{1,0:T(8,128)(2,1)S(1)}, u32[]{:S(2)}, u32[]{:S(2)}) collective-permute-start(bf16[64,2048]{1,0:T(8,128)(2,1)S(1)} %get-tuple-element.90), channel_id=1, source_target_pairs={{0,4},{1,5},{2,6},{3,7},{4,0},{5,1},{6,2},{7,3},{8,13},{9,12},{10,... | collective-permute-start | bytes 786440 | tf_op jit(solution)/shard_map/ppermute | solution.py:293
  30.1 6.6 %collective-permute-done.6.far_ref = bf16[128,2048]{1,0:T(8,128)(2,1)S(1)} collective-permute-done((bf16[128,2048]{1,0:T(8,128)(2,1)S(1)}, bf16[128,2048]{1,0:T(8,128)(2,1)S(1)}, u32[]{:S(2)}, u32[]{:S(2)}) %collective-permute-start.6) | collective-permute-done | bytes 524320 | tf_op jit(solution)/shard_map/ppermute | solution.py:26
  37.3 2.9 %collective-permute-start.12 = (bf16[48,2048]{1,0:T(8,128)(2,1)S(1)}, bf16[48,2048]{1,0:T(8,128)(2,1)S(1)}, u32[]{:S(2)}, u32[]{:S(2)}) collective-permute-start(bf16[48,2048]{1,0:T(8,128)(2,1)S(1)} %get-tuple-element.98), channel_id=1, source_target_pairs={{0,4},{1,5},{2,6},{3,7},{4,0},{5,1},{6,2},{7,3},{8,12},{9,13},{10,... | collective-permute-start | bytes 589832 | tf_op jit(solution)/shard_map/ppermute | solution.py:26
  43.1 8.6 %collective-permute-start.10 = (bf16[48,2048]{1,0:T(8,128)(2,1)S(1)}, bf16[48,2048]{1,0:T(8,128)(2,1)S(1)}, u32[]{:S(2)}, u32[]{:S(2)}) collective-permute-start(bf16[48,2048]{1,0:T(8,128)(2,1)S(1)} %get-tuple-element.96), channel_id=1, source_target_pairs={{0,2},{1,3},{2,0},{3,1},{4,6},{5,7},{6,4},{7,5},{8,10},{9,11},{10,... | collective-permute-start | bytes 589832 | tf_op jit(solution)/shard_map/ppermute | solution.py:26
  52.2 2.1 %collective-permute-done.12.refs_0_ = bf16[48,2048]{1,0:T(8,128)(2,1)S(1)} collective-permute-done((bf16[48,2048]{1,0:T(8,128)(2,1)S(1)}, bf16[48,2048]{1,0:T(8,128)(2,1)S(1)}, u32[]{:S(2)}, u32[]{:S(2)}) %collective-permute-start.12) | collective-permute-done | bytes 196640 | tf_op jit(solution)/shard_map/ppermute | solution.py:26
  54.3 3.4 %collective-permute-start.15 = (bf16[48,2048]{1,0:T(8,128)(2,1)S(1)}, bf16[48,2048]{1,0:T(8,128)(2,1)S(1)}, u32[]{:S(2)}, u32[]{:S(2)}) collective-permute-start(bf16[48,2048]{1,0:T(8,128)(2,1)S(1)} %get-tuple-element.111), channel_id=1, source_target_pairs={{0,6},{1,7},{2,4},{3,5},{4,2},{5,3},{6,0},{7,1},{8,14},{9,15},{10,... | collective-permute-start | bytes 589832 | tf_op jit(solution)/shard_map/ppermute | solution.py:26
  59.5 5.7 %collective-permute-start.14 = (bf16[128,2048]{1,0:T(8,128)(2,1)S(1)}, bf16[128,2048]{1,0:T(8,128)(2,1)S(1)}, u32[]{:S(2)}, u32[]{:S(2)}) collective-permute-start(bf16[128,2048]{1,0:T(8,128)(2,1)S(1)} %join.2.refs_0_), channel_id=1, source_target_pairs={{0,16},{8,24},{16,0},{24,8},{1,17},{9,25},{17,1},{25,9},{2,18},{10... | collective-permute-start | bytes 1572872 | tf_op jit(solution)/shard_map/ppermute | solution.py:26
  65.1 2.2 %expert.3 = (bf16[48,2048]{1,0:T(8,128)(2,1)S(1)}, bf16[48,2048]{1,0:T(8,128)(2,1)S(1)}) custom-call(bf16[48,2048]{1,0:T(8,128)(2,1)S(1)} %collective-permute-done.12.refs_0_, bf16[48,2048]{1,0:T(8,128)(2,1)S(1)} %collective-permute-done.13.refs_1_, bf16[2048,2048]{1,0:T(8,128)(2,1)S(1)} %bitcast.25, bf16[1024,2048]{1,0:T(8,128)(2,1)S(1)} %bitcast.28), custom_call_target="tpu_custom_call" | custom-call | flops 34359738368 | tf_op jit(solution)/shard_map/expert/pallas_call | solution.py:38
  67.3 3.9 %collective-permute-start.16 = (bf16[48,2048]{1,0:T(8,128)(2,1)S(1)}, bf16[48,2048]{1,0:T(8,128)(2,1)S(1)}, u32[]{:S(2)}, u32[]{:S(2)}) collective-permute-start(bf16[48,2048]{1,0:T(8,128)(2,1)S(1)} %get-tuple-element.112), channel_id=1, source_target_pairs={{0,7},{1,6},{2,5},{3,4},{4,3},{5,2},{6,1},{7,0},{8,15},{9,14},{10,... | collective-permute-start | bytes 589832 | tf_op jit(solution)/shard_map/ppermute | solution.py:26
  71.2 2.4 %collective-permute-done.11.refs_3_ = bf16[48,2048]{1,0:T(8,128)(2,1)S(1)} collective-permute-done((bf16[48,2048]{1,0:T(8,128)(2,1)S(1)}, bf16[48,2048]{1,0:T(8,128)(2,1)S(1)}, u32[]{:S(2)}, u32[]{:S(2)}) %collective-permute-start.11) | collective-permute-done | bytes 196640 | tf_op jit(solution)/shard_map/ppermute | solution.py:26
  75.3 2.7 %expert.4 = (bf16[48,2048]{1,0:T(8,128)(2,1)S(1)}, bf16[48,2048]{1,0:T(8,128)(2,1)S(1)}, bf16[48,2048]{1,0:T(8,128)(2,1)S(1)}, bf16[48,2048]{1,0:T(8,128)(2,1)S(1)}) custom-call(bf16[48,2048]{1,0:T(8,128)(2,1)S(1)} %get-tuple-element.103.refs_0_, bf16[48,2048]{1,0:T(8,128)(2,1)S(1)} %collective-permute-done.9.refs_1_, ...), custom_call_target="tpu_custom_call" | custom-call | flops 34359738368 | tf_op jit(solution)/shard_map/expert/pallas_call | solution.py:38
  78.1 2.2 %expert.5 = (bf16[48,2048]{1,0:T(8,128)(2,1)S(1)}, bf16[48,2048]{1,0:T(8,128)(2,1)S(1)}) custom-call(bf16[48,2048]{1,0:T(8,128)(2,1)S(1)} %collective-permute-done.15.refs_0_, bf16[48,2048]{1,0:T(8,128)(2,1)S(1)} %collective-permute-done.16.refs_1_, bf16[2048,2048]{1,0:T(8,128)(2,1)S(1)} %bitcast.27, bf16[1024,2048]{1,0:T(8,128)(2,1)S(1)} %bitcast.30), custom_call_target="tpu_custom_call" | custom-call | flops 34359738368 | tf_op jit(solution)/shard_map/expert/pallas_call | solution.py:38
  80.3 2.0 %collective-permute-start.20 = (bf16[48,2048]{1,0:T(8,128)(2,1)S(1)}, bf16[48,2048]{1,0:T(8,128)(2,1)S(1)}, u32[]{:S(2)}, u32[]{:S(2)}) collective-permute-start(bf16[48,2048]{1,0:T(8,128)(2,1)S(1)} %get-tuple-element.115), channel_id=1, source_target_pairs={{0,6},{1,7},{2,4},{3,5},{4,2},{5,3},{6,0},{7,1},{8,14},{9,15},{10,... | collective-permute-start | bytes 589832 | tf_op jit(solution)/shard_map/ppermute | solution.py:26
  83.3 10.6 %collective-permute-start.23 = (bf16[48,2048]{1,0:T(8,128)(2,1)S(1)}, bf16[48,2048]{1,0:T(8,128)(2,1)S(1)}, u32[]{:S(2)}, u32[]{:S(2)}) collective-permute-start(bf16[48,2048]{1,0:T(8,128)(2,1)S(1)} %get-tuple-element.125), channel_id=1, source_target_pairs={{0,2},{1,3},{2,0},{3,1},{4,6},{5,7},{6,4},{7,5},{8,10},{9,11},{10,... | collective-permute-start | bytes 589832 | tf_op jit(solution)/shard_map/ppermute | solution.py:26
  95.4 2.7 %collective-permute-done.19.refs_1_ = bf16[48,2048]{1,0:T(8,128)(2,1)S(1)} collective-permute-done((bf16[48,2048]{1,0:T(8,128)(2,1)S(1)}, bf16[48,2048]{1,0:T(8,128)(2,1)S(1)}, u32[]{:S(2)}, u32[]{:S(2)}) %collective-permute-start.19) | collective-permute-done | bytes 196640 | tf_op jit(solution)/shard_map/ppermute | solution.py:26
  98.0 2.9 %collective-permute-start.21 = (bf16[48,2048]{1,0:T(8,128)(2,1)S(1)}, bf16[48,2048]{1,0:T(8,128)(2,1)S(1)}, u32[]{:S(2)}, u32[]{:S(2)}) collective-permute-start(bf16[48,2048]{1,0:T(8,128)(2,1)S(1)} %get-tuple-element.116), channel_id=1, source_target_pairs={{0,7},{1,6},{2,5},{3,4},{4,3},{5,2},{6,1},{7,0},{8,15},{9,14},{10,... | collective-permute-start | bytes 589832 | tf_op jit(solution)/shard_map/ppermute | solution.py:26
  101.7 4.1 %cache.1 = bf16[1,8,64,1024]{3,2,1,0:T(8,128)(2,1)} custom-call(bf16[256,2048]{1,0:T(8,128)(2,1)S(1)} %join.3.mine_ref, bf16[256,2048]{1,0:T(8,128)(2,1)S(1)} %collective-permute-done.17.theirs_ref, bf16[2,2048]{1,0:T(2,128)(2,1)S(1)} %pad_maximum_fusion.refs_2_.refs_1_.gain.gain_ref, bf16[2048,1536]{1,0:T(8,128)(2,1)S(1)} %bitcast.13), custom_call_target="tpu_custom_call" | custom-call | tf_op jit(solution)/shard_map/cache/pallas_call | solution.py:38
  105.8 4.5 %collective-permute-done.24.refs_5_ = bf16[48,2048]{1,0:T(8,128)(2,1)S(1)} collective-permute-done((bf16[48,2048]{1,0:T(8,128)(2,1)S(1)}, bf16[48,2048]{1,0:T(8,128)(2,1)S(1)}, u32[]{:S(2)}, u32[]{:S(2)}) %collective-permute-start.24) | collective-permute-done | bytes 196640 | tf_op jit(solution)/shard_map/ppermute | solution.py:26
  (68 shorter events, 20.8 us)
Async XLA Ops:
  0.6 21.3 %collective-permute-start.5 = (bf16[512,2048]{1,0:T(8,128)(2,1)}, bf16[512,2048]{1,0:T(8,128)(2,1)S(1)}, u32[]{:S(2)}, u32[]{:S(2)}) collective-permute-start(bf16[512,2048]{1,0:T(8,128)(2,1)} %bitcast.14), channel_id=1, source_target_pairs={{0,8},{8,0},{16,24},{24,16},{1,9},{9,1},{17,25},{25,17},{2,10},{10... | collective-permute-start | bytes 6291464 | tf_op jit(solution)/shard_map/ppermute | solution.py:26
  1.1 8.4 %collective-permute-start.1 = (bf16[128,2048]{1,0:T(8,128)(2,1)}, bf16[128,2048]{1,0:T(8,128)(2,1)S(1)}, u32[]{:S(2)}, u32[]{:S(2)}) collective-permute-start(bf16[128,2048]{1,0:T(8,128)(2,1)} %bitcast.17), channel_id=1, source_target_pairs={{0,8},{8,0},{16,24},{24,16},{1,9},{9,1},{17,25},{25,17},{2,10},{10... | collective-permute-start | bytes 1572872 | tf_op jit(solution)/shard_map/ppermute | solution.py:26
  1.2 15.3 %collective-permute-start = (bf16[128,2048]{1,0:T(8,128)(2,1)}, bf16[128,2048]{1,0:T(8,128)(2,1)S(1)}, u32[]{:S(2)}, u32[]{:S(2)}) collective-permute-start(bf16[128,2048]{1,0:T(8,128)(2,1)} %bitcast.18), channel_id=1, source_target_pairs={{0,16},{8,24},{16,0},{24,8},{1,17},{9,25},{17,1},{25,9},{2,18},{10... | collective-permute-start | bytes 1572872 | tf_op jit(solution)/shard_map/ppermute | solution.py:26
  16.5 1.9 %collective-permute-start.2 = (bf16[128,2048]{1,0:T(8,128)(2,1)S(1)}, bf16[128,2048]{1,0:T(8,128)(2,1)S(1)}, u32[]{:S(2)}, u32[]{:S(2)}) collective-permute-start(bf16[128,2048]{1,0:T(8,128)(2,1)S(1)} %collective-permute-done.refs_0_.refs_2_), channel_id=1, source_target_pairs={{0,8},{8,0},{16,24},{24,16},{1,9},{9,1},{17,25},{25,17},{2,10},{10... | collective-permute-start | bytes 1572872 | tf_op jit(solution)/shard_map/ppermute | solution.py:26
  22.6 14.0 %collective-permute-start.6 = (bf16[128,2048]{1,0:T(8,128)(2,1)S(1)}, bf16[128,2048]{1,0:T(8,128)(2,1)S(1)}, u32[]{:S(2)}, u32[]{:S(2)}) collective-permute-start(bf16[128,2048]{1,0:T(8,128)(2,1)S(1)} %out_project.3), channel_id=1, source_target_pairs={{0,16},{8,24},{16,0},{24,8},{1,17},{9,25},{17,1},{25,9},{2,18},{10... | collective-permute-start | bytes 1572872 | tf_op jit(solution)/shard_map/ppermute | solution.py:26
  25.6 3.8 %collective-permute-start.4 = (bf16[128,512]{1,0:T(8,128)(2,1)S(1)}, bf16[128,512]{1,0:T(8,128)(2,1)S(1)}, u32[]{:S(2)}, u32[]{:S(2)}) collective-permute-start(bf16[128,512]{1,0:T(8,128)(2,1)S(1)} %get-tuple-element.80), channel_id=1, source_target_pairs={{0,8},{8,0},{16,24},{24,16},{1,9},{9,1},{17,25},{25,17},{2,10},{10... | collective-permute-start | bytes 393224 | tf_op jit(solution)/shard_map/ppermute | solution.py:26
  25.8 16.1 %collective-permute-start.7 = (bf16[64,2048]{1,0:T(8,128)(2,1)S(1)}, bf16[64,2048]{1,0:T(8,128)(2,1)S(1)}, u32[]{:S(2)}, u32[]{:S(2)}) collective-permute-start(bf16[64,2048]{1,0:T(8,128)(2,1)S(1)} %get-tuple-element.90), channel_id=1, source_target_pairs={{0,4},{1,5},{2,6},{3,7},{4,0},{5,1},{6,2},{7,3},{8,13},{9,12},{10,... | collective-permute-start | bytes 786440 | tf_op jit(solution)/shard_map/ppermute | solution.py:293
  28.5 13.5 %collective-permute-start.8 = (bf16[64,2048]{1,0:T(8,128)(2,1)S(1)}, bf16[64,2048]{1,0:T(8,128)(2,1)S(1)}, u32[]{:S(2)}, u32[]{:S(2)}) collective-permute-start(bf16[64,2048]{1,0:T(8,128)(2,1)S(1)} %get-tuple-element.91), channel_id=1, source_target_pairs={{0,0},{1,1},{2,2},{3,3},{4,4},{5,5},{6,6},{7,7},{8,9},{9,8},{10,11... | collective-permute-start | bytes 786440 | tf_op jit(solution)/shard_map/ppermute | solution.py:293
  37.3 17.0 %collective-permute-start.12 = (bf16[48,2048]{1,0:T(8,128)(2,1)S(1)}, bf16[48,2048]{1,0:T(8,128)(2,1)S(1)}, u32[]{:S(2)}, u32[]{:S(2)}) collective-permute-start(bf16[48,2048]{1,0:T(8,128)(2,1)S(1)} %get-tuple-element.98), channel_id=1, source_target_pairs={{0,4},{1,5},{2,6},{3,7},{4,0},{5,1},{6,2},{7,3},{8,12},{9,13},{10,... | collective-permute-start | bytes 589832 | tf_op jit(solution)/shard_map/ppermute | solution.py:26
  40.2 19.3 %collective-permute-start.13 = (bf16[48,2048]{1,0:T(8,128)(2,1)S(1)}, bf16[48,2048]{1,0:T(8,128)(2,1)S(1)}, u32[]{:S(2)}, u32[]{:S(2)}) collective-permute-start(bf16[48,2048]{1,0:T(8,128)(2,1)S(1)} %get-tuple-element.99), channel_id=1, source_target_pairs={{0,5},{1,4},{2,7},{3,6},{4,1},{5,0},{6,3},{7,2},{8,13},{9,12},{10,... | collective-permute-start | bytes 589832 | tf_op jit(solution)/shard_map/ppermute | solution.py:26
  42.0 25.4 %collective-permute-start.9 = (bf16[48,2048]{1,0:T(8,128)(2,1)S(1)}, bf16[48,2048]{1,0:T(8,128)(2,1)S(1)}, u32[]{:S(2)}, u32[]{:S(2)}) collective-permute-start(bf16[48,2048]{1,0:T(8,128)(2,1)S(1)} %get-tuple-element.95), channel_id=1, source_target_pairs={{0,1},{1,0},{2,3},{3,2},{4,5},{5,4},{6,7},{7,6},{8,9},{9,8},{10,11... | collective-permute-start | bytes 589832 | tf_op jit(solution)/shard_map/ppermute | solution.py:26
  43.1 28.1 %collective-permute-start.10 = (bf16[48,2048]{1,0:T(8,128)(2,1)S(1)}, bf16[48,2048]{1,0:T(8,128)(2,1)S(1)}, u32[]{:S(2)}, u32[]{:S(2)}) collective-permute-start(bf16[48,2048]{1,0:T(8,128)(2,1)S(1)} %get-tuple-element.96), channel_id=1, source_target_pairs={{0,2},{1,3},{2,0},{3,1},{4,6},{5,7},{6,4},{7,5},{8,10},{9,11},{10,... | collective-permute-start | bytes 589832 | tf_op jit(solution)/shard_map/ppermute | solution.py:26
  51.7 21.9 %collective-permute-start.11 = (bf16[48,2048]{1,0:T(8,128)(2,1)S(1)}, bf16[48,2048]{1,0:T(8,128)(2,1)S(1)}, u32[]{:S(2)}, u32[]{:S(2)}) collective-permute-start(bf16[48,2048]{1,0:T(8,128)(2,1)S(1)} %get-tuple-element.97), channel_id=1, source_target_pairs={{0,3},{1,2},{2,1},{3,0},{4,7},{5,6},{6,5},{7,4},{8,11},{9,10},{10,... | collective-permute-start | bytes 589832 | tf_op jit(solution)/shard_map/ppermute | solution.py:26
  54.3 23.7 %collective-permute-start.15 = (bf16[48,2048]{1,0:T(8,128)(2,1)S(1)}, bf16[48,2048]{1,0:T(8,128)(2,1)S(1)}, u32[]{:S(2)}, u32[]{:S(2)}) collective-permute-start(bf16[48,2048]{1,0:T(8,128)(2,1)S(1)} %get-tuple-element.111), channel_id=1, source_target_pairs={{0,6},{1,7},{2,4},{3,5},{4,2},{5,3},{6,0},{7,1},{8,14},{9,15},{10,... | collective-permute-start | bytes 589832 | tf_op jit(solution)/shard_map/ppermute | solution.py:26
  59.5 15.7 %collective-permute-start.14 = (bf16[128,2048]{1,0:T(8,128)(2,1)S(1)}, bf16[128,2048]{1,0:T(8,128)(2,1)S(1)}, u32[]{:S(2)}, u32[]{:S(2)}) collective-permute-start(bf16[128,2048]{1,0:T(8,128)(2,1)S(1)} %join.2.refs_0_), channel_id=1, source_target_pairs={{0,16},{8,24},{16,0},{24,8},{1,17},{9,25},{17,1},{25,9},{2,18},{10... | collective-permute-start | bytes 1572872 | tf_op jit(solution)/shard_map/ppermute | solution.py:26
  67.3 10.7 %collective-permute-start.16 = (bf16[48,2048]{1,0:T(8,128)(2,1)S(1)}, bf16[48,2048]{1,0:T(8,128)(2,1)S(1)}, u32[]{:S(2)}, u32[]{:S(2)}) collective-permute-start(bf16[48,2048]{1,0:T(8,128)(2,1)S(1)} %get-tuple-element.112), channel_id=1, source_target_pairs={{0,7},{1,6},{2,5},{3,4},{4,3},{5,2},{6,1},{7,0},{8,15},{9,14},{10,... | collective-permute-start | bytes 589832 | tf_op jit(solution)/shard_map/ppermute | solution.py:26
  71.2 22.7 %collective-permute-start.18 = (bf16[48,2048]{1,0:T(8,128)(2,1)S(1)}, bf16[48,2048]{1,0:T(8,128)(2,1)S(1)}, u32[]{:S(2)}, u32[]{:S(2)}) collective-permute-start(bf16[48,2048]{1,0:T(8,128)(2,1)S(1)} %get-tuple-element.100), channel_id=1, source_target_pairs={{0,4},{1,5},{2,6},{3,7},{4,0},{5,1},{6,2},{7,3},{8,12},{9,13},{10,... | collective-permute-start | bytes 589832 | tf_op jit(solution)/shard_map/ppermute | solution.py:26
  73.6 24.4 %collective-permute-start.19 = (bf16[48,2048]{1,0:T(8,128)(2,1)S(1)}, bf16[48,2048]{1,0:T(8,128)(2,1)S(1)}, u32[]{:S(2)}, u32[]{:S(2)}) collective-permute-start(bf16[48,2048]{1,0:T(8,128)(2,1)S(1)} %get-tuple-element.101), channel_id=1, source_target_pairs={{0,5},{1,4},{2,7},{3,6},{4,1},{5,0},{6,3},{7,2},{8,13},{9,12},{10,... | collective-permute-start | bytes 589832 | tf_op jit(solution)/shard_map/ppermute | solution.py:26
  75.3 2.8 %collective-permute-start.17 = (bf16[256,2048]{1,0:T(8,128)(2,1)S(1)}, bf16[256,2048]{1,0:T(8,128)(2,1)S(1)}, u32[]{:S(2)}, u32[]{:S(2)}) collective-permute-start(bf16[256,2048]{1,0:T(8,128)(2,1)S(1)} %join.3.mine_ref), channel_id=1, source_target_pairs={{0,8},{8,0},{16,24},{24,16},{1,9},{9,1},{17,25},{25,17},{2,10},{10... | collective-permute-start | bytes 3145736 | tf_op jit(solution)/shard_map/ppermute | solution.py:26
  80.3 30.1 %collective-permute-start.20 = (bf16[48,2048]{1,0:T(8,128)(2,1)S(1)}, bf16[48,2048]{1,0:T(8,128)(2,1)S(1)}, u32[]{:S(2)}, u32[]{:S(2)}) collective-permute-start(bf16[48,2048]{1,0:T(8,128)(2,1)S(1)} %get-tuple-element.115), channel_id=1, source_target_pairs={{0,6},{1,7},{2,4},{3,5},{4,2},{5,3},{6,0},{7,1},{8,14},{9,15},{10,... | collective-permute-start | bytes 589832 | tf_op jit(solution)/shard_map/ppermute | solution.py:26
  82.3 23.6 %collective-permute-start.22 = (bf16[48,2048]{1,0:T(8,128)(2,1)S(1)}, bf16[48,2048]{1,0:T(8,128)(2,1)S(1)}, u32[]{:S(2)}, u32[]{:S(2)}) collective-permute-start(bf16[48,2048]{1,0:T(8,128)(2,1)S(1)} %get-tuple-element.124), channel_id=1, source_target_pairs={{0,1},{1,0},{2,3},{3,2},{4,5},{5,4},{6,7},{7,6},{8,9},{9,8},{10,11... | collective-permute-start | bytes 589832 | tf_op jit(solution)/shard_map/ppermute | solution.py:26
  83.3 22.5 %collective-permute-start.23 = (bf16[48,2048]{1,0:T(8,128)(2,1)S(1)}, bf16[48,2048]{1,0:T(8,128)(2,1)S(1)}, u32[]{:S(2)}, u32[]{:S(2)}) collective-permute-start(bf16[48,2048]{1,0:T(8,128)(2,1)S(1)} %get-tuple-element.125), channel_id=1, source_target_pairs={{0,2},{1,3},{2,0},{3,1},{4,6},{5,7},{6,4},{7,5},{8,10},{9,11},{10,... | collective-permute-start | bytes 589832 | tf_op jit(solution)/shard_map/ppermute | solution.py:26
  93.9 16.5 %collective-permute-start.24 = (bf16[48,2048]{1,0:T(8,128)(2,1)S(1)}, bf16[48,2048]{1,0:T(8,128)(2,1)S(1)}, u32[]{:S(2)}, u32[]{:S(2)}) collective-permute-start(bf16[48,2048]{1,0:T(8,128)(2,1)S(1)} %get-tuple-element.126), channel_id=1, source_target_pairs={{0,3},{1,2},{2,1},{3,0},{4,7},{5,6},{6,5},{7,4},{8,11},{9,10},{10,... | collective-permute-start | bytes 589832 | tf_op jit(solution)/shard_map/ppermute | solution.py:26
  98.0 12.3 %collective-permute-start.21 = (bf16[48,2048]{1,0:T(8,128)(2,1)S(1)}, bf16[48,2048]{1,0:T(8,128)(2,1)S(1)}, u32[]{:S(2)}, u32[]{:S(2)}) collective-permute-start(bf16[48,2048]{1,0:T(8,128)(2,1)S(1)} %get-tuple-element.116), channel_id=1, source_target_pairs={{0,7},{1,6},{2,5},{3,4},{4,3},{5,2},{6,1},{7,0},{8,15},{9,14},{10,... | collective-permute-start | bytes 589832 | tf_op jit(solution)/shard_map/ppermute | solution.py:26
  (10 other events, 122.5 us)

commit v8 on v7

--- a/solution.py
+++ b/solution.py
@@ -516,8 +516,8 @@
     blk_count = lax.axis_size("blk")
 
     slots = own.shape[0] * 3 // 8
-    half = (4 + blk_count) // 2
-    near, first, last = tuple(range(4)), tuple(range(4, half)), tuple(range(half, blk_count))
+    near = tuple(range(4))
+    first, last = tuple(range(4, blk_count, 2)), tuple(range(5, blk_count, 2))
     groups = (first, (*near, *last))
     picks = plan(routes[0].T, groups)
 
@@ -525,7 +525,7 @@
     w_mine = w_out.reshape(heads_here * head_dim, width)
     core = swap(own, "seq", 1)
     w_theirs = swap(w_mine, "seq", 1)
-    gains = jnp.stack([attn_gain, ffn_gain])
+    gains = jnp.stack([attn_gain, ffn_gain]).astype(F32)
 
     w_flat = held(w_qkv.reshape(width, heads_here * 3 * head_dim))
     q_near, kv_near = project((own, core), gains, w_flat, heads_here, head_dim)
@@ -573,7 +573,6 @@
     rows_last, both_core = lax.optimization_barrier((rows_last, both_core))
     last_out = work(rows_last)
     back_last = there(last, last_out)
-    near_out, last_out, both_core = lax.optimization_barrier((near_out, last_out, both_core))
     back_near = there(near, near_out)
     kv_cache = cache(both, both_core, gains, w_flat, blk_count, heads_here, head_dim)
 

time: 112 us -> 110 us (0.982)
  waiting for transfers between devices: 26.1 us -> 23.8 us
    ppermute x23, waiting for transfers between devices: 26.1 us -> 23.8 us  [swap(): return lax.ppermute(value, axis, [(i, i ^ step) for i in range(size)])]
where the time goes in v8:
time: 110 us; the launch traced here: 109 us
  starting transfers between devices  55.5 us (50%)
  waiting for transfers between devices  23.8 us (22%)
  Pallas kernels  22.9 us (21%)
  local copies, waits for them, and re-layouts  5.43 us (5%)
    ppermute x23, starting transfers between devices, swap(): return lax.ppermute(value, axis, [(i, i ^ step) for i in range(size)])  52 us
    ppermute x23, waiting for transfers between devices, swap(): return lax.ppermute(value, axis, [(i, i ^ step) for i in range(size)])  23.8 us
    pallas_call x18, Pallas kernels, call(): pl.pallas_call(kernel, out_shape=out_shape, in_specs=[SMEM_SPEC] * scalar...  21.8 us
    unnamed x19, local copies, waits for them, and re-layouts  4.05 us
    ppermute x2, starting transfers between devices, to_owner(): return lax.ppermute(page, ('seq', 'blk'), pairs)  3.5 us
  transfers between devices with their start and end apart: 25, of which 9 were waited for; matrix products, arithmetic and copies ran while one was open for 5% of the time, Pallas kernels for 19%

profile of v8, /device:TPU:0, one launch (start us, length us, event | category | flops | bytes accessed | tf_op | source)
XLA Modules:
  0.0 108.7 jit_solution(11591168950962947416)
XLA Ops:
  1.2 2.9 %collective-permute-start = (bf16[128,2048]{1,0:T(8,128)(2,1)}, bf16[128,2048]{1,0:T(8,128)(2,1)S(1)}, u32[]{:S(2)}, u32[]{:S(2)}) collective-permute-start(bf16[128,2048]{1,0:T(8,128)(2,1)} %bitcast.18), channel_id=1, source_target_pairs={{0,16},{8,24},{16,0},{24,8},{1,17},{9,25},{17,1},{25,9},{2,18},{10... | collective-permute-start | bytes 1572872 | tf_op jit(solution)/shard_map/ppermute | solution.py:26
  5.5 4.0 %copy.13 = bf16[256,8,4,384]{3,1,2,0:T(8,128)(2,1)S(1)} copy(bf16[256,8,4,384]{3,2,1,0:T(4,128)(2,1)} %bitcast.32) | data formatting | bytes 12582912
  9.6 2.0 %project.2 = (bf16[256,512]{1,0:T(8,128)(2,1)S(1)}, bf16[256,1024]{1,0:T(8,128)(2,1)S(1)}) custom-call(bf16[128,2048]{1,0:T(8,128)(2,1)S(1)} %bitcast.19, bf16[128,2048]{1,0:T(8,128)(2,1)S(1)} %collective-permute-done.1.refs_1_, f32[2,2048]{1,0:T(2,128)S(1)} %maximum_convert_fusion.refs_2_.refs_1_.gain.gain_ref, bf16[2048,1536]{1,0:T(8,128)(2,1)S(1)} %bitcast.10), custom_call_target="tpu_custom_call" | custom-call | tf_op jit(solution)/shard_map/project/pallas_call | solution.py:38
  11.6 4.9 %collective-permute-done.refs_0_.refs_2_ = bf16[128,2048]{1,0:T(8,128)(2,1)S(1)} collective-permute-done((bf16[128,2048]{1,0:T(8,128)(2,1)}, bf16[128,2048]{1,0:T(8,128)(2,1)S(1)}, u32[]{:S(2)}, u32[]{:S(2)}) %collective-permute-start) | collective-permute-done | bytes 524320 | tf_op jit(solution)/shard_map/ppermute | solution.py:26
  18.4 2.0 %attend_far.1 = (bf16[128,512]{1,0:T(8,128)(2,1)S(1)}, bf16[128,512]{1,0:T(8,128)(2,1)S(1)}, bf16[128,1024]{1,0:T(8,128)(2,1)S(1)}) custom-call(s32[1,512]{1,0:T(1,128)S(1)} %copy-done.3, bf16[128,512]{1,0:T(8,128)(2,1)S(1)} %get-tuple-element.66.q_far, bf16[256,1024]{1,0:T(8,128)(2,1)S(1)} %get-tuple-element.63.kv_near, ...), custom_call_target="tpu_custom_call" | custom-call | tf_op jit(solution)/shard_map/attend_far/pallas_call | solution.py:38
  22.6 1.8 %collective-permute-start.6 = (bf16[128,2048]{1,0:T(8,128)(2,1)S(1)}, bf16[128,2048]{1,0:T(8,128)(2,1)S(1)}, u32[]{:S(2)}, u32[]{:S(2)}) collective-permute-start(bf16[128,2048]{1,0:T(8,128)(2,1)S(1)} %out_project.3), channel_id=1, source_target_pairs={{0,16},{8,24},{16,0},{24,8},{1,17},{9,25},{17,1},{25,9},{2,18},{10... | collective-permute-start | bytes 1572872 | tf_op jit(solution)/shard_map/ppermute | solution.py:26
  25.8 2.7 %collective-permute-start.7 = (bf16[64,2048]{1,0:T(8,128)(2,1)S(1)}, bf16[64,2048]{1,0:T(8,128)(2,1)S(1)}, u32[]{:S(2)}, u32[]{:S(2)}) collective-permute-start(bf16[64,2048]{1,0:T(8,128)(2,1)S(1)} %get-tuple-element.85), channel_id=1, source_target_pairs={{0,4},{1,5},{2,6},{3,7},{4,0},{5,1},{6,2},{7,3},{8,13},{9,12},{10,... | collective-permute-start | bytes 786440 | tf_op jit(solution)/shard_map/ppermute | solution.py:293
  30.1 6.6 %collective-permute-done.6.far_ref = bf16[128,2048]{1,0:T(8,128)(2,1)S(1)} collective-permute-done((bf16[128,2048]{1,0:T(8,128)(2,1)S(1)}, bf16[128,2048]{1,0:T(8,128)(2,1)S(1)}, u32[]{:S(2)}, u32[]{:S(2)}) %collective-permute-start.6) | collective-permute-done | bytes 524320 | tf_op jit(solution)/shard_map/ppermute | solution.py:26
  37.3 2.9 %collective-permute-start.12 = (bf16[48,2048]{1,0:T(8,128)(2,1)S(1)}, bf16[48,2048]{1,0:T(8,128)(2,1)S(1)}, u32[]{:S(2)}, u32[]{:S(2)}) collective-permute-start(bf16[48,2048]{1,0:T(8,128)(2,1)S(1)} %get-tuple-element.93), channel_id=1, source_target_pairs={{0,4},{1,5},{2,6},{3,7},{4,0},{5,1},{6,2},{7,3},{8,12},{9,13},{10,... | collective-permute-start | bytes 589832 | tf_op jit(solution)/shard_map/ppermute | solution.py:26
  42.0 1.6 %collective-permute-start.9 = (bf16[48,2048]{1,0:T(8,128)(2,1)S(1)}, bf16[48,2048]{1,0:T(8,128)(2,1)S(1)}, u32[]{:S(2)}, u32[]{:S(2)}) collective-permute-start(bf16[48,2048]{1,0:T(8,128)(2,1)S(1)} %get-tuple-element.90), channel_id=1, source_target_pairs={{0,1},{1,0},{2,3},{3,2},{4,5},{5,4},{6,7},{7,6},{8,9},{9,8},{10,11... | collective-permute-start | bytes 589832 | tf_op jit(solution)/shard_map/ppermute | solution.py:26
  43.6 8.1 %collective-permute-start.10 = (bf16[48,2048]{1,0:T(8,128)(2,1)S(1)}, bf16[48,2048]{1,0:T(8,128)(2,1)S(1)}, u32[]{:S(2)}, u32[]{:S(2)}) collective-permute-start(bf16[48,2048]{1,0:T(8,128)(2,1)S(1)} %get-tuple-element.91), channel_id=1, source_target_pairs={{0,2},{1,3},{2,0},{3,1},{4,6},{5,7},{6,4},{7,5},{8,10},{9,11},{10,... | collective-permute-start | bytes 589832 | tf_op jit(solution)/shard_map/ppermute | solution.py:26
  52.1 2.2 %collective-permute-done.12.refs_0_ = bf16[48,2048]{1,0:T(8,128)(2,1)S(1)} collective-permute-done((bf16[48,2048]{1,0:T(8,128)(2,1)S(1)}, bf16[48,2048]{1,0:T(8,128)(2,1)S(1)}, u32[]{:S(2)}, u32[]{:S(2)}) %collective-permute-start.12) | collective-permute-done | bytes 196640 | tf_op jit(solution)/shard_map/ppermute | solution.py:26
  54.3 1.8 %collective-permute-start.15 = (bf16[48,2048]{1,0:T(8,128)(2,1)S(1)}, bf16[48,2048]{1,0:T(8,128)(2,1)S(1)}, u32[]{:S(2)}, u32[]{:S(2)}) collective-permute-start(bf16[48,2048]{1,0:T(8,128)(2,1)S(1)} %get-tuple-element.98), channel_id=1, source_target_pairs={{0,5},{1,4},{2,7},{3,6},{4,1},{5,0},{6,3},{7,2},{8,13},{9,12},{10,... | collective-permute-start | bytes 589832 | tf_op jit(solution)/shard_map/ppermute | solution.py:26
  56.3 2.2 %expert.3 = (bf16[48,2048]{1,0:T(8,128)(2,1)S(1)}, bf16[48,2048]{1,0:T(8,128)(2,1)S(1)}) custom-call(bf16[48,2048]{1,0:T(8,128)(2,1)S(1)} %collective-permute-done.12.refs_0_, bf16[48,2048]{1,0:T(8,128)(2,1)S(1)} %collective-permute-done.13.refs_1_, bf16[2048,2048]{1,0:T(8,128)(2,1)S(1)} %bitcast.25, bf16[1024,2048]{1,0:T(8,128)(2,1)S(1)} %bitcast.28), custom_call_target="tpu_custom_call" | custom-call | flops 34359738368 | tf_op jit(solution)/shard_map/expert/pallas_call | solution.py:38
  58.4 3.8 %collective-permute-start.16 = (bf16[48,2048]{1,0:T(8,128)(2,1)S(1)}, bf16[48,2048]{1,0:T(8,128)(2,1)S(1)}, u32[]{:S(2)}, u32[]{:S(2)}) collective-permute-start(bf16[48,2048]{1,0:T(8,128)(2,1)S(1)} %get-tuple-element.99), channel_id=1, source_target_pairs={{0,7},{1,6},{2,5},{3,4},{4,3},{5,2},{6,1},{7,0},{8,15},{9,14},{10,... | collective-permute-start | bytes 589832 | tf_op jit(solution)/shard_map/ppermute | solution.py:26
  62.3 4.9 %collective-permute-start.18 = (bf16[48,2048]{1,0:T(8,128)(2,1)S(1)}, bf16[48,2048]{1,0:T(8,128)(2,1)S(1)}, u32[]{:S(2)}, u32[]{:S(2)}) collective-permute-start(bf16[48,2048]{1,0:T(8,128)(2,1)S(1)} %get-tuple-element.95), channel_id=1, source_target_pairs={{0,4},{1,5},{2,6},{3,7},{4,0},{5,1},{6,2},{7,3},{8,12},{9,13},{10,... | collective-permute-start | bytes 589832 | tf_op jit(solution)/shard_map/ppermute | solution.py:26
  67.3 3.4 %collective-permute-start.19 = (bf16[48,2048]{1,0:T(8,128)(2,1)S(1)}, bf16[48,2048]{1,0:T(8,128)(2,1)S(1)}, u32[]{:S(2)}, u32[]{:S(2)}) collective-permute-start(bf16[48,2048]{1,0:T(8,128)(2,1)S(1)} %get-tuple-element.96), channel_id=1, source_target_pairs={{0,6},{1,7},{2,4},{3,5},{4,2},{5,3},{6,0},{7,1},{8,14},{9,15},{10,... | collective-permute-start | bytes 589832 | tf_op jit(solution)/shard_map/ppermute | solution.py:26
  70.9 2.6 %expert.5 = (bf16[48,2048]{1,0:T(8,128)(2,1)S(1)}, bf16[48,2048]{1,0:T(8,128)(2,1)S(1)}, bf16[48,2048]{1,0:T(8,128)(2,1)S(1)}, bf16[48,2048]{1,0:T(8,128)(2,1)S(1)}) custom-call(bf16[48,2048]{1,0:T(8,128)(2,1)S(1)} %get-tuple-element.109.refs_0_, bf16[48,2048]{1,0:T(8,128)(2,1)S(1)} %collective-permute-done.9.refs_1_, ...), custom_call_target="tpu_custom_call" | custom-call | flops 34359738368 | tf_op jit(solution)/shard_map/expert/pallas_call | solution.py:38
  74.8 11.1 %collective-permute-start.23 = (bf16[48,2048]{1,0:T(8,128)(2,1)S(1)}, bf16[48,2048]{1,0:T(8,128)(2,1)S(1)}, u32[]{:S(2)}, u32[]{:S(2)}) collective-permute-start(bf16[48,2048]{1,0:T(8,128)(2,1)S(1)} %get-tuple-element.115), channel_id=1, source_target_pairs={{0,2},{1,3},{2,0},{3,1},{4,6},{5,7},{6,4},{7,5},{8,10},{9,11},{10,... | collective-permute-start | bytes 589832 | tf_op jit(solution)/shard_map/ppermute | solution.py:26
  86.7 2.2 %expert.4 = (bf16[48,2048]{1,0:T(8,128)(2,1)S(1)}, bf16[48,2048]{1,0:T(8,128)(2,1)S(1)}) custom-call(bf16[48,2048]{1,0:T(8,128)(2,1)S(1)} %collective-permute-done.15.refs_0_, bf16[48,2048]{1,0:T(8,128)(2,1)S(1)} %collective-permute-done.16.refs_1_, bf16[2048,2048]{1,0:T(8,128)(2,1)S(1)} %bitcast.27, bf16[1024,2048]{1,0:T(8,128)(2,1)S(1)} %bitcast.30), custom_call_target="tpu_custom_call" | custom-call | flops 34359738368 | tf_op jit(solution)/shard_map/expert/pallas_call | solution.py:38
  89.4 3.4 %collective-permute-start.20 = (bf16[48,2048]{1,0:T(8,128)(2,1)S(1)}, bf16[48,2048]{1,0:T(8,128)(2,1)S(1)}, u32[]{:S(2)}, u32[]{:S(2)}) collective-permute-start(bf16[48,2048]{1,0:T(8,128)(2,1)S(1)} %get-tuple-element.107), channel_id=1, source_target_pairs={{0,5},{1,4},{2,7},{3,6},{4,1},{5,0},{6,3},{7,2},{8,13},{9,12},{10,... | collective-permute-start | bytes 589832 | tf_op jit(solution)/shard_map/ppermute | solution.py:26
  95.0 4.1 %cache.1 = bf16[1,8,64,1024]{3,2,1,0:T(8,128)(2,1)} custom-call(bf16[256,2048]{1,0:T(8,128)(2,1)S(1)} %join.3.mine_ref, bf16[256,2048]{1,0:T(8,128)(2,1)S(1)} %collective-permute-done.17.theirs_ref, f32[2,2048]{1,0:T(2,128)S(1)} %maximum_convert_fusion.refs_2_.refs_1_.gain.gain_ref, bf16[2048,1536]{1,0:T(8,128)(2,1)S(1)} %bitcast.13), custom_call_target="tpu_custom_call" | custom-call | tf_op jit(solution)/shard_map/cache/pallas_call | solution.py:38
  99.1 4.1 %collective-permute-done.24.refs_5_ = bf16[48,2048]{1,0:T(8,128)(2,1)S(1)} collective-permute-done((bf16[48,2048]{1,0:T(8,128)(2,1)S(1)}, bf16[48,2048]{1,0:T(8,128)(2,1)S(1)}, u32[]{:S(2)}, u32[]{:S(2)}) %collective-permute-start.24) | collective-permute-done | bytes 196640 | tf_op jit(solution)/shard_map/ppermute | solution.py:26
  103.2 4.2 %collective-permute-done.20.refs_0_ = bf16[48,2048]{1,0:T(8,128)(2,1)S(1)} collective-permute-done((bf16[48,2048]{1,0:T(8,128)(2,1)S(1)}, bf16[48,2048]{1,0:T(8,128)(2,1)S(1)}, u32[]{:S(2)}, u32[]{:S(2)}) %collective-permute-start.20) | collective-permute-done | bytes 196640 | tf_op jit(solution)/shard_map/ppermute | solution.py:26
  (68 shorter events, 18.2 us)
Async XLA Ops:
  0.6 21.3 %collective-permute-start.5 = (bf16[512,2048]{1,0:T(8,128)(2,1)}, bf16[512,2048]{1,0:T(8,128)(2,1)S(1)}, u32[]{:S(2)}, u32[]{:S(2)}) collective-permute-start(bf16[512,2048]{1,0:T(8,128)(2,1)} %bitcast.14), channel_id=1, source_target_pairs={{0,8},{8,0},{16,24},{24,16},{1,9},{9,1},{17,25},{25,17},{2,10},{10... | collective-permute-start | bytes 6291464 | tf_op jit(solution)/shard_map/ppermute | solution.py:26
  1.1 8.4 %collective-permute-start.1 = (bf16[128,2048]{1,0:T(8,128)(2,1)}, bf16[128,2048]{1,0:T(8,128)(2,1)S(1)}, u32[]{:S(2)}, u32[]{:S(2)}) collective-permute-start(bf16[128,2048]{1,0:T(8,128)(2,1)} %bitcast.17), channel_id=1, source_target_pairs={{0,8},{8,0},{16,24},{24,16},{1,9},{9,1},{17,25},{25,17},{2,10},{10... | collective-permute-start | bytes 1572872 | tf_op jit(solution)/shard_map/ppermute | solution.py:26
  1.2 15.3 %collective-permute-start = (bf16[128,2048]{1,0:T(8,128)(2,1)}, bf16[128,2048]{1,0:T(8,128)(2,1)S(1)}, u32[]{:S(2)}, u32[]{:S(2)}) collective-permute-start(bf16[128,2048]{1,0:T(8,128)(2,1)} %bitcast.18), channel_id=1, source_target_pairs={{0,16},{8,24},{16,0},{24,8},{1,17},{9,25},{17,1},{25,9},{2,18},{10... | collective-permute-start | bytes 1572872 | tf_op jit(solution)/shard_map/ppermute | solution.py:26
  16.5 1.9 %collective-permute-start.2 = (bf16[128,2048]{1,0:T(8,128)(2,1)S(1)}, bf16[128,2048]{1,0:T(8,128)(2,1)S(1)}, u32[]{:S(2)}, u32[]{:S(2)}) collective-permute-start(bf16[128,2048]{1,0:T(8,128)(2,1)S(1)} %collective-permute-done.refs_0_.refs_2_), channel_id=1, source_target_pairs={{0,8},{8,0},{16,24},{24,16},{1,9},{9,1},{17,25},{25,17},{2,10},{10... | collective-permute-start | bytes 1572872 | tf_op jit(solution)/shard_map/ppermute | solution.py:26
  22.6 14.0 %collective-permute-start.6 = (bf16[128,2048]{1,0:T(8,128)(2,1)S(1)}, bf16[128,2048]{1,0:T(8,128)(2,1)S(1)}, u32[]{:S(2)}, u32[]{:S(2)}) collective-permute-start(bf16[128,2048]{1,0:T(8,128)(2,1)S(1)} %out_project.3), channel_id=1, source_target_pairs={{0,16},{8,24},{16,0},{24,8},{1,17},{9,25},{17,1},{25,9},{2,18},{10... | collective-permute-start | bytes 1572872 | tf_op jit(solution)/shard_map/ppermute | solution.py:26
  25.6 3.8 %collective-permute-start.4 = (bf16[128,512]{1,0:T(8,128)(2,1)S(1)}, bf16[128,512]{1,0:T(8,128)(2,1)S(1)}, u32[]{:S(2)}, u32[]{:S(2)}) collective-permute-start(bf16[128,512]{1,0:T(8,128)(2,1)S(1)} %get-tuple-element.75), channel_id=1, source_target_pairs={{0,8},{8,0},{16,24},{24,16},{1,9},{9,1},{17,25},{25,17},{2,10},{10... | collective-permute-start | bytes 393224 | tf_op jit(solution)/shard_map/ppermute | solution.py:26
  25.8 16.2 %collective-permute-start.7 = (bf16[64,2048]{1,0:T(8,128)(2,1)S(1)}, bf16[64,2048]{1,0:T(8,128)(2,1)S(1)}, u32[]{:S(2)}, u32[]{:S(2)}) collective-permute-start(bf16[64,2048]{1,0:T(8,128)(2,1)S(1)} %get-tuple-element.85), channel_id=1, source_target_pairs={{0,4},{1,5},{2,6},{3,7},{4,0},{5,1},{6,2},{7,3},{8,13},{9,12},{10,... | collective-permute-start | bytes 786440 | tf_op jit(solution)/shard_map/ppermute | solution.py:293
  28.5 13.5 %collective-permute-start.8 = (bf16[64,2048]{1,0:T(8,128)(2,1)S(1)}, bf16[64,2048]{1,0:T(8,128)(2,1)S(1)}, u32[]{:S(2)}, u32[]{:S(2)}) collective-permute-start(bf16[64,2048]{1,0:T(8,128)(2,1)S(1)} %get-tuple-element.86), channel_id=1, source_target_pairs={{0,0},{1,1},{2,2},{3,3},{4,4},{5,5},{6,6},{7,7},{8,9},{9,8},{10,11... | collective-permute-start | bytes 786440 | tf_op jit(solution)/shard_map/ppermute | solution.py:293
  37.3 17.0 %collective-permute-start.12 = (bf16[48,2048]{1,0:T(8,128)(2,1)S(1)}, bf16[48,2048]{1,0:T(8,128)(2,1)S(1)}, u32[]{:S(2)}, u32[]{:S(2)}) collective-permute-start(bf16[48,2048]{1,0:T(8,128)(2,1)S(1)} %get-tuple-element.93), channel_id=1, source_target_pairs={{0,4},{1,5},{2,6},{3,7},{4,0},{5,1},{6,2},{7,3},{8,12},{9,13},{10,... | collective-permute-start | bytes 589832 | tf_op jit(solution)/shard_map/ppermute | solution.py:26
  40.2 15.9 %collective-permute-start.13 = (bf16[48,2048]{1,0:T(8,128)(2,1)S(1)}, bf16[48,2048]{1,0:T(8,128)(2,1)S(1)}, u32[]{:S(2)}, u32[]{:S(2)}) collective-permute-start(bf16[48,2048]{1,0:T(8,128)(2,1)S(1)} %get-tuple-element.94), channel_id=1, source_target_pairs={{0,6},{1,7},{2,4},{3,5},{4,2},{5,3},{6,0},{7,1},{8,14},{9,15},{10,... | collective-permute-start | bytes 589832 | tf_op jit(solution)/shard_map/ppermute | solution.py:26
  42.0 16.4 %collective-permute-start.9 = (bf16[48,2048]{1,0:T(8,128)(2,1)S(1)}, bf16[48,2048]{1,0:T(8,128)(2,1)S(1)}, u32[]{:S(2)}, u32[]{:S(2)}) collective-permute-start(bf16[48,2048]{1,0:T(8,128)(2,1)S(1)} %get-tuple-element.90), channel_id=1, source_target_pairs={{0,1},{1,0},{2,3},{3,2},{4,5},{5,4},{6,7},{7,6},{8,9},{9,8},{10,11... | collective-permute-start | bytes 589832 | tf_op jit(solution)/shard_map/ppermute | solution.py:26
  43.6 18.6 %collective-permute-start.10 = (bf16[48,2048]{1,0:T(8,128)(2,1)S(1)}, bf16[48,2048]{1,0:T(8,128)(2,1)S(1)}, u32[]{:S(2)}, u32[]{:S(2)}) collective-permute-start(bf16[48,2048]{1,0:T(8,128)(2,1)S(1)} %get-tuple-element.91), channel_id=1, source_target_pairs={{0,2},{1,3},{2,0},{3,1},{4,6},{5,7},{6,4},{7,5},{8,10},{9,11},{10,... | collective-permute-start | bytes 589832 | tf_op jit(solution)/shard_map/ppermute | solution.py:26
  51.7 15.6 %collective-permute-start.11 = (bf16[48,2048]{1,0:T(8,128)(2,1)S(1)}, bf16[48,2048]{1,0:T(8,128)(2,1)S(1)}, u32[]{:S(2)}, u32[]{:S(2)}) collective-permute-start(bf16[48,2048]{1,0:T(8,128)(2,1)S(1)} %get-tuple-element.92), channel_id=1, source_target_pairs={{0,3},{1,2},{2,1},{3,0},{4,7},{5,6},{6,5},{7,4},{8,11},{9,10},{10,... | collective-permute-start | bytes 589832 | tf_op jit(solution)/shard_map/ppermute | solution.py:26
  54.3 19.2 %collective-permute-start.15 = (bf16[48,2048]{1,0:T(8,128)(2,1)S(1)}, bf16[48,2048]{1,0:T(8,128)(2,1)S(1)}, u32[]{:S(2)}, u32[]{:S(2)}) collective-permute-start(bf16[48,2048]{1,0:T(8,128)(2,1)S(1)} %get-tuple-element.98), channel_id=1, source_target_pairs={{0,5},{1,4},{2,7},{3,6},{4,1},{5,0},{6,3},{7,2},{8,13},{9,12},{10,... | collective-permute-start | bytes 589832 | tf_op jit(solution)/shard_map/ppermute | solution.py:26
  56.1 14.6 %collective-permute-start.14 = (bf16[128,2048]{1,0:T(8,128)(2,1)S(1)}, bf16[128,2048]{1,0:T(8,128)(2,1)S(1)}, u32[]{:S(2)}, u32[]{:S(2)}) collective-permute-start(bf16[128,2048]{1,0:T(8,128)(2,1)S(1)} %join.2.refs_0_), channel_id=1, source_target_pairs={{0,16},{8,24},{16,0},{24,8},{1,17},{9,25},{17,1},{25,9},{2,18},{10... | collective-permute-start | bytes 1572872 | tf_op jit(solution)/shard_map/ppermute | solution.py:26
  58.4 16.4 %collective-permute-start.16 = (bf16[48,2048]{1,0:T(8,128)(2,1)S(1)}, bf16[48,2048]{1,0:T(8,128)(2,1)S(1)}, u32[]{:S(2)}, u32[]{:S(2)}) collective-permute-start(bf16[48,2048]{1,0:T(8,128)(2,1)S(1)} %get-tuple-element.99), channel_id=1, source_target_pairs={{0,7},{1,6},{2,5},{3,4},{4,3},{5,2},{6,1},{7,0},{8,15},{9,14},{10,... | collective-permute-start | bytes 589832 | tf_op jit(solution)/shard_map/ppermute | solution.py:26
  62.3 27.2 %collective-permute-start.18 = (bf16[48,2048]{1,0:T(8,128)(2,1)S(1)}, bf16[48,2048]{1,0:T(8,128)(2,1)S(1)}, u32[]{:S(2)}, u32[]{:S(2)}) collective-permute-start(bf16[48,2048]{1,0:T(8,128)(2,1)S(1)} %get-tuple-element.95), channel_id=1, source_target_pairs={{0,4},{1,5},{2,6},{3,7},{4,0},{5,1},{6,2},{7,3},{8,12},{9,13},{10,... | collective-permute-start | bytes 589832 | tf_op jit(solution)/shard_map/ppermute | solution.py:26
  67.3 25.5 %collective-permute-start.19 = (bf16[48,2048]{1,0:T(8,128)(2,1)S(1)}, bf16[48,2048]{1,0:T(8,128)(2,1)S(1)}, u32[]{:S(2)}, u32[]{:S(2)}) collective-permute-start(bf16[48,2048]{1,0:T(8,128)(2,1)S(1)} %get-tuple-element.96), channel_id=1, source_target_pairs={{0,6},{1,7},{2,4},{3,5},{4,2},{5,3},{6,0},{7,1},{8,14},{9,15},{10,... | collective-permute-start | bytes 589832 | tf_op jit(solution)/shard_map/ppermute | solution.py:26
  70.8 15.1 %collective-permute-start.17 = (bf16[256,2048]{1,0:T(8,128)(2,1)S(1)}, bf16[256,2048]{1,0:T(8,128)(2,1)S(1)}, u32[]{:S(2)}, u32[]{:S(2)}) collective-permute-start(bf16[256,2048]{1,0:T(8,128)(2,1)S(1)} %join.3.mine_ref), channel_id=1, source_target_pairs={{0,8},{8,0},{16,24},{24,16},{1,9},{9,1},{17,25},{25,17},{2,10},{10... | collective-permute-start | bytes 3145736 | tf_op jit(solution)/shard_map/ppermute | solution.py:26
  73.5 25.6 %collective-permute-start.22 = (bf16[48,2048]{1,0:T(8,128)(2,1)S(1)}, bf16[48,2048]{1,0:T(8,128)(2,1)S(1)}, u32[]{:S(2)}, u32[]{:S(2)}) collective-permute-start(bf16[48,2048]{1,0:T(8,128)(2,1)S(1)} %get-tuple-element.114), channel_id=1, source_target_pairs={{0,1},{1,0},{2,3},{3,2},{4,5},{5,4},{6,7},{7,6},{8,9},{9,8},{10,11... | collective-permute-start | bytes 589832 | tf_op jit(solution)/shard_map/ppermute | solution.py:26
  74.8 24.3 %collective-permute-start.23 = (bf16[48,2048]{1,0:T(8,128)(2,1)S(1)}, bf16[48,2048]{1,0:T(8,128)(2,1)S(1)}, u32[]{:S(2)}, u32[]{:S(2)}) collective-permute-start(bf16[48,2048]{1,0:T(8,128)(2,1)S(1)} %get-tuple-element.115), channel_id=1, source_target_pairs={{0,2},{1,3},{2,0},{3,1},{4,6},{5,7},{6,4},{7,5},{8,10},{9,11},{10,... | collective-permute-start | bytes 589832 | tf_op jit(solution)/shard_map/ppermute | solution.py:26
  85.9 17.3 %collective-permute-start.24 = (bf16[48,2048]{1,0:T(8,128)(2,1)S(1)}, bf16[48,2048]{1,0:T(8,128)(2,1)S(1)}, u32[]{:S(2)}, u32[]{:S(2)}) collective-permute-start(bf16[48,2048]{1,0:T(8,128)(2,1)S(1)} %get-tuple-element.116), channel_id=1, source_target_pairs={{0,3},{1,2},{2,1},{3,0},{4,7},{5,6},{6,5},{7,4},{8,11},{9,10},{10,... | collective-permute-start | bytes 589832 | tf_op jit(solution)/shard_map/ppermute | solution.py:26
  89.4 17.9 %collective-permute-start.20 = (bf16[48,2048]{1,0:T(8,128)(2,1)S(1)}, bf16[48,2048]{1,0:T(8,128)(2,1)S(1)}, u32[]{:S(2)}, u32[]{:S(2)}) collective-permute-start(bf16[48,2048]{1,0:T(8,128)(2,1)S(1)} %get-tuple-element.107), channel_id=1, source_target_pairs={{0,5},{1,4},{2,7},{3,6},{4,1},{5,0},{6,3},{7,2},{8,13},{9,12},{10,... | collective-permute-start | bytes 589832 | tf_op jit(solution)/shard_map/ppermute | solution.py:26
  92.8 14.6 %collective-permute-start.21 = (bf16[48,2048]{1,0:T(8,128)(2,1)S(1)}, bf16[48,2048]{1,0:T(8,128)(2,1)S(1)}, u32[]{:S(2)}, u32[]{:S(2)}) collective-permute-start(bf16[48,2048]{1,0:T(8,128)(2,1)S(1)} %get-tuple-element.108), channel_id=1, source_target_pairs={{0,7},{1,6},{2,5},{3,4},{4,3},{5,2},{6,1},{7,0},{8,15},{9,14},{10,... | collective-permute-start | bytes 589832 | tf_op jit(solution)/shard_map/ppermute | solution.py:26
  (10 other events, 81.2 us)

commit v9 on v8

--- a/solution.py
+++ b/solution.py
@@ -141,11 +141,11 @@
     scores = [score + bias[...] for score in scores]
     tops = [jnp.max(score, axis=-1, keepdims=True) for score in scores]
     weights = [jnp.exp2((score - top) * factor) for score, top in zip(scores, tops)]
-    totals = [jnp.sum(weight, axis=-1, keepdims=True) for weight in weights]
+    ones = jnp.ones((row.shape[1], head_dim), BF16)
     for h in heads:
-        value = rows_of(kvs, columns[2 * h + 1])
+        value = jnp.concatenate([rows_of(kvs, columns[2 * h + 1]), ones], axis=1)
         context = jnp.dot(weights[h].astype(BF16), value, preferred_element_type=F32)
-        context = (context / totals[h]).astype(BF16)
+        context = (context[:, :head_dim] / context[:, head_dim:]).astype(BF16)
         keep_ref[:, columns[h]] = context[:block]
         send_ref[:, columns[h]] = context[block:]
 

time: 110 us -> 111 us (level)
  the two profiles are of different devices: /device:TPU:0 before, /device:TPU:16 now
where the time goes in v9:
time: 111 us
  starting transfers between devices  45.4 us (41%)
  waiting for transfers between devices  35.9 us (32%)
  Pallas kernels  22.7 us (20%)
  local copies, waits for them, and re-layouts  5.43 us (5%)
    ppermute x23, starting transfers between devices, swap(): return lax.ppermute(value, axis, [(i, i ^ step) for i in range(size)])  44.1 us
    ppermute x23, waiting for transfers between devices, swap(): return lax.ppermute(value, axis, [(i, i ^ step) for i in range(size)])  35.9 us
    pallas_call x18, Pallas kernels, call(): pl.pallas_call(kernel, out_shape=out_shape, in_specs=[SMEM_SPEC] * scalar...  21.5 us
    unnamed x19, local copies, waits for them, and re-layouts  4.05 us
  transfers between devices with their start and end apart: 25, of which 11 were waited for; matrix products, arithmetic and copies ran while one was open for 5% of the time, Pallas kernels for 19%

profile of v9, /device:TPU:16, one launch (start us, length us, event | category | flops | bytes accessed | tf_op | source)
XLA Modules:
  0.0 110.5 jit_solution(6985812451406758787)
XLA Ops:
  1.2 1.5 %collective-permute-start = (bf16[128,2048]{1,0:T(8,128)(2,1)}, bf16[128,2048]{1,0:T(8,128)(2,1)S(1)}, u32[]{:S(2)}, u32[]{:S(2)}) collective-permute-start(bf16[128,2048]{1,0:T(8,128)(2,1)} %bitcast.18), channel_id=1, source_target_pairs={{0,16},{8,24},{16,0},{24,8},{1,17},{9,25},{17,1},{25,9},{2,18},{10... | collective-permute-start | bytes 1572872 | tf_op jit(solution)/shard_map/ppermute | solution.py:26
  4.1 4.0 %copy.13 = bf16[256,8,4,384]{3,1,2,0:T(8,128)(2,1)S(1)} copy(bf16[256,8,4,384]{3,2,1,0:T(4,128)(2,1)} %bitcast.32) | data formatting | bytes 12582912
  8.2 2.0 %project.2 = (bf16[256,512]{1,0:T(8,128)(2,1)S(1)}, bf16[256,1024]{1,0:T(8,128)(2,1)S(1)}) custom-call(bf16[128,2048]{1,0:T(8,128)(2,1)S(1)} %bitcast.19, bf16[128,2048]{1,0:T(8,128)(2,1)S(1)} %collective-permute-done.1.refs_1_, f32[2,2048]{1,0:T(2,128)S(1)} %maximum_convert_fusion.refs_2_.refs_1_.gain.gain_ref, bf16[2048,1536]{1,0:T(8,128)(2,1)S(1)} %bitcast.10), custom_call_target="tpu_custom_call" | custom-call | tf_op jit(solution)/shard_map/project/pallas_call | solution.py:38
  10.2 5.2 %collective-permute-done.refs_0_.refs_2_ = bf16[128,2048]{1,0:T(8,128)(2,1)S(1)} collective-permute-done((bf16[128,2048]{1,0:T(8,128)(2,1)}, bf16[128,2048]{1,0:T(8,128)(2,1)S(1)}, u32[]{:S(2)}, u32[]{:S(2)}) %collective-permute-start) | collective-permute-done | bytes 524320 | tf_op jit(solution)/shard_map/ppermute | solution.py:26
  17.2 1.9 %attend_far.1 = (bf16[128,512]{1,0:T(8,128)(2,1)S(1)}, bf16[128,512]{1,0:T(8,128)(2,1)S(1)}, bf16[128,1024]{1,0:T(8,128)(2,1)S(1)}) custom-call(s32[1,512]{1,0:T(1,128)S(1)} %copy-done.3, bf16[128,512]{1,0:T(8,128)(2,1)S(1)} %get-tuple-element.66.q_far, bf16[256,1024]{1,0:T(8,128)(2,1)S(1)} %get-tuple-element.63.kv_near, ...), custom_call_target="tpu_custom_call" | custom-call | tf_op jit(solution)/shard_map/attend_far/pallas_call | solution.py:38
  21.3 1.6 %collective-permute-start.6 = (bf16[128,2048]{1,0:T(8,128)(2,1)S(1)}, bf16[128,2048]{1,0:T(8,128)(2,1)S(1)}, u32[]{:S(2)}, u32[]{:S(2)}) collective-permute-start(bf16[128,2048]{1,0:T(8,128)(2,1)S(1)} %out_project.3), channel_id=1, source_target_pairs={{0,16},{8,24},{16,0},{24,8},{1,17},{9,25},{17,1},{25,9},{2,18},{10... | collective-permute-start | bytes 1572872 | tf_op jit(solution)/shard_map/ppermute | solution.py:26
  26.2 9.2 %collective-permute-done.6.far_ref = bf16[128,2048]{1,0:T(8,128)(2,1)S(1)} collective-permute-done((bf16[128,2048]{1,0:T(8,128)(2,1)S(1)}, bf16[128,2048]{1,0:T(8,128)(2,1)S(1)}, u32[]{:S(2)}, u32[]{:S(2)}) %collective-permute-start.6) | collective-permute-done | bytes 524320 | tf_op jit(solution)/shard_map/ppermute | solution.py:26
  36.1 3.0 %collective-permute-start.13 = (bf16[48,2048]{1,0:T(8,128)(2,1)S(1)}, bf16[48,2048]{1,0:T(8,128)(2,1)S(1)}, u32[]{:S(2)}, u32[]{:S(2)}) collective-permute-start(bf16[48,2048]{1,0:T(8,128)(2,1)S(1)} %get-tuple-element.94), channel_id=1, source_target_pairs={{0,6},{1,7},{2,4},{3,5},{4,2},{5,3},{6,0},{7,1},{8,14},{9,15},{10,... | collective-permute-start | bytes 589832 | tf_op jit(solution)/shard_map/ppermute | solution.py:26
  39.6 1.6 %collective-permute-start.9 = (bf16[48,2048]{1,0:T(8,128)(2,1)S(1)}, bf16[48,2048]{1,0:T(8,128)(2,1)S(1)}, u32[]{:S(2)}, u32[]{:S(2)}) collective-permute-start(bf16[48,2048]{1,0:T(8,128)(2,1)S(1)} %get-tuple-element.90), channel_id=1, source_target_pairs={{0,1},{1,0},{2,3},{3,2},{4,5},{5,4},{6,7},{7,6},{8,9},{9,8},{10,11... | collective-permute-start | bytes 589832 | tf_op jit(solution)/shard_map/ppermute | solution.py:26
  41.2 9.7 %collective-permute-start.10 = (bf16[48,2048]{1,0:T(8,128)(2,1)S(1)}, bf16[48,2048]{1,0:T(8,128)(2,1)S(1)}, u32[]{:S(2)}, u32[]{:S(2)}) collective-permute-start(bf16[48,2048]{1,0:T(8,128)(2,1)S(1)} %get-tuple-element.91), channel_id=1, source_target_pairs={{0,2},{1,3},{2,0},{3,1},{4,6},{5,7},{6,4},{7,5},{8,10},{9,11},{10,... | collective-permute-start | bytes 589832 | tf_op jit(solution)/shard_map/ppermute | solution.py:26
  51.3 2.7 %collective-permute-start.15 = (bf16[48,2048]{1,0:T(8,128)(2,1)S(1)}, bf16[48,2048]{1,0:T(8,128)(2,1)S(1)}, u32[]{:S(2)}, u32[]{:S(2)}) collective-permute-start(bf16[48,2048]{1,0:T(8,128)(2,1)S(1)} %get-tuple-element.98), channel_id=1, source_target_pairs={{0,5},{1,4},{2,7},{3,6},{4,1},{5,0},{6,3},{7,2},{8,13},{9,12},{10,... | collective-permute-start | bytes 589832 | tf_op jit(solution)/shard_map/ppermute | solution.py:26
  54.0 2.8 %collective-permute-done.13.refs_1_ = bf16[48,2048]{1,0:T(8,128)(2,1)S(1)} collective-permute-done((bf16[48,2048]{1,0:T(8,128)(2,1)S(1)}, bf16[48,2048]{1,0:T(8,128)(2,1)S(1)}, u32[]{:S(2)}, u32[]{:S(2)}) %collective-permute-start.13) | collective-permute-done | bytes 196640 | tf_op jit(solution)/shard_map/ppermute | solution.py:26
  57.8 2.2 %expert.3 = (bf16[48,2048]{1,0:T(8,128)(2,1)S(1)}, bf16[48,2048]{1,0:T(8,128)(2,1)S(1)}) custom-call(bf16[48,2048]{1,0:T(8,128)(2,1)S(1)} %collective-permute-done.12.refs_0_, bf16[48,2048]{1,0:T(8,128)(2,1)S(1)} %collective-permute-done.13.refs_1_, bf16[2048,2048]{1,0:T(8,128)(2,1)S(1)} %bitcast.25, bf16[1024,2048]{1,0:T(8,128)(2,1)S(1)} %bitcast.28), custom_call_target="tpu_custom_call" | custom-call | flops 34359738368 | tf_op jit(solution)/shard_map/expert/pallas_call | solution.py:38
  59.9 3.1 %collective-permute-start.16 = (bf16[48,2048]{1,0:T(8,128)(2,1)S(1)}, bf16[48,2048]{1,0:T(8,128)(2,1)S(1)}, u32[]{:S(2)}, u32[]{:S(2)}) collective-permute-start(bf16[48,2048]{1,0:T(8,128)(2,1)S(1)} %get-tuple-element.99), channel_id=1, source_target_pairs={{0,7},{1,6},{2,5},{3,4},{4,3},{5,2},{6,1},{7,0},{8,15},{9,14},{10,... | collective-permute-start | bytes 589832 | tf_op jit(solution)/shard_map/ppermute | solution.py:26
  64.4 11.6 %collective-permute-start.19 = (bf16[48,2048]{1,0:T(8,128)(2,1)S(1)}, bf16[48,2048]{1,0:T(8,128)(2,1)S(1)}, u32[]{:S(2)}, u32[]{:S(2)}) collective-permute-start(bf16[48,2048]{1,0:T(8,128)(2,1)S(1)} %get-tuple-element.96), channel_id=1, source_target_pairs={{0,6},{1,7},{2,4},{3,5},{4,2},{5,3},{6,0},{7,1},{8,14},{9,15},{10,... | collective-permute-start | bytes 589832 | tf_op jit(solution)/shard_map/ppermute | solution.py:26
  76.2 2.6 %expert.5 = (bf16[48,2048]{1,0:T(8,128)(2,1)S(1)}, bf16[48,2048]{1,0:T(8,128)(2,1)S(1)}, bf16[48,2048]{1,0:T(8,128)(2,1)S(1)}, bf16[48,2048]{1,0:T(8,128)(2,1)S(1)}) custom-call(bf16[48,2048]{1,0:T(8,128)(2,1)S(1)} %get-tuple-element.109.refs_0_, bf16[48,2048]{1,0:T(8,128)(2,1)S(1)} %collective-permute-done.9.refs_1_, ...), custom_call_target="tpu_custom_call" | custom-call | flops 34359738368 | tf_op jit(solution)/shard_map/expert/pallas_call | solution.py:38
  78.8 3.4 %collective-permute-start.22 = (bf16[48,2048]{1,0:T(8,128)(2,1)S(1)}, bf16[48,2048]{1,0:T(8,128)(2,1)S(1)}, u32[]{:S(2)}, u32[]{:S(2)}) collective-permute-start(bf16[48,2048]{1,0:T(8,128)(2,1)S(1)} %get-tuple-element.114), channel_id=1, source_target_pairs={{0,1},{1,0},{2,3},{3,2},{4,5},{5,4},{6,7},{7,6},{8,9},{9,8},{10,11... | collective-permute-start | bytes 589832 | tf_op jit(solution)/shard_map/ppermute | solution.py:26
  83.3 3.5 %collective-permute-start.24 = (bf16[48,2048]{1,0:T(8,128)(2,1)S(1)}, bf16[48,2048]{1,0:T(8,128)(2,1)S(1)}, u32[]{:S(2)}, u32[]{:S(2)}) collective-permute-start(bf16[48,2048]{1,0:T(8,128)(2,1)S(1)} %get-tuple-element.116), channel_id=1, source_target_pairs={{0,3},{1,2},{2,1},{3,0},{4,7},{5,6},{6,5},{7,4},{8,11},{9,10},{10,... | collective-permute-start | bytes 589832 | tf_op jit(solution)/shard_map/ppermute | solution.py:26
  86.8 2.1 %expert.4 = (bf16[48,2048]{1,0:T(8,128)(2,1)S(1)}, bf16[48,2048]{1,0:T(8,128)(2,1)S(1)}) custom-call(bf16[48,2048]{1,0:T(8,128)(2,1)S(1)} %collective-permute-done.15.refs_0_, bf16[48,2048]{1,0:T(8,128)(2,1)S(1)} %collective-permute-done.16.refs_1_, bf16[2048,2048]{1,0:T(8,128)(2,1)S(1)} %bitcast.27, bf16[1024,2048]{1,0:T(8,128)(2,1)S(1)} %bitcast.30), custom_call_target="tpu_custom_call" | custom-call | flops 34359738368 | tf_op jit(solution)/shard_map/expert/pallas_call | solution.py:38
  89.0 3.0 %collective-permute-done.19.refs_1_ = bf16[48,2048]{1,0:T(8,128)(2,1)S(1)} collective-permute-done((bf16[48,2048]{1,0:T(8,128)(2,1)S(1)}, bf16[48,2048]{1,0:T(8,128)(2,1)S(1)}, u32[]{:S(2)}, u32[]{:S(2)}) %collective-permute-start.19) | collective-permute-done | bytes 196640 | tf_op jit(solution)/shard_map/ppermute | solution.py:26
  92.9 4.1 %cache.1 = bf16[1,8,64,1024]{3,2,1,0:T(8,128)(2,1)} custom-call(bf16[256,2048]{1,0:T(8,128)(2,1)S(1)} %join.3.mine_ref, bf16[256,2048]{1,0:T(8,128)(2,1)S(1)} %collective-permute-done.17.theirs_ref, f32[2,2048]{1,0:T(2,128)S(1)} %maximum_convert_fusion.refs_2_.refs_1_.gain.gain_ref, bf16[2048,1536]{1,0:T(8,128)(2,1)S(1)} %bitcast.13), custom_call_target="tpu_custom_call" | custom-call | tf_op jit(solution)/shard_map/cache/pallas_call | solution.py:38
  97.0 1.4 %collective-permute-done.24.refs_5_ = bf16[48,2048]{1,0:T(8,128)(2,1)S(1)} collective-permute-done((bf16[48,2048]{1,0:T(8,128)(2,1)S(1)}, bf16[48,2048]{1,0:T(8,128)(2,1)S(1)}, u32[]{:S(2)}, u32[]{:S(2)}) %collective-permute-start.24) | collective-permute-done | bytes 196640 | tf_op jit(solution)/shard_map/ppermute | solution.py:26
  98.4 4.5 %collective-permute-done.20.refs_0_ = bf16[48,2048]{1,0:T(8,128)(2,1)S(1)} collective-permute-done((bf16[48,2048]{1,0:T(8,128)(2,1)S(1)}, bf16[48,2048]{1,0:T(8,128)(2,1)S(1)}, u32[]{:S(2)}, u32[]{:S(2)}) %collective-permute-start.20) | collective-permute-done | bytes 196640 | tf_op jit(solution)/shard_map/ppermute | solution.py:26
  102.9 6.4 %collective-permute-done.21.refs_1_ = bf16[48,2048]{1,0:T(8,128)(2,1)S(1)} collective-permute-done((bf16[48,2048]{1,0:T(8,128)(2,1)S(1)}, bf16[48,2048]{1,0:T(8,128)(2,1)S(1)}, u32[]{:S(2)}, u32[]{:S(2)}) %collective-permute-start.21) | collective-permute-done | bytes 196640 | tf_op jit(solution)/shard_map/ppermute | solution.py:26
  (68 shorter events, 16.5 us)
Async XLA Ops:
  0.6 20.0 %collective-permute-start.5 = (bf16[512,2048]{1,0:T(8,128)(2,1)}, bf16[512,2048]{1,0:T(8,128)(2,1)S(1)}, u32[]{:S(2)}, u32[]{:S(2)}) collective-permute-start(bf16[512,2048]{1,0:T(8,128)(2,1)} %bitcast.14), channel_id=1, source_target_pairs={{0,8},{8,0},{16,24},{24,16},{1,9},{9,1},{17,25},{25,17},{2,10},{10... | collective-permute-start | bytes 6291464 | tf_op jit(solution)/shard_map/ppermute | solution.py:26
  0.7 7.4 %collective-permute-start.1 = (bf16[128,2048]{1,0:T(8,128)(2,1)}, bf16[128,2048]{1,0:T(8,128)(2,1)S(1)}, u32[]{:S(2)}, u32[]{:S(2)}) collective-permute-start(bf16[128,2048]{1,0:T(8,128)(2,1)} %bitcast.17), channel_id=1, source_target_pairs={{0,8},{8,0},{16,24},{24,16},{1,9},{9,1},{17,25},{25,17},{2,10},{10... | collective-permute-start | bytes 1572872 | tf_op jit(solution)/shard_map/ppermute | solution.py:26
  1.2 14.1 %collective-permute-start = (bf16[128,2048]{1,0:T(8,128)(2,1)}, bf16[128,2048]{1,0:T(8,128)(2,1)S(1)}, u32[]{:S(2)}, u32[]{:S(2)}) collective-permute-start(bf16[128,2048]{1,0:T(8,128)(2,1)} %bitcast.18), channel_id=1, source_target_pairs={{0,16},{8,24},{16,0},{24,8},{1,17},{9,25},{17,1},{25,9},{2,18},{10... | collective-permute-start | bytes 1572872 | tf_op jit(solution)/shard_map/ppermute | solution.py:26
  15.3 1.9 %collective-permute-start.2 = (bf16[128,2048]{1,0:T(8,128)(2,1)S(1)}, bf16[128,2048]{1,0:T(8,128)(2,1)S(1)}, u32[]{:S(2)}, u32[]{:S(2)}) collective-permute-start(bf16[128,2048]{1,0:T(8,128)(2,1)S(1)} %collective-permute-done.refs_0_.refs_2_), channel_id=1, source_target_pairs={{0,8},{8,0},{16,24},{24,16},{1,9},{9,1},{17,25},{25,17},{2,10},{10... | collective-permute-start | bytes 1572872 | tf_op jit(solution)/shard_map/ppermute | solution.py:26
  21.3 14.0 %collective-permute-start.6 = (bf16[128,2048]{1,0:T(8,128)(2,1)S(1)}, bf16[128,2048]{1,0:T(8,128)(2,1)S(1)}, u32[]{:S(2)}, u32[]{:S(2)}) collective-permute-start(bf16[128,2048]{1,0:T(8,128)(2,1)S(1)} %out_project.3), channel_id=1, source_target_pairs={{0,16},{8,24},{16,0},{24,8},{1,17},{9,25},{17,1},{25,9},{2,18},{10... | collective-permute-start | bytes 1572872 | tf_op jit(solution)/shard_map/ppermute | solution.py:26
  23.9 1.5 %collective-permute-start.4 = (bf16[128,512]{1,0:T(8,128)(2,1)S(1)}, bf16[128,512]{1,0:T(8,128)(2,1)S(1)}, u32[]{:S(2)}, u32[]{:S(2)}) collective-permute-start(bf16[128,512]{1,0:T(8,128)(2,1)S(1)} %get-tuple-element.75), channel_id=1, source_target_pairs={{0,8},{8,0},{16,24},{24,16},{1,9},{9,1},{17,25},{25,17},{2,10},{10... | collective-permute-start | bytes 393224 | tf_op jit(solution)/shard_map/ppermute | solution.py:26
  24.2 15.4 %collective-permute-start.7 = (bf16[64,2048]{1,0:T(8,128)(2,1)S(1)}, bf16[64,2048]{1,0:T(8,128)(2,1)S(1)}, u32[]{:S(2)}, u32[]{:S(2)}) collective-permute-start(bf16[64,2048]{1,0:T(8,128)(2,1)S(1)} %get-tuple-element.85), channel_id=1, source_target_pairs={{0,4},{1,5},{2,6},{3,7},{4,0},{5,1},{6,2},{7,3},{8,13},{9,12},{10,... | collective-permute-start | bytes 786440 | tf_op jit(solution)/shard_map/ppermute | solution.py:293
  24.6 15.0 %collective-permute-start.8 = (bf16[64,2048]{1,0:T(8,128)(2,1)S(1)}, bf16[64,2048]{1,0:T(8,128)(2,1)S(1)}, u32[]{:S(2)}, u32[]{:S(2)}) collective-permute-start(bf16[64,2048]{1,0:T(8,128)(2,1)S(1)} %get-tuple-element.86), channel_id=1, source_target_pairs={{0,0},{1,1},{2,2},{3,3},{4,4},{5,5},{6,6},{7,7},{8,9},{9,8},{10,11... | collective-permute-start | bytes 786440 | tf_op jit(solution)/shard_map/ppermute | solution.py:293
  36.0 15.3 %collective-permute-start.12 = (bf16[48,2048]{1,0:T(8,128)(2,1)S(1)}, bf16[48,2048]{1,0:T(8,128)(2,1)S(1)}, u32[]{:S(2)}, u32[]{:S(2)}) collective-permute-start(bf16[48,2048]{1,0:T(8,128)(2,1)S(1)} %get-tuple-element.93), channel_id=1, source_target_pairs={{0,4},{1,5},{2,6},{3,7},{4,0},{5,1},{6,2},{7,3},{8,12},{9,13},{10,... | collective-permute-start | bytes 589832 | tf_op jit(solution)/shard_map/ppermute | solution.py:26
  36.1 20.6 %collective-permute-start.13 = (bf16[48,2048]{1,0:T(8,128)(2,1)S(1)}, bf16[48,2048]{1,0:T(8,128)(2,1)S(1)}, u32[]{:S(2)}, u32[]{:S(2)}) collective-permute-start(bf16[48,2048]{1,0:T(8,128)(2,1)S(1)} %get-tuple-element.94), channel_id=1, source_target_pairs={{0,6},{1,7},{2,4},{3,5},{4,2},{5,3},{6,0},{7,1},{8,14},{9,15},{10,... | collective-permute-start | bytes 589832 | tf_op jit(solution)/shard_map/ppermute | solution.py:26
  39.6 20.4 %collective-permute-start.9 = (bf16[48,2048]{1,0:T(8,128)(2,1)S(1)}, bf16[48,2048]{1,0:T(8,128)(2,1)S(1)}, u32[]{:S(2)}, u32[]{:S(2)}) collective-permute-start(bf16[48,2048]{1,0:T(8,128)(2,1)S(1)} %get-tuple-element.90), channel_id=1, source_target_pairs={{0,1},{1,0},{2,3},{3,2},{4,5},{5,4},{6,7},{7,6},{8,9},{9,8},{10,11... | collective-permute-start | bytes 589832 | tf_op jit(solution)/shard_map/ppermute | solution.py:26
  41.2 21.8 %collective-permute-start.10 = (bf16[48,2048]{1,0:T(8,128)(2,1)S(1)}, bf16[48,2048]{1,0:T(8,128)(2,1)S(1)}, u32[]{:S(2)}, u32[]{:S(2)}) collective-permute-start(bf16[48,2048]{1,0:T(8,128)(2,1)S(1)} %get-tuple-element.91), channel_id=1, source_target_pairs={{0,2},{1,3},{2,0},{3,1},{4,6},{5,7},{6,4},{7,5},{8,10},{9,11},{10,... | collective-permute-start | bytes 589832 | tf_op jit(solution)/shard_map/ppermute | solution.py:26
  50.9 13.5 %collective-permute-start.11 = (bf16[48,2048]{1,0:T(8,128)(2,1)S(1)}, bf16[48,2048]{1,0:T(8,128)(2,1)S(1)}, u32[]{:S(2)}, u32[]{:S(2)}) collective-permute-start(bf16[48,2048]{1,0:T(8,128)(2,1)S(1)} %get-tuple-element.92), channel_id=1, source_target_pairs={{0,3},{1,2},{2,1},{3,0},{4,7},{5,6},{6,5},{7,4},{8,11},{9,10},{10,... | collective-permute-start | bytes 589832 | tf_op jit(solution)/shard_map/ppermute | solution.py:26
  51.3 27.5 %collective-permute-start.15 = (bf16[48,2048]{1,0:T(8,128)(2,1)S(1)}, bf16[48,2048]{1,0:T(8,128)(2,1)S(1)}, u32[]{:S(2)}, u32[]{:S(2)}) collective-permute-start(bf16[48,2048]{1,0:T(8,128)(2,1)S(1)} %get-tuple-element.98), channel_id=1, source_target_pairs={{0,5},{1,4},{2,7},{3,6},{4,1},{5,0},{6,3},{7,2},{8,13},{9,12},{10,... | collective-permute-start | bytes 589832 | tf_op jit(solution)/shard_map/ppermute | solution.py:26
  56.7 19.3 %collective-permute-start.14 = (bf16[128,2048]{1,0:T(8,128)(2,1)S(1)}, bf16[128,2048]{1,0:T(8,128)(2,1)S(1)}, u32[]{:S(2)}, u32[]{:S(2)}) collective-permute-start(bf16[128,2048]{1,0:T(8,128)(2,1)S(1)} %join.2.refs_0_), channel_id=1, source_target_pairs={{0,16},{8,24},{16,0},{24,8},{1,17},{9,25},{17,1},{25,9},{2,18},{10... | collective-permute-start | bytes 1572872 | tf_op jit(solution)/shard_map/ppermute | solution.py:26
  59.9 23.4 %collective-permute-start.16 = (bf16[48,2048]{1,0:T(8,128)(2,1)S(1)}, bf16[48,2048]{1,0:T(8,128)(2,1)S(1)}, u32[]{:S(2)}, u32[]{:S(2)}) collective-permute-start(bf16[48,2048]{1,0:T(8,128)(2,1)S(1)} %get-tuple-element.99), channel_id=1, source_target_pairs={{0,7},{1,6},{2,5},{3,4},{4,3},{5,2},{6,1},{7,0},{8,15},{9,14},{10,... | collective-permute-start | bytes 589832 | tf_op jit(solution)/shard_map/ppermute | solution.py:26
  63.0 25.9 %collective-permute-start.18 = (bf16[48,2048]{1,0:T(8,128)(2,1)S(1)}, bf16[48,2048]{1,0:T(8,128)(2,1)S(1)}, u32[]{:S(2)}, u32[]{:S(2)}) collective-permute-start(bf16[48,2048]{1,0:T(8,128)(2,1)S(1)} %get-tuple-element.95), channel_id=1, source_target_pairs={{0,4},{1,5},{2,6},{3,7},{4,0},{5,1},{6,2},{7,3},{8,12},{9,13},{10,... | collective-permute-start | bytes 589832 | tf_op jit(solution)/shard_map/ppermute | solution.py:26
  64.4 27.7 %collective-permute-start.19 = (bf16[48,2048]{1,0:T(8,128)(2,1)S(1)}, bf16[48,2048]{1,0:T(8,128)(2,1)S(1)}, u32[]{:S(2)}, u32[]{:S(2)}) collective-permute-start(bf16[48,2048]{1,0:T(8,128)(2,1)S(1)} %get-tuple-element.96), channel_id=1, source_target_pairs={{0,6},{1,7},{2,4},{3,5},{4,2},{5,3},{6,0},{7,1},{8,14},{9,15},{10,... | collective-permute-start | bytes 589832 | tf_op jit(solution)/shard_map/ppermute | solution.py:26
  76.1 7.2 %collective-permute-start.17 = (bf16[256,2048]{1,0:T(8,128)(2,1)S(1)}, bf16[256,2048]{1,0:T(8,128)(2,1)S(1)}, u32[]{:S(2)}, u32[]{:S(2)}) collective-permute-start(bf16[256,2048]{1,0:T(8,128)(2,1)S(1)} %join.3.mine_ref), channel_id=1, source_target_pairs={{0,8},{8,0},{16,24},{24,16},{1,9},{9,1},{17,25},{25,17},{2,10},{10... | collective-permute-start | bytes 3145736 | tf_op jit(solution)/shard_map/ppermute | solution.py:26
  78.8 18.2 %collective-permute-start.22 = (bf16[48,2048]{1,0:T(8,128)(2,1)S(1)}, bf16[48,2048]{1,0:T(8,128)(2,1)S(1)}, u32[]{:S(2)}, u32[]{:S(2)}) collective-permute-start(bf16[48,2048]{1,0:T(8,128)(2,1)S(1)} %get-tuple-element.114), channel_id=1, source_target_pairs={{0,1},{1,0},{2,3},{3,2},{4,5},{5,4},{6,7},{7,6},{8,9},{9,8},{10,11... | collective-permute-start | bytes 589832 | tf_op jit(solution)/shard_map/ppermute | solution.py:26
  83.3 13.7 %collective-permute-start.23 = (bf16[48,2048]{1,0:T(8,128)(2,1)S(1)}, bf16[48,2048]{1,0:T(8,128)(2,1)S(1)}, u32[]{:S(2)}, u32[]{:S(2)}) collective-permute-start(bf16[48,2048]{1,0:T(8,128)(2,1)S(1)} %get-tuple-element.115), channel_id=1, source_target_pairs={{0,2},{1,3},{2,0},{3,1},{4,6},{5,7},{6,4},{7,5},{8,10},{9,11},{10,... | collective-permute-start | bytes 589832 | tf_op jit(solution)/shard_map/ppermute | solution.py:26
  83.3 15.1 %collective-permute-start.24 = (bf16[48,2048]{1,0:T(8,128)(2,1)S(1)}, bf16[48,2048]{1,0:T(8,128)(2,1)S(1)}, u32[]{:S(2)}, u32[]{:S(2)}) collective-permute-start(bf16[48,2048]{1,0:T(8,128)(2,1)S(1)} %get-tuple-element.116), channel_id=1, source_target_pairs={{0,3},{1,2},{2,1},{3,0},{4,7},{5,6},{6,5},{7,4},{8,11},{9,10},{10,... | collective-permute-start | bytes 589832 | tf_op jit(solution)/shard_map/ppermute | solution.py:26
  89.0 13.9 %collective-permute-start.20 = (bf16[48,2048]{1,0:T(8,128)(2,1)S(1)}, bf16[48,2048]{1,0:T(8,128)(2,1)S(1)}, u32[]{:S(2)}, u32[]{:S(2)}) collective-permute-start(bf16[48,2048]{1,0:T(8,128)(2,1)S(1)} %get-tuple-element.107), channel_id=1, source_target_pairs={{0,5},{1,4},{2,7},{3,6},{4,1},{5,0},{6,3},{7,2},{8,13},{9,12},{10,... | collective-permute-start | bytes 589832 | tf_op jit(solution)/shard_map/ppermute | solution.py:26
  92.0 17.2 %collective-permute-start.21 = (bf16[48,2048]{1,0:T(8,128)(2,1)S(1)}, bf16[48,2048]{1,0:T(8,128)(2,1)S(1)}, u32[]{:S(2)}, u32[]{:S(2)}) collective-permute-start(bf16[48,2048]{1,0:T(8,128)(2,1)S(1)} %get-tuple-element.108), channel_id=1, source_target_pairs={{0,7},{1,6},{2,5},{3,4},{4,3},{5,2},{6,1},{7,0},{8,15},{9,14},{10,... | collective-permute-start | bytes 589832 | tf_op jit(solution)/shard_map/ppermute | solution.py:26
  (10 other events, 92.3 us)
